TPU v7x, 512 devices: a whole 4x8x8 slice. The times are simulated.
512 devices in a mesh: hier: 32 (over y, x), col: 16 (over z, core).
Axes of the slice: x: 4, y: 8, z: 8, core: 2. Of those that a mesh axis runs over, the one named last changes fastest.
Arguments:
- densities: float32 [128, 2, 256, 256], P('hier', None, 'col'), may hold values from -6 to 6
- hamiltonian: float32 [256, 256], replicated, may hold values from -0.35355339 to 0.35355339, as said below
- couplings: float32 [2, 256, 256], replicated, may hold values from -0.088388348 to 0.088388348, as said below
- gamma: float32 [2], replicated, may hold values from 0.005 to 0.05
- coeff: float32 [2, 2], replicated, may hold values from -0.5 to 0.5
- node_count: int32 [32], replicated, may hold values from 2 to 4, as said below
Outputs:
- new_densities: float32 [128, 2, 256, 256], P('hier', None, 'col')
Inputs may be any that keep to these rules, and one draw needn't show every extreme that they name: `node_count`: at least one index of hier holds 4 nodes; every index holds 2 or more. `hamiltonian`: symmetric. `couplings`: each of the two matrices is symmetric.
All inputs are finite; a program needn't handle non-finite values.
Results may differ from a plain program's by a relative error of at most 0.00012.
Values sent between devices are 32-bit elements; how exact they have to be, the bound alone decides.
No kernel may reach another device: no remote copies, remote signals or barrier semaphores. Data moves between devices by JAX's collectives and lax.ppermute only.
A program may use at most 64 MiB of HBM per device.

v0:
```python
import jax
import jax.numpy as jnp
from jax import lax
from jax.sharding import PartitionSpec as P

DEPTH2 = 2


step_size = 0.2


def passed_along(block, axis, distance):
    devices = range(lax.axis_size(axis))
    route = [(i - distance, i) for i in devices if i - distance in devices]
    return lax.ppermute(block, axis, route)


def hierarchy(node_count, device, slot):
    shards = node_count.shape[0]
    columns = jnp.arange(shards, dtype=jnp.int32)
    offsets = jnp.cumsum(node_count) - node_count
    live_total = jnp.sum(node_count) // DEPTH2 * DEPTH2

    def lookup(table, which):
        return jnp.sum(jnp.where(which[:, None] == columns[None, :], table[None, :], 0), axis=1)

    index = lookup(offsets, device) + slot
    live = (slot < lookup(node_count, device)) & (index < live_total)
    first = index // DEPTH2
    second = index % DEPTH2
    targets = (index + DEPTH2, index + 1, index - DEPTH2, index - 1)
    allowed = (
        live & (index + DEPTH2 < live_total),
        live & (second + 1 < DEPTH2),
        live & (first > 0),
        live & (second > 0),
    )
    found = []
    for target, valid in zip(targets, allowed):
        owner = jnp.sum((offsets[None, :] <= target[:, None]).astype(jnp.int32), axis=1) - 1
        within = target - lookup(offsets, owner)
        owner_count = lookup(node_count, owner)
        found.append((owner, within, valid, owner_count))
    return (live, first, second, found)


def combine(upward, downward, raise_w, lower_w, real, imag):
    rise = raise_w[:, None, None]
    fall = lower_w[:, None, None]
    part_re = rise * upward[:, 0] + fall * (real * downward[:, 0] - imag * downward[:, 1])
    part_im = rise * upward[:, 1] + fall * (real * downward[:, 1] + imag * downward[:, 0])
    return jnp.stack([part_re, part_im], axis=1)


def mixes(linked, levels, coeff, sign):
    result = []
    for mode in range(2):
        result.append(
            combine(
                linked[mode],
                linked[mode + 2],
                jnp.sqrt(levels[mode] + 1.0),
                jnp.sqrt(levels[mode]),
                coeff[mode, 0],
                sign * coeff[mode, 1],
            )
        )
    return result


def pick(wide, positions, masks):
    return [jnp.take(wide, positions[j], axis=0) * masks[j] for j in range(4)]


def tail_slots(block, start, half):
    return lax.dynamic_slice_in_dim(block, start, half, 0)


def slope(state, left_mat, right_mat, gamma, coeff, layout_info):
    alive, levels, positions, masks, tail_start = layout_info
    half = state.shape[0] // 2
    high = lax.Precision.HIGHEST
    own_cols = lax.all_to_all(state, "col", split_axis=3, concat_axis=2, tiled=True)
    lower = passed_along(
        (tail_slots(state, tail_start, half), tail_slots(own_cols, tail_start, half)), "hier", 1
    )
    upper = passed_along((state[:half], own_cols[:half]), "hier", -1)
    wide_rows = jnp.concatenate([lower[0], state, upper[0]], axis=0)
    wide_cols = jnp.concatenate([lower[1], own_cols, upper[1]], axis=0)
    rights = mixes(pick(wide_rows, positions, masks), levels, coeff, -1.0)
    lefts = mixes(pick(wide_cols, positions, masks), levels, coeff, 1.0)
    col_stack = jnp.concatenate([own_cols] + lefts, axis=2)
    right = jnp.einsum(
        "scij,jk->scik", jnp.concatenate([state] + rights, axis=3), right_mat, precision=high
    )
    left_cols = jnp.einsum("ij,scjk->scik", left_mat, col_stack, precision=high)
    left = lax.all_to_all(left_cols, "col", split_axis=2, concat_axis=3, tiled=True)
    comm = left - right
    damping = (levels[0] * gamma[0] + levels[1] * gamma[1])[:, None, None]
    out_re = comm[:, 1] - damping * state[:, 0]
    out_im = -comm[:, 0] - damping * state[:, 1]
    return jnp.stack([out_re, out_im], axis=1) * alive


def on_device(densities, hamiltonian, couplings, gamma, coeff, node_count):
    width = densities.shape[0]
    half = width // 2
    here = lax.axis_index("hier")
    device = jnp.full((width,), here, jnp.int32)
    slot = jnp.arange(width, dtype=jnp.int32)
    live, first, second, found = hierarchy(node_count, device, slot)
    own_count = jnp.sum(
        jnp.where(jnp.arange(node_count.shape[0], dtype=jnp.int32) == here, node_count, 0)
    )
    tail_start = own_count - half
    positions = []
    for o, w, v, c in found:
        place = jnp.where(
            o == here, half + w, jnp.where(o < here, w - (c - half), half + width + w)
        )
        positions.append(jnp.where(v, place, 0))
    masks = [v.astype(jnp.float32)[:, None, None, None] for o, w, v, c in found]
    levels = (first.astype(jnp.float32), second.astype(jnp.float32))
    alive = live.astype(jnp.float32)[:, None, None, None]
    layout_info = (alive, levels, positions, masks, tail_start)
    left_mat = jnp.concatenate([hamiltonian, couplings[0], couplings[1]], axis=1)
    right_mat = jnp.concatenate([hamiltonian, couplings[0], couplings[1]], axis=0)
    first_slope = slope(densities, left_mat, right_mat, gamma, coeff, layout_info)
    middle = densities + 0.5 * step_size * first_slope
    second_slope = slope(middle, left_mat, right_mat, gamma, coeff, layout_info)
    return densities + step_size * second_slope


def solution(mesh):
    placed = (P("hier", None, "col", None), P(), P(), P(), P(), P())
    return jax.shard_map(
        on_device,
        mesh=mesh,
        in_specs=placed,
        out_specs=P("hier", None, "col", None),
        check_vma=False,
    )
```

profile of v0, /device:TPU:31, one launch (start us, length us, event | category | flops | bytes accessed | tf_op | source)
XLA Modules:
  0.0 152.4 jit_solution(11104363821746486487)
XLA Ops:
  0.0 1.4 copy.35
  1.4 1.5 reshape.391
  2.9 11.1 %all-to-all-start = ((f32[16,1,2048]{2,1,0:T(1,128)}), f32[16,1,2048]{2,1,0:T(1,128)S(1)}, u32[]{:S(2)}, u32[]{:S(2)}) async-start(f32[16,1,2048]{2,1,0:T(1,128)} %reshape.391), calls=%async_computation | async-start | bytes 262144 | tf_op jit(solution)/shard_map/all_to_all | solution.py:83
  16.8 4.4 %collective-permute-start.2 = (f32[2,2,16,256]{3,2,1,0:T(8,128)S(1)}, f32[2,2,16,256]{3,2,1,0:T(8,128)S(1)}, u32[]{:S(2)}, u32[]{:S(2)}) collective-permute-start(f32[2,2,16,256]{3,2,1,0:T(8,128)S(1)} %get-tuple-element.59), channel_id=1, source_target_pairs={{0,16},{16,32},{32,48},{48,64},{64,80},{80,96},{96,112},{112,128},... | collective-permute-start | bytes 196616 | tf_op jit(solution)/shard_map/ppermute | solution.py:15
  21.2 1.9 %collective-permute-start.3 = (f32[2,2,16,256]{3,2,1,0:T(8,128)S(1)}, f32[2,2,16,256]{3,2,1,0:T(8,128)S(1)}, u32[]{:S(2)}, u32[]{:S(2)}) collective-permute-start(f32[2,2,16,256]{3,2,1,0:T(8,128)S(1)} %get-tuple-element.58), channel_id=1, source_target_pairs={{16,0},{32,16},{48,32},{64,48},{80,64},{96,80},{112,96},{128,112},... | collective-permute-start | bytes 196616 | tf_op jit(solution)/shard_map/ppermute | solution.py:15
  38.0 6.7 %collective-permute-start = (f32[2,2,256,16]{2,3,1,0:T(8,128)S(1)}, f32[2,2,256,16]{2,3,1,0:T(8,128)S(1)}, u32[]{:S(2)}, u32[]{:S(2)}) collective-permute-start(f32[2,2,256,16]{2,3,1,0:T(8,128)S(1)} %constant_dynamic-slice_fusion.3), channel_id=1, source_target_pairs={{0,16},{16,32},{32,48},{48,64},{64,80},{80,96},{96,112},{112,128},... | collective-permute-start | bytes 196616 | tf_op jit(solution)/shard_map/ppermute | solution.py:15
  45.1 1.9 %collective-permute-start.1 = (f32[2,2,256,16]{2,3,1,0:T(8,128)S(1)}, f32[2,2,256,16]{2,3,1,0:T(8,128)S(1)}, u32[]{:S(2)}, u32[]{:S(2)}) collective-permute-start(f32[2,2,256,16]{2,3,1,0:T(8,128)S(1)} %slice.195), channel_id=1, source_target_pairs={{16,0},{32,16},{48,32},{64,48},{80,64},{96,80},{112,96},{128,112},... | collective-permute-start | bytes 196616 | tf_op jit(solution)/shard_map/ppermute | solution.py:15
  47.0 6.4 %collective-permute-done.1 = f32[2,2,256,16]{2,3,1,0:T(8,128)S(1)} collective-permute-done((f32[2,2,256,16]{2,3,1,0:T(8,128)S(1)}, f32[2,2,256,16]{2,3,1,0:T(8,128)S(1)}, u32[]{:S(2)}, u32[]{:S(2)}) %collective-permute-start.1) | collective-permute-done | bytes 65568 | tf_op jit(solution)/shard_map/ppermute | solution.py:15
  60.4 2.1 %reshape.393 = f32[16,1,2048]{2,1,0:T(1,128)} reshape(f32[256,4,2,16]{3,2,1,0:T(2,128)S(1)} %bitcast.75) | data formatting | bytes 262144
  62.5 9.2 %all-to-all-start.1 = ((f32[16,1,2048]{2,1,0:T(1,128)}), f32[16,1,2048]{2,1,0:T(1,128)S(1)}, u32[]{:S(2)}, u32[]{:S(2)}) async-start(f32[16,1,2048]{2,1,0:T(1,128)} %reshape.393), calls=%async_computation.1 | async-start | bytes 262144 | tf_op jit(solution)/shard_map/all_to_all | solution.py:97
  73.0 7.8 %all-to-all-done.1 = f32[16,1,2048]{2,1,0:T(1,128)S(1)} async-done(((f32[16,1,2048]{2,1,0:T(1,128)}), f32[16,1,2048]{2,1,0:T(1,128)S(1)}, u32[]{:S(2)}, u32[]{:S(2)}) %all-to-all-start.1) | async-done | bytes 131104 | tf_op jit(solution)/shard_map/all_to_all | solution.py:97
  81.9 1.4 reshape.394
  85.5 1.9 %collective-permute-start.7 = (f32[2,2,16,256]{3,2,1,0:T(8,128)S(1)}, f32[2,2,16,256]{3,2,1,0:T(8,128)S(1)}, u32[]{:S(2)}, u32[]{:S(2)}) collective-permute-start(f32[2,2,16,256]{3,2,1,0:T(8,128)S(1)} %get-tuple-element.57), channel_id=1, source_target_pairs={{16,0},{32,16},{48,32},{64,48},{80,64},{96,80},{112,96},{128,112},... | collective-permute-start | bytes 196616 | tf_op jit(solution)/shard_map/ppermute | solution.py:15
  87.5 6.9 %collective-permute-start.6 = (f32[2,2,16,256]{3,2,1,0:T(8,128)S(1)}, f32[2,2,16,256]{3,2,1,0:T(8,128)S(1)}, u32[]{:S(2)}, u32[]{:S(2)}) collective-permute-start(f32[2,2,16,256]{3,2,1,0:T(8,128)S(1)} %get-tuple-element.56), channel_id=1, source_target_pairs={{0,16},{16,32},{32,48},{48,64},{64,80},{80,96},{96,112},{112,128},... | collective-permute-start | bytes 196616 | tf_op jit(solution)/shard_map/ppermute | solution.py:15
  95.1 2.1 %reshape.395 = f32[16,1,2048]{2,1,0:T(1,128)} reshape(f32[256,4,2,16]{3,2,1,0:T(2,128)S(1)} %bitcast.78) | data formatting | bytes 262144
  97.2 3.5 %all-to-all-start.2 = ((f32[16,1,2048]{2,1,0:T(1,128)}), f32[16,1,2048]{2,1,0:T(1,128)S(1)}, u32[]{:S(2)}, u32[]{:S(2)}) async-start(f32[16,1,2048]{2,1,0:T(1,128)} %reshape.395), calls=%async_computation.2 | async-start | bytes 262144 | tf_op jit(solution)/shard_map/all_to_all | solution.py:83
  103.3 6.6 %all-to-all-done.2 = f32[16,1,2048]{2,1,0:T(1,128)S(1)} async-done(((f32[16,1,2048]{2,1,0:T(1,128)}), f32[16,1,2048]{2,1,0:T(1,128)S(1)}, u32[]{:S(2)}, u32[]{:S(2)}) %all-to-all-start.2) | async-done | bytes 131104 | tf_op jit(solution)/shard_map/all_to_all | solution.py:83
  111.0 1.4 reshape.396
  113.4 1.9 %collective-permute-start.4 = (f32[2,2,256,16]{2,3,1,0:T(8,128)S(1)}, f32[2,2,256,16]{2,3,1,0:T(8,128)S(1)}, u32[]{:S(2)}, u32[]{:S(2)}) collective-permute-start(f32[2,2,256,16]{2,3,1,0:T(8,128)S(1)} %constant_dynamic-slice_fusion.1), channel_id=1, source_target_pairs={{0,16},{16,32},{32,48},{48,64},{64,80},{80,96},{96,112},{112,128},... | collective-permute-start | bytes 196616 | tf_op jit(solution)/shard_map/ppermute | solution.py:15
  115.7 3.4 %collective-permute-start.5 = (f32[2,2,256,16]{2,3,1,0:T(8,128)S(1)}, f32[2,2,256,16]{2,3,1,0:T(8,128)S(1)}, u32[]{:S(2)}, u32[]{:S(2)}) collective-permute-start(f32[2,2,256,16]{2,3,1,0:T(8,128)S(1)} %slice.226), channel_id=1, source_target_pairs={{16,0},{32,16},{48,32},{64,48},{80,64},{96,80},{112,96},{128,112},... | collective-permute-start | bytes 196616 | tf_op jit(solution)/shard_map/ppermute | solution.py:15
  119.3 5.6 %collective-permute-done.5 = f32[2,2,256,16]{2,3,1,0:T(8,128)S(1)} collective-permute-done((f32[2,2,256,16]{2,3,1,0:T(8,128)S(1)}, f32[2,2,256,16]{2,3,1,0:T(8,128)S(1)}, u32[]{:S(2)}, u32[]{:S(2)}) %collective-permute-start.5) | collective-permute-done | bytes 65568 | tf_op jit(solution)/shard_map/ppermute | solution.py:15
  131.9 2.1 %reshape.397 = f32[16,1,2048]{2,1,0:T(1,128)} reshape(f32[256,4,2,16]{3,2,1,0:T(2,128)S(1)} %bitcast.76) | data formatting | bytes 262144
  134.0 3.9 %all-to-all-start.3 = ((f32[16,1,2048]{2,1,0:T(1,128)}), f32[16,1,2048]{2,1,0:T(1,128)S(1)}, u32[]{:S(2)}, u32[]{:S(2)}) async-start(f32[16,1,2048]{2,1,0:T(1,128)} %reshape.397), calls=%async_computation.3 | async-start | bytes 262144 | tf_op jit(solution)/shard_map/all_to_all | solution.py:97
  139.2 7.9 %all-to-all-done.3 = f32[16,1,2048]{2,1,0:T(1,128)S(1)} async-done(((f32[16,1,2048]{2,1,0:T(1,128)}), f32[16,1,2048]{2,1,0:T(1,128)S(1)}, u32[]{:S(2)}, u32[]{:S(2)}) %all-to-all-start.3) | async-done | bytes 131104 | tf_op jit(solution)/shard_map/all_to_all | solution.py:97
  (133 shorter events, 43.5 us)
Async XLA Ops:
  1.4 24.5 %copy-start.1 = (f32[2,256,256]{2,1,0:T(8,128)S(1)}, f32[2,256,256]{2,1,0:T(8,128)}, u32[]{:S(2)}) copy-start(f32[2,256,256]{2,1,0:T(8,128)} %param.12) | copy-start | bytes 1572868
  2.9 13.9 %copy-start = (f32[4,2,16,256]{3,2,1,0:T(8,128)S(1)}, f32[4,2,16,256]{3,2,1,0:T(8,128)}, u32[]{:S(2)}) copy-start(f32[4,2,16,256]{3,2,1,0:T(8,128)} %param.10) | copy-start | bytes 393220
  2.9 31.7 %all-to-all-start = ((f32[16,1,2048]{2,1,0:T(1,128)}), f32[16,1,2048]{2,1,0:T(1,128)S(1)}, u32[]{:S(2)}, u32[]{:S(2)}) async-start(f32[16,1,2048]{2,1,0:T(1,128)} %reshape.391), calls=%async_computation | async-start | bytes 262144 | tf_op jit(solution)/shard_map/all_to_all | solution.py:83
  14.0 0.7 copy-start.2
  16.8 15.2 %collective-permute-start.2 = (f32[2,2,16,256]{3,2,1,0:T(8,128)S(1)}, f32[2,2,16,256]{3,2,1,0:T(8,128)S(1)}, u32[]{:S(2)}, u32[]{:S(2)}) collective-permute-start(f32[2,2,16,256]{3,2,1,0:T(8,128)S(1)} %get-tuple-element.59), channel_id=1, source_target_pairs={{0,16},{16,32},{32,48},{48,64},{64,80},{80,96},{96,112},{112,128},... | collective-permute-start | bytes 196616 | tf_op jit(solution)/shard_map/ppermute | solution.py:15
  21.2 10.9 %collective-permute-start.3 = (f32[2,2,16,256]{3,2,1,0:T(8,128)S(1)}, f32[2,2,16,256]{3,2,1,0:T(8,128)S(1)}, u32[]{:S(2)}, u32[]{:S(2)}) collective-permute-start(f32[2,2,16,256]{3,2,1,0:T(8,128)S(1)} %get-tuple-element.58), channel_id=1, source_target_pairs={{16,0},{32,16},{48,32},{64,48},{80,64},{96,80},{112,96},{128,112},... | collective-permute-start | bytes 196616 | tf_op jit(solution)/shard_map/ppermute | solution.py:15
  26.3 0.7 copy-start.4
  29.4 0.7 copy-start.3
  38.0 9.0 %collective-permute-start = (f32[2,2,256,16]{2,3,1,0:T(8,128)S(1)}, f32[2,2,256,16]{2,3,1,0:T(8,128)S(1)}, u32[]{:S(2)}, u32[]{:S(2)}) collective-permute-start(f32[2,2,256,16]{2,3,1,0:T(8,128)S(1)} %constant_dynamic-slice_fusion.3), channel_id=1, source_target_pairs={{0,16},{16,32},{32,48},{48,64},{64,80},{80,96},{96,112},{112,128},... | collective-permute-start | bytes 196616 | tf_op jit(solution)/shard_map/ppermute | solution.py:15
  45.1 8.3 %collective-permute-start.1 = (f32[2,2,256,16]{2,3,1,0:T(8,128)S(1)}, f32[2,2,256,16]{2,3,1,0:T(8,128)S(1)}, u32[]{:S(2)}, u32[]{:S(2)}) collective-permute-start(f32[2,2,256,16]{2,3,1,0:T(8,128)S(1)} %slice.195), channel_id=1, source_target_pairs={{16,0},{32,16},{48,32},{64,48},{80,64},{96,80},{112,96},{128,112},... | collective-permute-start | bytes 196616 | tf_op jit(solution)/shard_map/ppermute | solution.py:15
  57.4 1.3 copy-start.5
  62.5 18.4 %all-to-all-start.1 = ((f32[16,1,2048]{2,1,0:T(1,128)}), f32[16,1,2048]{2,1,0:T(1,128)S(1)}, u32[]{:S(2)}, u32[]{:S(2)}) async-start(f32[16,1,2048]{2,1,0:T(1,128)} %reshape.393), calls=%async_computation.1 | async-start | bytes 262144 | tf_op jit(solution)/shard_map/all_to_all | solution.py:97
  83.9 1.0 copy-start.6
  85.5 15.2 %collective-permute-start.7 = (f32[2,2,16,256]{3,2,1,0:T(8,128)S(1)}, f32[2,2,16,256]{3,2,1,0:T(8,128)S(1)}, u32[]{:S(2)}, u32[]{:S(2)}) collective-permute-start(f32[2,2,16,256]{3,2,1,0:T(8,128)S(1)} %get-tuple-element.57), channel_id=1, source_target_pairs={{16,0},{32,16},{48,32},{64,48},{80,64},{96,80},{112,96},{128,112},... | collective-permute-start | bytes 196616 | tf_op jit(solution)/shard_map/ppermute | solution.py:15
  87.5 13.3 %collective-permute-start.6 = (f32[2,2,16,256]{3,2,1,0:T(8,128)S(1)}, f32[2,2,16,256]{3,2,1,0:T(8,128)S(1)}, u32[]{:S(2)}, u32[]{:S(2)}) collective-permute-start(f32[2,2,16,256]{3,2,1,0:T(8,128)S(1)} %get-tuple-element.56), channel_id=1, source_target_pairs={{0,16},{16,32},{32,48},{48,64},{64,80},{80,96},{96,112},{112,128},... | collective-permute-start | bytes 196616 | tf_op jit(solution)/shard_map/ppermute | solution.py:15
  97.2 12.7 %all-to-all-start.2 = ((f32[16,1,2048]{2,1,0:T(1,128)}), f32[16,1,2048]{2,1,0:T(1,128)S(1)}, u32[]{:S(2)}, u32[]{:S(2)}) async-start(f32[16,1,2048]{2,1,0:T(1,128)} %reshape.395), calls=%async_computation.2 | async-start | bytes 262144 | tf_op jit(solution)/shard_map/all_to_all | solution.py:83
  113.4 5.8 %collective-permute-start.4 = (f32[2,2,256,16]{2,3,1,0:T(8,128)S(1)}, f32[2,2,256,16]{2,3,1,0:T(8,128)S(1)}, u32[]{:S(2)}, u32[]{:S(2)}) collective-permute-start(f32[2,2,256,16]{2,3,1,0:T(8,128)S(1)} %constant_dynamic-slice_fusion.1), channel_id=1, source_target_pairs={{0,16},{16,32},{32,48},{48,64},{64,80},{80,96},{96,112},{112,128},... | collective-permute-start | bytes 196616 | tf_op jit(solution)/shard_map/ppermute | solution.py:15
  115.7 9.2 %collective-permute-start.5 = (f32[2,2,256,16]{2,3,1,0:T(8,128)S(1)}, f32[2,2,256,16]{2,3,1,0:T(8,128)S(1)}, u32[]{:S(2)}, u32[]{:S(2)}) collective-permute-start(f32[2,2,256,16]{2,3,1,0:T(8,128)S(1)} %slice.226), channel_id=1, source_target_pairs={{16,0},{32,16},{48,32},{64,48},{80,64},{96,80},{112,96},{128,112},... | collective-permute-start | bytes 196616 | tf_op jit(solution)/shard_map/ppermute | solution.py:15
  128.8 1.3 copy-start.7
  134.0 13.1 %all-to-all-start.3 = ((f32[16,1,2048]{2,1,0:T(1,128)}), f32[16,1,2048]{2,1,0:T(1,128)S(1)}, u32[]{:S(2)}, u32[]{:S(2)}) async-start(f32[16,1,2048]{2,1,0:T(1,128)} %reshape.397), calls=%async_computation.3 | async-start | bytes 262144 | tf_op jit(solution)/shard_map/all_to_all | solution.py:97
  150.1 1.0 copy-start.8
where the time goes:
time: 153 us; the launch traced here: 152 us
  starting transfers between devices  56.7 us (37%)
  local copies, waits for them, and re-layouts  35 us (23%)
  waiting for transfers between devices  34.5 us (23%)
  other arithmetic  17.4 us (11%)
  between operations  5.98 us (4%)
  matrix products  2.87 us (2%)
    ppermute x8, starting transfers between devices, passed_along(): return lax.ppermute(block, axis, route)  28.9 us
    unnamed x33, local copies, waits for them, and re-layouts  17.1 us
    all_to_all x2, waiting for transfers between devices, slope(): lax.all_to_all(left_cols, 'col', split_axis=2, concat_axis=3, tiled=True)  15.7 us
    all_to_all x2, starting transfers between devices, slope(): lax.all_to_all(state, 'col', split_axis=3, concat_axis=2, tiled=True)  14.7 us
    all_to_all x2, starting transfers between devices, slope(): lax.all_to_all(left_cols, 'col', split_axis=2, concat_axis=3, tiled=True)  13 us
    ppermute x8, waiting for transfers between devices, passed_along(): return lax.ppermute(block, axis, route)  12.1 us
    gather x16, local copies, waits for them, and re-layouts, pick(): return [jnp.take(wide, positions[j], axis=0) * masks[j] for j in range(4)]  8.91 us
    add x8, other arithmetic, combine(): rise * upward[:, 0] + fall * (real * downward[:, 0] - imag * downward[:, 1])  7.95 us
  transfers between devices with their start and end apart: 12, of which 6 were waited for; matrix products, arithmetic and copies ran while one was open for 10% of the time, Pallas kernels for 0%

commit v1 on v0

v1 whole, which is shorter than its diff:
```python
import jax
import jax.numpy as jnp
import numpy as np
from jax import lax
from jax.experimental import pallas as pl
from jax.experimental.pallas import tpu as pltpu
from jax.sharding import Mesh, PartitionSpec as P

STEP = 0.2
HALF2 = 0.5 * STEP * STEP
SLOTS = 4
BF = jnp.bfloat16
F32 = jnp.float32


def split(v):
    hi = v.astype(BF)
    return hi, (v - hi.astype(F32)).astype(BF)


def dot(a, b):
    return jnp.dot(a, b, preferred_element_type=F32)


def granules(vs):
    lane = lax.broadcasted_iota(jnp.int32, vs[0].shape, 1) // 16
    for bit in (4, 2, 1):
        low = (lane & bit) == 0
        out = list(vs)
        for a in range(8):
            if not a & bit:
                b = a | bit
                out[a] = jnp.where(low, vs[a], pltpu.roll(vs[b], 16 * bit, 1))
                out[b] = jnp.where(low, pltpu.roll(vs[a], 128 - 16 * bit, 1), vs[b])
        vs = out
    return vs


class Nodes:
    def __init__(self, count_ref, table_ref, gamma_ref, first, below, above):
        total = jnp.int32(0)
        begin = jnp.int32(0)
        shards = count_ref.shape[0]
        for j in range(shards):
            c = count_ref[j]
            total = total + c
            begin = begin + jnp.where(j < first, c, 0)
        self.live = (total >> 1) << 1
        self.base = begin - 4
        self.begin = begin
        self.table = table_ref
        self.gamma = gamma_ref
        counts = [count_ref[jnp.clip(first + i, 0, shards - 1)] for i in range(-below, above)]
        self.counts = counts
        offs = [begin]
        for i in range(below - 1, -1, -1):
            offs.insert(0, offs[0] - counts[i])
        for i in range(below, len(counts) - 1):
            offs.append(offs[-1] + counts[i])
        self.offs = offs

    def slot(self, p):
        g = self.base + p
        which = jnp.int32(0)
        off = self.offs[0]
        for o in self.offs[1:]:
            inside = g >= o
            which = which + inside.astype(jnp.int32)
            off = jnp.where(inside, o, off)
        return which * SLOTS + jnp.clip(g - off, 0, SLOTS - 1)

    def root(self, n):
        return self.table[jnp.clip(n, 0, self.table.shape[0] - 1)]

    def up(self, p):
        g = self.base + p
        return jnp.where((g >= 0) & (g + 2 < self.live), self.root((g >> 1) + 1), 0.0)

    def down(self, p):
        g = self.base + p
        return jnp.where((g >= 2) & (g < self.live), self.root(g >> 1), 0.0)

    def middle(self, p):
        g = self.base + p
        n = (g >> 1).astype(F32)
        ok = (g >= 0) & (g < self.live)
        upper = jnp.where(ok & (g + 2 < self.live), n + 1.0, 0.0)
        return upper + jnp.where(ok & (g >= 2), n, 0.0)

    def even(self, p):
        g = self.base + p
        return jnp.where((g >= 0) & (g < self.live) & ((g & 1) == 0), 1.0, 0.0).astype(F32)

    def odd(self, p):
        g = self.base + p
        return jnp.where((g >= 0) & (g < self.live) & ((g & 1) == 1), 1.0, 0.0).astype(F32)

    def damp(self, p):
        g = self.base + p
        n0 = (g >> 1).astype(F32)
        n1 = (g & 1).astype(F32)
        return n0 * self.gamma[0] + n1 * self.gamma[1]


def scaled(s, v):
    return (s * v[0], s * v[1])


def plus(a, b):
    return (a[0] + b[0], a[1] + b[1])


def times(re, im, v):
    return (re * v[0] - im * v[1], re * v[1] + im * v[0])


def both(nodes, x, p, re, im):
    r = plus(scaled(nodes.up(p), x[p + 2]), scaled(re * nodes.down(p), x[p - 2]))
    t = scaled(im * nodes.down(p), x[p - 2])
    return (r[0] - t[1], r[1] + t[0]), (r[0] + t[1], r[1] - t[0])


def both1(nodes, x, p, re, im):
    r = plus(scaled(nodes.even(p), x[p + 1]), scaled(re * nodes.odd(p), x[p - 1]))
    t = scaled(im * nodes.odd(p), x[p - 1])
    return (r[0] - t[1], r[1] + t[0]), (r[0] + t[1], r[1] - t[0])


def first_order(nodes, x, p, re, im):
    here = nodes.damp(p)

    def w(q):
        return STEP - HALF2 * (here + nodes.damp(q))

    zero = scaled(w(p), x[p])
    up, down = scaled(w(p + 2) * nodes.up(p), x[p + 2]), scaled(w(p - 2) * nodes.down(p), x[p - 2])
    one = plus(up, times(re[0], im[0], down))
    up, down = scaled(w(p + 1) * nodes.even(p), x[p + 1]), scaled(w(p - 1) * nodes.odd(p), x[p - 1])
    two = plus(up, times(re[1], im[1], down))
    return zero, one, two


def put(hi_ref, lo_ref, block, col, j, rows, v):
    hi, lo = split(jnp.concatenate([v[0], v[1]], axis=0))
    at = pl.ds(block * 128 + j * rows, rows)
    hi_ref[at, 256 * col : 256 * col + 256] = hi
    lo_ref[at, 256 * col : 256 * col + 256] = lo


def times_weights(hi_ref, lo_ref, ghi_ref, glo_ref):
    hi, g = hi_ref[...], ghi_ref[...]
    return dot(hi, g) + dot(lo_ref[...], g) + dot(hi, glo_ref[...])


def weights_kernel(h_ref, q_ref, vhi, vlo, hhi, hlo):
    for b in range(3):
        hi, lo = split(h_ref[...] if b == 0 else q_ref[b - 1])
        vhi[256 * b : 256 * b + 256, :] = hi
        vlo[256 * b : 256 * b + 256, :] = lo
        hhi[:, 256 * b : 256 * b + 256] = hi
        hlo[:, 256 * b : 256 * b + 256] = lo


def pack_kernel(x_ref, near_ref, far_ref, o_ref):
    for g, ref in enumerate((x_ref, near_ref, far_ref)):
        o_ref[:, 8 * g : 8 * g + 8, :] = ref[...].T.reshape(32, 8, 128)


def column_kernel(
    me_ref, count_ref, table_ref, gamma_ref, coeff_ref, got_ref, ghi_ref, glo_ref, o_ref, y_ref, hi_ref, lo_ref, hi2_ref, lo2_ref, z_ref
):
    nodes = Nodes(count_ref, table_ref, gamma_ref, 2 * me_ref[0], 2, 4)
    re = (coeff_ref[0, 0], coeff_ref[1, 0])
    im = (coeff_ref[0, 1], coeff_ref[1, 1])
    places = ((2, 0), (1, 0), (0, 0), (0, 1), (1, 1), (2, 1))
    for i, (g, r) in enumerate(places):
        vs = []
        for low in range(8):
            vs.append(jnp.concatenate([got_ref[(8 * high + low) * 2 + r, 8 * g : 8 * g + 8, :] for high in range(2)], axis=0))
        for m, v in enumerate(granules(vs)):
            y_ref[SLOTS * i + m // 2, m % 2] = jnp.concatenate([v[:8], v[8:]], axis=1)
    x = []
    for p in range(16):
        v = y_ref[nodes.slot(p)]
        x.append((v[0], v[1]))
    a2, b2 = {}, {}
    for p in range(2, 14):
        a2[p], b2[p] = both1(nodes, x, p, re[1], im[1])
    for j in range(8):
        p = j + 4
        a1, b1 = both(nodes, x, p, re[0], im[0])
        a12, b1a2 = both(nodes, a2, p, re[0], im[0])
        a1b2, _ = both(nodes, b2, p, re[0], im[0])
        far = scaled(nodes.up(p) * nodes.up(p + 2), x[p + 4])
        low = scaled(nodes.down(p) * nodes.down(p - 2), x[p - 4])
        mid = nodes.middle(p)
        here = scaled(mid, x[p])
        a11 = plus(plus(far, times(re[0], im[0], here)), times(re[0] * re[0] - im[0] * im[0], 2.0 * re[0] * im[0], low))
        s11 = plus(plus(scaled(2.0, far), scaled(2.0 * re[0], here)), scaled(2.0 * (re[0] * re[0] + im[0] * im[0]), low))
        rows = (
            (x[p], a1, a2[p]),
            (a1, a11, a12),
            (a2[p], a12, times(re[1], im[1], x[p])),
            (scaled(2.0, b1), s11, scaled(2.0, b1a2)),
            (scaled(2.0, b2[p]), scaled(2.0, a1b2), scaled(2.0 * re[1], x[p])),
        )
        for block, row in enumerate(rows):
            for col, v in enumerate(row):
                put(hi_ref, lo_ref, block, col, j, 16, v)
    sums = times_weights(hi_ref, lo_ref, ghi_ref, glo_ref)
    for j in range(8):
        p = j + 4
        for block, v in enumerate(first_order(nodes, x, p, re, im)):
            s = sums[block * 128 + 16 * j : block * 128 + 16 * j + 16]
            put(hi2_ref, lo2_ref, 0, block, j, 16, (v[1] - HALF2 * s[:8], -v[0] - HALF2 * s[8:]))
        z_ref[1, j] = (2.0 * HALF2) * sums[16 * j : 16 * j + 16].reshape(2, 8, 256)
        z_ref[2, j] = HALF2 * sums[384 + 16 * j : 400 + 16 * j].reshape(2, 8, 256)
        z_ref[3, j] = HALF2 * sums[512 + 16 * j : 528 + 16 * j].reshape(2, 8, 256)
    z_ref[0] = times_weights(hi2_ref, lo2_ref, ghi_ref, glo_ref).reshape(8, 2, 8, 256)
    own = nodes.counts[2]
    for z in range(4):
        for r in range(2):
            vs = []
            for m in range(8):
                v = z_ref[z, m // 2 if r == 0 else own + m // 2, m % 2]
                vs.append(jnp.concatenate([v[:, :128], v[:, 128:]], axis=0))
            for low, v in enumerate(granules(vs)):
                for high in range(2):
                    o_ref[(8 * high + low) * 2 + r, 8 * z : 8 * z + 8, :] = v[8 * high : 8 * high + 8]


def row_kernel(
    me_ref, count_ref, table_ref, gamma_ref, coeff_ref, x_ref, p1_ref, p2_ref, p3_ref, p4_ref, ghi_ref, glo_ref, o_ref, w_ref, hi_ref, lo_ref, hi2_ref, lo2_ref
):
    me = me_ref[0] * 2 + me_ref[1]
    nodes = Nodes(count_ref, table_ref, gamma_ref, me, 2, 3)
    re = (coeff_ref[0, 0], coeff_ref[1, 0])
    im = (-coeff_ref[0, 1], -coeff_ref[1, 1])
    up = me_ref[1]
    w_ref[pl.ds(2 * SLOTS, SLOTS)] = x_ref[...]
    w_ref[pl.ds((1 + 2 * up) * SLOTS, SLOTS)] = p1_ref[...]
    w_ref[pl.ds(4 * up * SLOTS, SLOTS)] = p2_ref[...]
    w_ref[pl.ds((3 - 2 * up) * SLOTS, SLOTS)] = p3_ref[...]
    w_ref[pl.ds((4 - 4 * up) * SLOTS, SLOTS)] = p4_ref[...]
    x = []
    for p in range(12):
        v = w_ref[nodes.slot(p)]
        x.append((v[0], v[1]))
    b2 = {}
    for p in range(2, 10):
        b2[p], _ = both1(nodes, x, p, re[1], im[1])
    for j in range(4):
        p = j + 4
        b1, _ = both(nodes, x, p, re[0], im[0])
        b12, _ = both(nodes, b2, p, re[0], im[0])
        far = scaled(nodes.up(p) * nodes.up(p + 2), x[p + 4])
        low = scaled(nodes.down(p) * nodes.down(p - 2), x[p - 4])
        here = scaled(nodes.middle(p), x[p])
        b11 = plus(plus(far, times(re[0], im[0], here)), times(re[0] * re[0] - im[0] * im[0], 2.0 * re[0] * im[0], low))
        rows = ((x[p], b1, b2[p]), (b1, b11, b12), (b2[p], b12, times(re[1], im[1], x[p])))
        for block, row in enumerate(rows):
            for col, v in enumerate(row):
                put(hi_ref, lo_ref, block, col, j, 32, v)
    sums = times_weights(hi_ref, lo_ref, ghi_ref, glo_ref)
    for j in range(4):
        p = j + 4
        for block, v in enumerate(first_order(nodes, x, p, re, im)):
            s = sums[block * 128 + 32 * j : block * 128 + 32 * j + 32]
            put(hi2_ref, lo2_ref, 0, block, j, 32, (-v[1] - HALF2 * s[:16], v[0] - HALF2 * s[16:]))
    right = times_weights(hi2_ref, lo2_ref, ghi_ref, glo_ref)
    for j in range(4):
        d = nodes.damp(j + 4)
        keep = 1.0 - STEP * d + HALF2 * d * d
        old = x_ref[j].reshape(32, 256)
        live = (j < nodes.counts[2]) & (nodes.begin + j < nodes.live)
        o_ref[32 * j : 32 * j + 32, :] = jnp.where(live, keep * old + right[32 * j : 32 * j + 32], old)


def finish_kernel(me_ref, count_ref, got_ref, base_ref, ghi_ref, glo_ref, o_ref):
    me = me_ref[0] * 2 + me_ref[1]
    total = jnp.int32(0)
    begin = jnp.int32(0)
    for j in range(count_ref.shape[0]):
        c = count_ref[j]
        total = total + c
        begin = begin + jnp.where(j < me, c, 0)
    limit = (total >> 1) << 1
    his, los = [], []
    for z in range(1, 4):
        hi, lo = split(got_ref[:, 8 * z : 8 * z + 8, :].reshape(256, 128))
        his.append(hi)
        los.append(lo)
    hi, lo = jnp.concatenate(his, axis=0), jnp.concatenate(los, axis=0)
    g = ghi_ref[...]
    out = dot(g, hi) + dot(g, lo) + dot(glo_ref[...], hi) + got_ref[:, :8, :].reshape(256, 128)
    out = out.T
    for j in range(4):
        live = (j < count_ref[me]) & (begin + j < limit)
        rows = slice(32 * j, 32 * j + 32)
        o_ref[rows, :] = base_ref[rows, :] + jnp.where(live, out[rows], 0.0)


SMEM = pl.BlockSpec(memory_space=pltpu.SMEM)
VMEM = pl.BlockSpec(memory_space=pltpu.VMEM)


def call(kernel, outs, specs, scratch=(), flops=1_000_000, name=None):
    return pl.pallas_call(
        kernel,
        out_shape=outs,
        in_specs=specs,
        out_specs=jax.tree.map(lambda _: VMEM, outs),
        scratch_shapes=list(scratch),
        compiler_params=pltpu.CompilerParams(vmem_limit_bytes=48 * 1024 * 1024),
        cost_estimate=pl.CostEstimate(flops=flops, bytes_accessed=4_000_000, transcendentals=0),
        name=name,
    )


def struct(shape, dtype=F32):
    return jax.ShapeDtypeStruct(shape, dtype)


weights_call = call(
    weights_kernel,
    (struct((768, 256), BF), struct((768, 256), BF), struct((256, 768), BF), struct((256, 768), BF)),
    [VMEM] * 2,
    name="weights",
)
pack_call = call(pack_kernel, struct((32, 24, 128)), [VMEM] * 3, name="pack")
column_call = call(
    column_kernel,
    struct((32, 32, 128)),
    [SMEM] * 5 + [VMEM] * 3,
    [
        pltpu.VMEM((24, 2, 8, 256), F32),
        pltpu.VMEM((640, 768), BF),
        pltpu.VMEM((640, 768), BF),
        pltpu.VMEM((128, 768), BF),
        pltpu.VMEM((128, 768), BF),
        pltpu.VMEM((4, 8, 2, 8, 256), F32),
    ],
    flops=1_000_000_000,
    name="columns",
)
row_call = call(
    row_kernel,
    struct((128, 256)),
    [SMEM] * 5 + [VMEM] * 7,
    [
        pltpu.VMEM((20, 2, 16, 256), F32),
        pltpu.VMEM((384, 768), BF),
        pltpu.VMEM((384, 768), BF),
        pltpu.VMEM((128, 768), BF),
        pltpu.VMEM((128, 768), BF),
    ],
    flops=1_000_000_000,
    name="rows",
)
finish_call = call(finish_kernel, struct((128, 256)), [SMEM] * 2 + [VMEM] * 4, flops=300_000_000, name="finish")


def swap_routes(shards):
    pairs = [(i, i + 1) for i in range(1, shards - 1, 2)]
    near = pairs + [(b, a) for a, b in pairs]
    far = [(i, i + 2) for i in range(0, shards - 2, 2)] + [(i, i - 2) for i in range(3, shards, 2)]
    pairs = [(i, i + 1) for i in range(0, shards, 2)]
    inner = pairs + [(b, a) for a, b in pairs]
    back = [(i, i - 2) for i in range(2, shards, 2)] + [(i, i + 2) for i in range(1, shards - 2, 2)]
    return near, far, inner, back


def on_device(densities, hamiltonian, couplings, gamma, coeff, node_count):
    hier = ("team", "r")
    group = ("col", "r")
    table = jnp.asarray(np.sqrt(np.arange(72, dtype=np.float32)))
    me = jnp.stack([lax.axis_index("team"), lax.axis_index("r")]).astype(jnp.int32)
    near, far, inner, back = swap_routes(node_count.shape[0])
    flat = densities.reshape(128, 256)
    p1 = lax.ppermute(densities, hier, near)
    p2 = lax.ppermute(densities, hier, far)
    vhi, vlo, hhi, hlo = weights_call(hamiltonian, couplings)
    sent = pack_call(flat, p1.reshape(128, 256), p2.reshape(128, 256))
    got = lax.all_to_all(sent, group, 0, 0, tiled=True)
    back_sent = column_call(me, node_count, table, gamma, coeff, got, vhi, vlo)
    back_sent, again = lax.optimization_barrier((back_sent, densities))
    p3 = lax.ppermute(again, hier, inner)
    p4 = lax.ppermute(again, hier, back)
    back_got = lax.all_to_all(back_sent, group, 0, 0, tiled=True)
    base = row_call(me, node_count, table, gamma, coeff, densities, p1, p2, p3, p4, vhi, vlo)
    out = finish_call(me, node_count, back_got, base, hhi, hlo)
    return out.reshape(4, 2, 16, 256)


def solution(mesh):
    devices = mesh.devices
    inside = Mesh(devices.reshape(devices.shape[0] // 2, 2, devices.shape[1]), ("team", "r", "col"))
    spec = P(("team", "r"), None, "col", None)
    return jax.shard_map(
        on_device,
        mesh=inside,
        in_specs=(spec, P(), P(), P(), P(), P()),
        out_specs=spec,
        check_vma=False,
    )
```

time: 153 us -> 73.3 us (0.48)
  the two profiles are of different devices: /device:TPU:31 before, /device:TPU:24 now
where the time goes in v1:
time: 73.3 us; the launch traced here: 72.8 us
  waiting for transfers between devices  32.7 us (45%)
  starting transfers between devices  30.1 us (41%)
  Pallas kernels  8.19 us (11%)
  local copies, waits for them, and re-layouts  1.61 us (2%)
    all_to_all x1, waiting for transfers between devices, on_device(): got = lax.all_to_all(sent, group, 0, 0, tiled=True)  14.9 us
    all_to_all x1, starting transfers between devices, on_device(): got = lax.all_to_all(sent, group, 0, 0, tiled=True)  10.8 us
    ppermute x1, waiting for transfers between devices, on_device(): p4 = lax.ppermute(again, hier, back)  9.82 us
    ppermute x1, waiting for transfers between devices, on_device(): p2 = lax.ppermute(densities, hier, far)  4.59 us
    ppermute x1, starting transfers between devices, on_device(): p1 = lax.ppermute(densities, hier, near)  4.54 us
    ppermute x1, starting transfers between devices, on_device(): p4 = lax.ppermute(again, hier, back)  4.3 us
    all_to_all x1, starting transfers between devices, on_device(): back_got = lax.all_to_all(back_sent, group, 0, 0, tiled=True)  4.02 us
    ppermute x1, starting transfers between devices, on_device(): p3 = lax.ppermute(again, hier, inner)  3.59 us
  transfers between devices with their start and end apart: 6, of which 5 were waited for; matrix products, arithmetic and copies ran while one was open for 0% of the time, Pallas kernels for 3%

profile of v1, /device:TPU:24, one launch (start us, length us, event | category | flops | bytes accessed | tf_op | source)
XLA Modules:
  0.0 72.8 jit_solution(2130783080498910070)
XLA Ops:
  0.0 4.5 %collective-permute-start = (f32[4,2,16,256]{3,2,1,0:T(8,128)}, f32[4,2,16,256]{3,2,1,0:T(8,128)S(1)}, u32[]{:S(2)}, u32[]{:S(2)}) collective-permute-start(f32[4,2,16,256]{3,2,1,0:T(8,128)} %x_ref.1), channel_id=1, source_target_pairs={{16,32},{48,64},{80,96},{112,128},{144,160},{176,192},{208,224},{2... | collective-permute-start | bytes 393224 | tf_op jit(solution)/shard_map/ppermute | solution.py:380
  4.6 2.8 %collective-permute-start.1 = (f32[4,2,16,256]{3,2,1,0:T(8,128)}, f32[4,2,16,256]{3,2,1,0:T(8,128)S(1)}, u32[]{:S(2)}, u32[]{:S(2)}) collective-permute-start(f32[4,2,16,256]{3,2,1,0:T(8,128)} %x_ref.1), channel_id=1, source_target_pairs={{0,32},{32,64},{64,96},{96,128},{128,160},{160,192},{192,224},{224... | collective-permute-start | bytes 393224 | tf_op jit(solution)/shard_map/ppermute | solution.py:381
  7.4 2.1 %collective-permute-done.p1_ref = f32[4,2,16,256]{3,2,1,0:T(8,128)S(1)} collective-permute-done((f32[4,2,16,256]{3,2,1,0:T(8,128)}, f32[4,2,16,256]{3,2,1,0:T(8,128)S(1)}, u32[]{:S(2)}, u32[]{:S(2)}) %collective-permute-start) | collective-permute-done | bytes 131104 | tf_op jit(solution)/shard_map/ppermute | solution.py:380
  9.4 4.6 %collective-permute-done.1.p2_ref = f32[4,2,16,256]{3,2,1,0:T(8,128)S(1)} collective-permute-done((f32[4,2,16,256]{3,2,1,0:T(8,128)}, f32[4,2,16,256]{3,2,1,0:T(8,128)S(1)}, u32[]{:S(2)}, u32[]{:S(2)}) %collective-permute-start.1) | collective-permute-done | bytes 131104 | tf_op jit(solution)/shard_map/ppermute | solution.py:381
  14.0 0.9 %copy-done.2 = f32[4,2,16,256]{3,2,1,0:T(8,128)S(1)} copy-done((f32[4,2,16,256]{3,2,1,0:T(8,128)S(1)}, f32[4,2,16,256]{3,2,1,0:T(8,128)}, u32[]{:S(2)}) %copy-start.2) | copy-done | bytes 131096
  14.9 0.9 %pack.1 = f32[32,24,128]{2,1,0:T(8,128)} custom-call(f32[128,256]{1,0:T(8,128)S(1)} %bitcast.6, f32[128,256]{1,0:T(8,128)S(1)} %bitcast.7, f32[128,256]{1,0:T(8,128)S(1)} %bitcast.8), custom_call_target="tpu_custom_call" | custom-call | flops 1000000 | bytes 4000000 | tf_op jit(solution)/shard_map/pack/pallas_call | solution.py:383
  15.9 10.8 %all-to-all-start = ((f32[32,24,128]{2,1,0:T(8,128)}), f32[32,24,128]{2,1,0:T(8,128)S(1)}, u32[]{:S(2)}, u32[]{:S(2)}) async-start(f32[32,24,128]{2,1,0:T(8,128)} %pack.1), calls=%async_computation | async-start | bytes 786432 | tf_op jit(solution)/shard_map/all_to_all | solution.py:384
  26.7 0.0 copy-done
  26.7 0.0 copy-start.6
  26.7 0.0 copy-start.7
  26.8 0.1 weights.1
  26.9 0.1 pad_add_fusion.me_ref
  27.0 14.9 %all-to-all-done.got_ref = f32[32,24,128]{2,1,0:T(8,128)S(1)} async-done(((f32[32,24,128]{2,1,0:T(8,128)}), f32[32,24,128]{2,1,0:T(8,128)S(1)}, u32[]{:S(2)}, u32[]{:S(2)}) %all-to-all-start) | async-done | bytes 393248 | tf_op jit(solution)/shard_map/all_to_all | solution.py:384
  41.9 0.6 copy-done.4
  42.5 0.0 copy-done.5
  42.6 3.6 %columns.1 = f32[32,32,128]{2,1,0:T(8,128)} custom-call(s32[2]{0:T(128)S(1)} %pad_add_fusion.me_ref, s32[32]{0:T(128)S(1)} %copy-done.4, f32[72]{0:T(128)S(1)} %copy-done.7, f32[2]{0:T(128)S(1)} %copy-done.6, f32[2,2]{1,0:T(2,128)S(1)} %copy-done.5, f32[32,24,128]{2,1,0:T(8,128)S(1)} %all-to-all-done.got_ref, ...), custom_call_target="tpu_custom_call" | custom-call | flops 1000000000 | bytes 4000000 | tf_op jit(solution)/shard_map/columns/pallas_call | solution.py:385
  46.2 4.0 %all-to-all-start.1 = ((f32[32,32,128]{2,1,0:T(8,128)}), f32[32,32,128]{2,1,0:T(8,128)S(1)}, u32[]{:S(2)}, u32[]{:S(2)}) async-start(f32[32,32,128]{2,1,0:T(8,128)} %columns.1), calls=%async_computation.1 | async-start | bytes 1048576 | tf_op jit(solution)/shard_map/all_to_all | solution.py:389
  50.2 3.6 %collective-permute-start.2 = (f32[4,2,16,256]{3,2,1,0:T(8,128)S(1)}, f32[4,2,16,256]{3,2,1,0:T(8,128)S(1)}, u32[]{:S(2)}, u32[]{:S(2)}) collective-permute-start(f32[4,2,16,256]{3,2,1,0:T(8,128)S(1)} %copy-done.3), channel_id=1, source_target_pairs={{0,16},{32,48},{64,80},{96,112},{128,144},{160,176},{192,208},{224... | collective-permute-start | bytes 393224 | tf_op jit(solution)/shard_map/ppermute | solution.py:387
  53.8 4.3 %collective-permute-start.3 = (f32[4,2,16,256]{3,2,1,0:T(8,128)S(1)}, f32[4,2,16,256]{3,2,1,0:T(8,128)S(1)}, u32[]{:S(2)}, u32[]{:S(2)}) collective-permute-start(f32[4,2,16,256]{3,2,1,0:T(8,128)S(1)} %copy-done.3), channel_id=1, source_target_pairs={{32,0},{64,32},{96,64},{128,96},{160,128},{192,160},{224,192},{256... | collective-permute-start | bytes 393224 | tf_op jit(solution)/shard_map/ppermute | solution.py:388
  58.1 1.3 %collective-permute-done.2.p3_ref = f32[4,2,16,256]{3,2,1,0:T(8,128)S(1)} collective-permute-done((f32[4,2,16,256]{3,2,1,0:T(8,128)S(1)}, f32[4,2,16,256]{3,2,1,0:T(8,128)S(1)}, u32[]{:S(2)}, u32[]{:S(2)}) %collective-permute-start.2) | collective-permute-done | bytes 131104 | tf_op jit(solution)/shard_map/ppermute | solution.py:387
  59.4 9.8 %collective-permute-done.3.p4_ref = f32[4,2,16,256]{3,2,1,0:T(8,128)S(1)} collective-permute-done((f32[4,2,16,256]{3,2,1,0:T(8,128)S(1)}, f32[4,2,16,256]{3,2,1,0:T(8,128)S(1)}, u32[]{:S(2)}, u32[]{:S(2)}) %collective-permute-start.3) | collective-permute-done | bytes 131104 | tf_op jit(solution)/shard_map/ppermute | solution.py:388
  69.2 1.8 %rows.1.base_ref = f32[128,256]{1,0:T(8,128)S(1)} custom-call(s32[2]{0:T(128)S(1)} %pad_add_fusion.me_ref, s32[32]{0:T(128)S(1)} %copy-done.4, f32[72]{0:T(128)S(1)} %copy-done.7, f32[2]{0:T(128)S(1)} %copy-done.6, f32[2,2]{1,0:T(2,128)S(1)} %copy-done.5, f32[4,2,16,256]{3,2,1,0:T(8,128)S(1)} %copy-done.3, ...), custom_call_target="tpu_custom_call" | custom-call | flops 1000000000 | bytes 4000000 | tf_op jit(solution)/shard_map/rows/pallas_call | solution.py:390
  71.1 0.0 all-to-all-done.1.got_ref
  71.1 1.7 %finish.1 = f32[128,256]{1,0:T(8,128)} custom-call(s32[2]{0:T(128)S(1)} %pad_add_fusion.me_ref, s32[32]{0:T(128)S(1)} %copy-done.4, f32[32,32,128]{2,1,0:T(8,128)S(1)} %all-to-all-done.1.got_ref, f32[128,256]{1,0:T(8,128)S(1)} %rows.1.base_ref, bf16[256,768]{1,0:T(8,128)(2,1)S(1)} %get-tuple-element.15.ghi_ref, bf16[256,768]{1,0:T(8,128)(2,1)S(1)} %get-tuple-element.16.glo_ref), custom_call_target="tpu_custom_call" | custom-call | flops 300000000 | bytes 4000000 | tf_op jit(solution)/shard_map/finish/pallas_call | solution.py:391
  (10 shorter events, 0.0 us)
Async XLA Ops:
  0.0 9.4 %collective-permute-start = (f32[4,2,16,256]{3,2,1,0:T(8,128)}, f32[4,2,16,256]{3,2,1,0:T(8,128)S(1)}, u32[]{:S(2)}, u32[]{:S(2)}) collective-permute-start(f32[4,2,16,256]{3,2,1,0:T(8,128)} %x_ref.1), channel_id=1, source_target_pairs={{16,32},{48,64},{80,96},{112,128},{144,160},{176,192},{208,224},{2... | collective-permute-start | bytes 393224 | tf_op jit(solution)/shard_map/ppermute | solution.py:380
  4.6 9.5 %collective-permute-start.1 = (f32[4,2,16,256]{3,2,1,0:T(8,128)}, f32[4,2,16,256]{3,2,1,0:T(8,128)S(1)}, u32[]{:S(2)}, u32[]{:S(2)}) collective-permute-start(f32[4,2,16,256]{3,2,1,0:T(8,128)} %x_ref.1), channel_id=1, source_target_pairs={{0,32},{32,64},{64,96},{96,128},{128,160},{160,192},{192,224},{224... | collective-permute-start | bytes 393224 | tf_op jit(solution)/shard_map/ppermute | solution.py:381
  14.0 0.9 %copy-start.2 = (f32[4,2,16,256]{3,2,1,0:T(8,128)S(1)}, f32[4,2,16,256]{3,2,1,0:T(8,128)}, u32[]{:S(2)}) copy-start(f32[4,2,16,256]{3,2,1,0:T(8,128)} %x_ref.1) | copy-start | bytes 393220
  15.9 10.9 %copy-start = (f32[2,256,256]{2,1,0:T(8,128)S(1)}, f32[2,256,256]{2,1,0:T(8,128)}, u32[]{:S(2)}) copy-start(f32[2,256,256]{2,1,0:T(8,128)} %q_ref.1) | copy-start | bytes 1572868
  15.9 10.9 %copy-start.1 = (f32[256,256]{1,0:T(8,128)S(1)}, f32[256,256]{1,0:T(8,128)}, u32[]{:S(2)}) copy-start(f32[256,256]{1,0:T(8,128)} %h_ref.1) | copy-start | bytes 786436
  15.9 26.0 %all-to-all-start = ((f32[32,24,128]{2,1,0:T(8,128)}), f32[32,24,128]{2,1,0:T(8,128)S(1)}, u32[]{:S(2)}, u32[]{:S(2)}) async-start(f32[32,24,128]{2,1,0:T(8,128)} %pack.1), calls=%async_computation | async-start | bytes 786432 | tf_op jit(solution)/shard_map/all_to_all | solution.py:384
  26.7 15.2 %copy-start.6 = (f32[2]{0:T(128)S(1)}, f32[2]{0:T(128)}, u32[]{:S(2)}) copy-start(f32[2]{0:T(128)} %gamma_ref.3) | copy-start | bytes 28
  26.7 15.1 %copy-start.7 = (f32[72]{0:T(128)S(1)}, f32[72]{0:T(128)}, u32[]{:S(2)}) copy-start(f32[72]{0:T(128)} %constant.13.clone.table_ref) | copy-start | bytes 868
  41.9 0.7 copy-start.4
  41.9 0.7 copy-start.5
  46.2 4.0 %copy-start.3 = (f32[4,2,16,256]{3,2,1,0:T(8,128)S(1)}, f32[4,2,16,256]{3,2,1,0:T(8,128)}, u32[]{:S(2)}) copy-start(f32[4,2,16,256]{3,2,1,0:T(8,128)} %x_ref.1) | copy-start | bytes 393220
  46.2 24.9 %all-to-all-start.1 = ((f32[32,32,128]{2,1,0:T(8,128)}), f32[32,32,128]{2,1,0:T(8,128)S(1)}, u32[]{:S(2)}, u32[]{:S(2)}) async-start(f32[32,32,128]{2,1,0:T(8,128)} %columns.1), calls=%async_computation.1 | async-start | bytes 1048576 | tf_op jit(solution)/shard_map/all_to_all | solution.py:389
  50.2 9.2 %collective-permute-start.2 = (f32[4,2,16,256]{3,2,1,0:T(8,128)S(1)}, f32[4,2,16,256]{3,2,1,0:T(8,128)S(1)}, u32[]{:S(2)}, u32[]{:S(2)}) collective-permute-start(f32[4,2,16,256]{3,2,1,0:T(8,128)S(1)} %copy-done.3), channel_id=1, source_target_pairs={{0,16},{32,48},{64,80},{96,112},{128,144},{160,176},{192,208},{224... | collective-permute-start | bytes 393224 | tf_op jit(solution)/shard_map/ppermute | solution.py:387
  53.8 15.4 %collective-permute-start.3 = (f32[4,2,16,256]{3,2,1,0:T(8,128)S(1)}, f32[4,2,16,256]{3,2,1,0:T(8,128)S(1)}, u32[]{:S(2)}, u32[]{:S(2)}) collective-permute-start(f32[4,2,16,256]{3,2,1,0:T(8,128)S(1)} %copy-done.3), channel_id=1, source_target_pairs={{32,0},{64,32},{96,64},{128,96},{160,128},{192,160},{224,192},{256... | collective-permute-start | bytes 393224 | tf_op jit(solution)/shard_map/ppermute | solution.py:388

commit v2 on v1

--- a/solution.py
+++ b/solution.py
@@ -1,6 +1,5 @@
 import jax
 import jax.numpy as jnp
-import numpy as np
 from jax import lax
 from jax.experimental import pallas as pl
 from jax.experimental.pallas import tpu as pltpu
@@ -9,6 +8,8 @@
 STEP = 0.2
 HALF2 = 0.5 * STEP * STEP
 SLOTS = 4
+TOTAL, TEAM_BEGIN, HERE_BEGIN, SIDE, COUNTS = 0, 1, 2, 3, 4
+ROOTS = 72
 BF = jnp.bfloat16
 F32 = jnp.float32
 
@@ -37,40 +38,17 @@
 
 
 class Nodes:
-    def __init__(self, count_ref, table_ref, gamma_ref, first, below, above):
-        total = jnp.int32(0)
-        begin = jnp.int32(0)
-        shards = count_ref.shape[0]
-        for j in range(shards):
-            c = count_ref[j]
-            total = total + c
-            begin = begin + jnp.where(j < first, c, 0)
-        self.live = (total >> 1) << 1
+    def __init__(self, ints_ref, reals_ref, begin):
+        self.live = (ints_ref[TOTAL] >> 1) << 1
+        self.begin = begin
         self.base = begin - 4
-        self.begin = begin
-        self.table = table_ref
-        self.gamma = gamma_ref
-        counts = [count_ref[jnp.clip(first + i, 0, shards - 1)] for i in range(-below, above)]
-        self.counts = counts
-        offs = [begin]
-        for i in range(below - 1, -1, -1):
-            offs.insert(0, offs[0] - counts[i])
-        for i in range(below, len(counts) - 1):
-            offs.append(offs[-1] + counts[i])
-        self.offs = offs
-
-    def slot(self, p):
-        g = self.base + p
-        which = jnp.int32(0)
-        off = self.offs[0]
-        for o in self.offs[1:]:
-            inside = g >= o
-            which = which + inside.astype(jnp.int32)
-            off = jnp.where(inside, o, off)
-        return which * SLOTS + jnp.clip(g - off, 0, SLOTS - 1)
+        self.reals = reals_ref
+        self.gamma = (reals_ref[0], reals_ref[1])
+        self.re = (reals_ref[2], reals_ref[4])
+        self.im = (reals_ref[3], reals_ref[5])
 
     def root(self, n):
-        return self.table[jnp.clip(n, 0, self.table.shape[0] - 1)]
+        return self.reals[jnp.clip(n, 0, ROOTS - 1) + 6]
 
     def up(self, p):
         g = self.base + p
@@ -161,27 +139,50 @@
         hlo[:, 256 * b : 256 * b + 256] = lo
 
 
-def pack_kernel(x_ref, near_ref, far_ref, o_ref):
-    for g, ref in enumerate((x_ref, near_ref, far_ref)):
-        o_ref[:, 8 * g : 8 * g + 8, :] = ref[...].T.reshape(32, 8, 128)
-
-
-def column_kernel(
-    me_ref, count_ref, table_ref, gamma_ref, coeff_ref, got_ref, ghi_ref, glo_ref, o_ref, y_ref, hi_ref, lo_ref, hi2_ref, lo2_ref, z_ref
-):
-    nodes = Nodes(count_ref, table_ref, gamma_ref, 2 * me_ref[0], 2, 4)
-    re = (coeff_ref[0, 0], coeff_ref[1, 0])
-    im = (coeff_ref[0, 1], coeff_ref[1, 1])
-    places = ((2, 0), (1, 0), (0, 0), (0, 1), (1, 1), (2, 1))
+def own_kernel(x_ref, o_ref, t_ref, sem):
+    t_ref[...] = x_ref[...].T.reshape(32, 8, 128)
+    copy = pltpu.make_async_copy(t_ref, o_ref.at[:, 0:8], sem)
+    copy.start()
+    copy.wait()
+
+
+def halo_kernel(ints_ref, near_ref, far_ref, _, o_ref, s_ref, t_ref, sem):
+    side = ints_ref[SIDE]
+    count = jnp.where(side == 0, ints_ref[COUNTS + 1], ints_ref[COUNTS + 3])
+    for i in range(4):
+        at = i + jnp.where(side == 0, count - 4, 0)
+        inside = jnp.where(side == 0, at >= 0, i < count)
+        other = jnp.where(side == 0, at + 2, i - count)
+        near = near_ref[jnp.clip(at, 0, 3)]
+        far = far_ref[jnp.clip(other, 0, 1)]
+        s_ref[32 * i : 32 * i + 32, :] = jnp.where(inside, near, far).reshape(32, 256)
+    t_ref[...] = s_ref[...].T.reshape(32, 8, 128)
+    copy = pltpu.make_async_copy(t_ref, o_ref.at[:, 8:16], sem)
+    copy.start()
+    copy.wait()
+
+
+def column_kernel(ints_ref, reals_ref, got_ref, ghi_ref, glo_ref, o_ref, y_ref, hi_ref, lo_ref, hi2_ref, lo2_ref, z_ref):
+    nodes = Nodes(ints_ref, reals_ref, ints_ref[TEAM_BEGIN])
+    own, other = ints_ref[COUNTS + 2 - ints_ref[SIDE]], ints_ref[COUNTS + 3 - ints_ref[SIDE]]
+    re, im = nodes.re, nodes.im
+    places = ((1, 0), (0, 0), (0, 1), (1, 1))
     for i, (g, r) in enumerate(places):
         vs = []
         for low in range(8):
             vs.append(jnp.concatenate([got_ref[(8 * high + low) * 2 + r, 8 * g : 8 * g + 8, :] for high in range(2)], axis=0))
         for m, v in enumerate(granules(vs)):
             y_ref[SLOTS * i + m // 2, m % 2] = jnp.concatenate([v[:8], v[8:]], axis=1)
+
+    def slot(p):
+        j = p - 4
+        if j < 0:
+            return p
+        return jnp.where(j < own, 4 + j, jnp.where(j < own + other, 8 + j - own, jnp.minimum(12 + j - own - other, 15)))
+
     x = []
     for p in range(16):
-        v = y_ref[nodes.slot(p)]
+        v = y_ref[slot(p)]
         x.append((v[0], v[1]))
     a2, b2 = {}, {}
     for p in range(2, 14):
@@ -217,7 +218,6 @@
         z_ref[2, j] = HALF2 * sums[384 + 16 * j : 400 + 16 * j].reshape(2, 8, 256)
         z_ref[3, j] = HALF2 * sums[512 + 16 * j : 528 + 16 * j].reshape(2, 8, 256)
     z_ref[0] = times_weights(hi2_ref, lo2_ref, ghi_ref, glo_ref).reshape(8, 2, 8, 256)
-    own = nodes.counts[2]
     for z in range(4):
         for r in range(2):
             vs = []
@@ -230,21 +230,27 @@
 
 
 def row_kernel(
-    me_ref, count_ref, table_ref, gamma_ref, coeff_ref, x_ref, p1_ref, p2_ref, p3_ref, p4_ref, ghi_ref, glo_ref, o_ref, w_ref, hi_ref, lo_ref, hi2_ref, lo2_ref
+    ints_ref, reals_ref, x_ref, p1_ref, p2_ref, p3_ref, p4_ref, ghi_ref, glo_ref, o_ref, w_ref, hi_ref, lo_ref, hi2_ref, lo2_ref
 ):
-    me = me_ref[0] * 2 + me_ref[1]
-    nodes = Nodes(count_ref, table_ref, gamma_ref, me, 2, 3)
-    re = (coeff_ref[0, 0], coeff_ref[1, 0])
-    im = (-coeff_ref[0, 1], -coeff_ref[1, 1])
-    up = me_ref[1]
-    w_ref[pl.ds(2 * SLOTS, SLOTS)] = x_ref[...]
-    w_ref[pl.ds((1 + 2 * up) * SLOTS, SLOTS)] = p1_ref[...]
-    w_ref[pl.ds(4 * up * SLOTS, SLOTS)] = p2_ref[...]
-    w_ref[pl.ds((3 - 2 * up) * SLOTS, SLOTS)] = p3_ref[...]
-    w_ref[pl.ds((4 - 4 * up) * SLOTS, SLOTS)] = p4_ref[...]
+    nodes = Nodes(ints_ref, reals_ref, ints_ref[HERE_BEGIN])
+    re, im = nodes.re, (-nodes.im[0], -nodes.im[1])
+    up = ints_ref[SIDE]
+    below, own, above = ints_ref[COUNTS + 1], ints_ref[COUNTS + 2], ints_ref[COUNTS + 3]
+    w_ref[8:12] = x_ref[...]
+    w_ref[pl.ds(4 + 8 * up, 4)] = p1_ref[...]
+    w_ref[pl.ds(2 + 14 * up, 2)] = p2_ref[...]
+    w_ref[pl.ds(12 - 8 * up, 4)] = p3_ref[...]
+    w_ref[pl.ds(16 - 14 * up, 2)] = p4_ref[...]
+
+    def slot(p):
+        j = p - 4
+        if j < 0:
+            return 4 + j + below
+        return jnp.where(j < own, 8 + j, jnp.where(j < own + above, 12 + j - own, jnp.minimum(16 + j - own - above, 17)))
+
     x = []
     for p in range(12):
-        v = w_ref[nodes.slot(p)]
+        v = w_ref[slot(p)]
         x.append((v[0], v[1]))
     b2 = {}
     for p in range(2, 10):
@@ -272,19 +278,12 @@
         d = nodes.damp(j + 4)
         keep = 1.0 - STEP * d + HALF2 * d * d
         old = x_ref[j].reshape(32, 256)
-        live = (j < nodes.counts[2]) & (nodes.begin + j < nodes.live)
+        live = (j < own) & (nodes.begin + j < nodes.live)
         o_ref[32 * j : 32 * j + 32, :] = jnp.where(live, keep * old + right[32 * j : 32 * j + 32], old)
 
 
-def finish_kernel(me_ref, count_ref, got_ref, base_ref, ghi_ref, glo_ref, o_ref):
-    me = me_ref[0] * 2 + me_ref[1]
-    total = jnp.int32(0)
-    begin = jnp.int32(0)
-    for j in range(count_ref.shape[0]):
-        c = count_ref[j]
-        total = total + c
-        begin = begin + jnp.where(j < me, c, 0)
-    limit = (total >> 1) << 1
+def finish_kernel(ints_ref, got_ref, base_ref, ghi_ref, glo_ref, o_ref):
+    own, begin, limit = ints_ref[COUNTS + 2], ints_ref[HERE_BEGIN], (ints_ref[TOTAL] >> 1) << 1
     his, los = [], []
     for z in range(1, 4):
         hi, lo = split(got_ref[:, 8 * z : 8 * z + 8, :].reshape(256, 128))
@@ -295,21 +294,23 @@
     out = dot(g, hi) + dot(g, lo) + dot(glo_ref[...], hi) + got_ref[:, :8, :].reshape(256, 128)
     out = out.T
     for j in range(4):
-        live = (j < count_ref[me]) & (begin + j < limit)
+        live = (j < own) & (begin + j < limit)
         rows = slice(32 * j, 32 * j + 32)
         o_ref[rows, :] = base_ref[rows, :] + jnp.where(live, out[rows], 0.0)
 
 
 SMEM = pl.BlockSpec(memory_space=pltpu.SMEM)
 VMEM = pl.BlockSpec(memory_space=pltpu.VMEM)
-
-
-def call(kernel, outs, specs, scratch=(), flops=1_000_000, name=None):
+ANY = pl.BlockSpec(memory_space=pl.ANY)
+
+
+def call(kernel, outs, specs, scratch=(), flops=1_000_000, name=None, out_specs=None, aliases=None):
     return pl.pallas_call(
         kernel,
         out_shape=outs,
         in_specs=specs,
-        out_specs=jax.tree.map(lambda _: VMEM, outs),
+        out_specs=out_specs or jax.tree.map(lambda _: VMEM, outs),
+        input_output_aliases=aliases or {},
         scratch_shapes=list(scratch),
         compiler_params=pltpu.CompilerParams(vmem_limit_bytes=48 * 1024 * 1024),
         cost_estimate=pl.CostEstimate(flops=flops, bytes_accessed=4_000_000, transcendentals=0),
@@ -327,13 +328,24 @@
     [VMEM] * 2,
     name="weights",
 )
-pack_call = call(pack_kernel, struct((32, 24, 128)), [VMEM] * 3, name="pack")
+own_call = call(
+    own_kernel, struct((32, 16, 128)), [VMEM], [pltpu.VMEM((32, 8, 128), F32), pltpu.SemaphoreType.DMA], out_specs=ANY, name="own"
+)
+halo_call = call(
+    halo_kernel,
+    struct((32, 16, 128)),
+    [SMEM] + [VMEM] * 2 + [ANY],
+    [pltpu.VMEM((128, 256), F32), pltpu.VMEM((32, 8, 128), F32), pltpu.SemaphoreType.DMA],
+    out_specs=ANY,
+    aliases={3: 0},
+    name="halo",
+)
 column_call = call(
     column_kernel,
     struct((32, 32, 128)),
-    [SMEM] * 5 + [VMEM] * 3,
+    [SMEM] * 2 + [VMEM] * 3,
     [
-        pltpu.VMEM((24, 2, 8, 256), F32),
+        pltpu.VMEM((16, 2, 8, 256), F32),
         pltpu.VMEM((640, 768), BF),
         pltpu.VMEM((640, 768), BF),
         pltpu.VMEM((128, 768), BF),
@@ -346,9 +358,9 @@
 row_call = call(
     row_kernel,
     struct((128, 256)),
-    [SMEM] * 5 + [VMEM] * 7,
+    [SMEM] * 2 + [VMEM] * 7,
     [
-        pltpu.VMEM((20, 2, 16, 256), F32),
+        pltpu.VMEM((18, 2, 16, 256), F32),
         pltpu.VMEM((384, 768), BF),
         pltpu.VMEM((384, 768), BF),
         pltpu.VMEM((128, 768), BF),
@@ -357,7 +369,7 @@
     flops=1_000_000_000,
     name="rows",
 )
-finish_call = call(finish_kernel, struct((128, 256)), [SMEM] * 2 + [VMEM] * 4, flops=300_000_000, name="finish")
+finish_call = call(finish_kernel, struct((128, 256)), [SMEM] + [VMEM] * 4, flops=300_000_000, name="finish")
 
 
 def swap_routes(shards):
@@ -370,25 +382,45 @@
     return near, far, inner, back
 
 
+def integers(node_count):
+    shards = node_count.shape[0]
+    team, side = lax.axis_index("team"), lax.axis_index("r")
+    here = 2 * team + side
+    row = jnp.arange(16, dtype=jnp.int32)[:, None]
+    column = jnp.arange(shards, dtype=jnp.int32)[None, :]
+    near = jnp.clip(here + row - (COUNTS + 2), 0, shards - 1)
+    wanted = (
+        (row == TOTAL)
+        | ((row == TEAM_BEGIN) & (column < 2 * team))
+        | ((row == HERE_BEGIN) & (column < here))
+        | ((row >= COUNTS) & (column == near))
+    )
+    sums = jnp.sum(jnp.where(wanted, node_count[None, :], 0), axis=1)
+    return sums + jnp.where(row[:, 0] == SIDE, side, 0)
+
+
 def on_device(densities, hamiltonian, couplings, gamma, coeff, node_count):
     hier = ("team", "r")
     group = ("col", "r")
-    table = jnp.asarray(np.sqrt(np.arange(72, dtype=np.float32)))
-    me = jnp.stack([lax.axis_index("team"), lax.axis_index("r")]).astype(jnp.int32)
+    ints = integers(node_count)
+    reals = jnp.concatenate([gamma, coeff.reshape(4), jnp.sqrt(jnp.arange(ROOTS, dtype=F32))])
     near, far, inner, back = swap_routes(node_count.shape[0])
-    flat = densities.reshape(128, 256)
     p1 = lax.ppermute(densities, hier, near)
-    p2 = lax.ppermute(densities, hier, far)
+    tail = ints[COUNTS + 2] - 2
+    side = lax.axis_index("r")
+    p2 = lax.ppermute(lax.dynamic_slice_in_dim(densities, jnp.where(side == 0, tail, 0), 2, 0), hier, far)
+    part = own_call(densities.reshape(128, 256))
     vhi, vlo, hhi, hlo = weights_call(hamiltonian, couplings)
-    sent = pack_call(flat, p1.reshape(128, 256), p2.reshape(128, 256))
+    sent = halo_call(ints, p1, p2, part)
+    sent, again = lax.optimization_barrier((sent, densities))
     got = lax.all_to_all(sent, group, 0, 0, tiled=True)
-    back_sent = column_call(me, node_count, table, gamma, coeff, got, vhi, vlo)
-    back_sent, again = lax.optimization_barrier((back_sent, densities))
     p3 = lax.ppermute(again, hier, inner)
-    p4 = lax.ppermute(again, hier, back)
+    p4 = lax.ppermute(lax.dynamic_slice_in_dim(again, jnp.where(side == 0, 0, tail), 2, 0), hier, back)
+    back_sent = column_call(ints, reals, got, vhi, vlo)
+    back_sent, p3, p4 = lax.optimization_barrier((back_sent, p3, p4))
     back_got = lax.all_to_all(back_sent, group, 0, 0, tiled=True)
-    base = row_call(me, node_count, table, gamma, coeff, densities, p1, p2, p3, p4, vhi, vlo)
-    out = finish_call(me, node_count, back_got, base, hhi, hlo)
+    base = row_call(ints, reals, densities, p1, p2, p3, p4, vhi, vlo)
+    out = finish_call(ints, back_got, base, hhi, hlo)
     return out.reshape(4, 2, 16, 256)
 
 

time: 73.3 us -> 73.1 us (level)
  the two profiles are of different devices: /device:TPU:24 before, /device:TPU:30 now
where the time goes in v2:
time: 73.1 us; the launch traced here: 72.6 us
  starting transfers between devices  32.3 us (44%)
  waiting for transfers between devices  26.5 us (36%)
  Pallas kernels  9.07 us (12%)
  local copies, waits for them, and re-layouts  2.87 us (4%)
  other arithmetic  0.95 us (1%)
  between operations  0.84 us (1%)
    all_to_all x1, waiting for transfers between devices, on_device(): back_got = lax.all_to_all(back_sent, group, 0, 0, tiled=True)  16 us
    all_to_all x1, starting transfers between devices, on_device(): got = lax.all_to_all(sent, group, 0, 0, tiled=True)  12.1 us
    ppermute x1, waiting for transfers between devices, on_device(): lax.ppermute(lax.dynamic_slice_in_dim(densities, jnp.where(side == 0, tai...  6.83 us
    all_to_all x1, starting transfers between devices, on_device(): back_got = lax.all_to_all(back_sent, group, 0, 0, tiled=True)  6.72 us
    ppermute x1, starting transfers between devices, on_device(): p1 = lax.ppermute(densities, hier, near)  4.73 us
    ppermute x1, starting transfers between devices, on_device(): lax.ppermute(lax.dynamic_slice_in_dim(again, jnp.where(side == 0, 0, tail...  4.55 us
    all_to_all x1, waiting for transfers between devices, on_device(): got = lax.all_to_all(sent, group, 0, 0, tiled=True)  3.7 us
    pallas_call x1, Pallas kernels, on_device(): back_sent = column_call(ints, reals, got, vhi, vlo)  3.38 us
  transfers between devices with their start and end apart: 6, of which 3 were waited for; matrix products, arithmetic and copies ran while one was open for 3% of the time, Pallas kernels for 8%

profile of v2, /device:TPU:30, one launch (start us, length us, event | category | flops | bytes accessed | tf_op | source)
XLA Modules:
  0.0 72.6 jit_solution(8305941453796462157)
XLA Ops:
  0.0 4.7 %collective-permute-start = (f32[4,2,16,256]{3,2,1,0:T(8,128)}, f32[4,2,16,256]{3,2,1,0:T(8,128)S(1)}, u32[]{:S(2)}, u32[]{:S(2)}) collective-permute-start(f32[4,2,16,256]{3,2,1,0:T(8,128)} %x_ref.1), channel_id=1, source_target_pairs={{16,32},{48,64},{80,96},{112,128},{144,160},{176,192},{208,224},{2... | collective-permute-start | bytes 393224 | tf_op jit(solution)/shard_map/ppermute | solution.py:408
  4.8 0.8 %select_reduce_fusion = s32[16]{0:T(128)S(1)} fusion(s32[32]{0:T(128)} %param.11, s32[16]{0:T(128)S(1)} %add_clamp_fusion, pred[16]{0:T(512)(128)(4,1)S(1)} %get-tuple-element.23, pred[16]{0:T(512)(128)(4,1)S(1)} %get-tuple-element.28, pred[32]{0:T(512)(128)(4,1)S(1)} %get-tuple-element.25, pred[32]{0:T(512)(128)(4,1)S(1)} %get-tuple-element.26, ...), kind=kLoop, calls=%fused_computation | loop fusion | flops 4592 | bytes 384 | tf_op jit(solution)/shard_map/reduce_sum | solution.py:398
  5.7 0.6 slice.3
  6.9 0.8 %constant_dynamic-slice_fusion = f32[2,2,16,256]{3,2,1,0:T(8,128)S(1)} fusion(f32[4,2,16,256]{3,2,1,0:T(8,128)} %x_ref.1, s32[]{:T(128)S(6)} %select_n.25), kind=kLoop, calls=%fused_computation.14 | loop fusion | bytes 131076 | tf_op jit(solution)/shard_map/dynamic_slice | solution.py:411
  7.8 2.1 %collective-permute-start.1 = (f32[2,2,16,256]{3,2,1,0:T(8,128)S(1)}, f32[2,2,16,256]{3,2,1,0:T(8,128)S(1)}, u32[]{:S(2)}, u32[]{:S(2)}) collective-permute-start(f32[2,2,16,256]{3,2,1,0:T(8,128)S(1)} %constant_dynamic-slice_fusion), channel_id=1, source_target_pairs={{0,32},{32,64},{64,96},{96,128},{128,160},{160,192},{192,224},{224... | collective-permute-start | bytes 196616 | tf_op jit(solution)/shard_map/ppermute | solution.py:411
  9.9 0.8 %own.1._ = f32[32,16,128]{2,1,0:T(8,128)} custom-call(f32[128,256]{1,0:T(8,128)S(1)} %bitcast.3), custom_call_target="tpu_custom_call" | custom-call | flops 1000000 | bytes 4000000 | tf_op jit(solution)/shard_map/own/pallas_call | solution.py:412
  10.7 0.0 copy-start.1
  10.7 6.8 %collective-permute-done.1.far_ref.p2_ref = f32[2,2,16,256]{3,2,1,0:T(8,128)S(1)} collective-permute-done((f32[2,2,16,256]{3,2,1,0:T(8,128)S(1)}, f32[2,2,16,256]{3,2,1,0:T(8,128)S(1)}, u32[]{:S(2)}, u32[]{:S(2)}) %collective-permute-start.1) | collective-permute-done | bytes 65568 | tf_op jit(solution)/shard_map/ppermute | solution.py:411
  17.5 1.3 %halo.1 = f32[32,16,128]{2,1,0:T(8,128)} custom-call(s32[16]{0:T(128)S(1)} %fusion.2.ints_ref, f32[4,2,16,256]{3,2,1,0:T(8,128)S(1)} %collective-permute-done.near_ref.p1_ref, f32[2,2,16,256]{3,2,1,0:T(8,128)S(1)} %collective-permute-done.1.far_ref.p2_ref, f32[32,16,128]{2,1,0:T(8,128)} %own.1._), custom_call_target="tpu_custom_call", output_to_operand_aliasing={{}: (3, {})} | custom-call | flops 1000000 | bytes 4000000 | tf_op jit(solution)/shard_map/halo/pallas_call | solution.py:414
  18.9 12.1 %all-to-all-start = ((f32[32,16,128]{2,1,0:T(8,128)}), f32[32,16,128]{2,1,0:T(8,128)S(1)}, u32[]{:S(2)}, u32[]{:S(2)}) async-start(f32[32,16,128]{2,1,0:T(8,128)} %halo.1), calls=%async_computation | async-start | bytes 524288 | tf_op jit(solution)/shard_map/all_to_all | solution.py:416
  31.0 0.7 copy-done.4
  31.6 0.1 reshape.51
  31.7 0.1 weights.1
  31.9 0.0 copy-start.3
  31.9 0.6 copy-done.3
  32.5 0.1 pad_maximum_fusion.reals_ref
  32.6 2.1 %collective-permute-start.2 = (f32[4,2,16,256]{3,2,1,0:T(8,128)S(1)}, f32[4,2,16,256]{3,2,1,0:T(8,128)S(1)}, u32[]{:S(2)}, u32[]{:S(2)}) collective-permute-start(f32[4,2,16,256]{3,2,1,0:T(8,128)S(1)} %copy-done), channel_id=1, source_target_pairs={{0,16},{32,48},{64,80},{96,112},{128,144},{160,176},{192,208},{224... | collective-permute-start | bytes 393224 | tf_op jit(solution)/shard_map/ppermute | solution.py:417
  34.8 4.6 %collective-permute-start.3 = (f32[2,2,16,256]{3,2,1,0:T(8,128)S(1)}, f32[2,2,16,256]{3,2,1,0:T(8,128)S(1)}, u32[]{:S(2)}, u32[]{:S(2)}) collective-permute-start(f32[2,2,16,256]{3,2,1,0:T(8,128)S(1)} %constant_dynamic-slice_fusion.1), channel_id=1, source_target_pairs={{32,0},{64,32},{96,64},{128,96},{160,128},{192,160},{224,192},{256... | collective-permute-start | bytes 196616 | tf_op jit(solution)/shard_map/ppermute | solution.py:418
  39.3 3.7 %all-to-all-done.got_ref = f32[32,16,128]{2,1,0:T(8,128)S(1)} async-done(((f32[32,16,128]{2,1,0:T(8,128)}), f32[32,16,128]{2,1,0:T(8,128)S(1)}, u32[]{:S(2)}, u32[]{:S(2)}) %all-to-all-start) | async-done | bytes 262176 | tf_op jit(solution)/shard_map/all_to_all | solution.py:416
  43.0 3.4 %columns.1 = f32[32,32,128]{2,1,0:T(8,128)} custom-call(s32[16]{0:T(128)S(1)} %fusion.2.ints_ref, f32[78]{0:T(128)S(1)} %pad_maximum_fusion.reals_ref, f32[32,16,128]{2,1,0:T(8,128)S(1)} %all-to-all-done.got_ref, bf16[768,256]{1,0:T(8,128)(2,1)S(1)} %get-tuple-element.15.ghi_ref, bf16[768,256]{1,0:T(8,128)(2,1)S(1)} %get-tuple-element.16.glo_ref), custom_call_target="tpu_custom_call" | custom-call | flops 1000000000 | bytes 4000000 | tf_op jit(solution)/shard_map/columns/pallas_call | solution.py:419
  46.4 6.7 %all-to-all-start.1 = ((f32[32,32,128]{2,1,0:T(8,128)}), f32[32,32,128]{2,1,0:T(8,128)S(1)}, u32[]{:S(2)}, u32[]{:S(2)}) async-start(f32[32,32,128]{2,1,0:T(8,128)} %columns.1), calls=%async_computation.1 | async-start | bytes 1048576 | tf_op jit(solution)/shard_map/all_to_all | solution.py:421
  53.1 1.7 %rows.1.base_ref = f32[128,256]{1,0:T(8,128)S(1)} custom-call(s32[16]{0:T(128)S(1)} %fusion.2.ints_ref, f32[78]{0:T(128)S(1)} %pad_maximum_fusion.reals_ref, f32[4,2,16,256]{3,2,1,0:T(8,128)S(1)} %copy-done, f32[4,2,16,256]{3,2,1,0:T(8,128)S(1)} %collective-permute-done.near_ref.p1_ref, f32[2,2,16,256]{3,2,1,0:T(8,128)S(1)} %collective-permute-done.1.far_ref.p2_ref, ...), custom_call_target="tpu_custom_call" | custom-call | flops 1000000000 | bytes 4000000 | tf_op jit(solution)/shard_map/rows/pallas_call | solution.py:422
  54.8 16.0 %all-to-all-done.1.got_ref = f32[32,32,128]{2,1,0:T(8,128)S(1)} async-done(((f32[32,32,128]{2,1,0:T(8,128)}), f32[32,32,128]{2,1,0:T(8,128)S(1)}, u32[]{:S(2)}, u32[]{:S(2)}) %all-to-all-start.1) | async-done | bytes 524320 | tf_op jit(solution)/shard_map/all_to_all | solution.py:421
  70.9 1.7 %finish.1 = f32[128,256]{1,0:T(8,128)} custom-call(s32[16]{0:T(128)S(1)} %fusion.2.ints_ref, f32[32,32,128]{2,1,0:T(8,128)S(1)} %all-to-all-done.1.got_ref, f32[128,256]{1,0:T(8,128)S(1)} %rows.1.base_ref, bf16[256,768]{1,0:T(8,128)(2,1)S(1)} %get-tuple-element.21.ghi_ref, bf16[256,768]{1,0:T(8,128)(2,1)S(1)} %get-tuple-element.22.glo_ref), custom_call_target="tpu_custom_call" | custom-call | flops 300000000 | bytes 4000000 | tf_op jit(solution)/shard_map/finish/pallas_call | solution.py:423
  (16 shorter events, 0.1 us)
Async XLA Ops:
  0.0 9.9 %copy-start = (f32[4,2,16,256]{3,2,1,0:T(8,128)S(1)}, f32[4,2,16,256]{3,2,1,0:T(8,128)}, u32[]{:S(2)}) copy-start(f32[4,2,16,256]{3,2,1,0:T(8,128)} %x_ref.1) | copy-start | bytes 393220
  0.0 17.5 %collective-permute-start = (f32[4,2,16,256]{3,2,1,0:T(8,128)}, f32[4,2,16,256]{3,2,1,0:T(8,128)S(1)}, u32[]{:S(2)}, u32[]{:S(2)}) collective-permute-start(f32[4,2,16,256]{3,2,1,0:T(8,128)} %x_ref.1), channel_id=1, source_target_pairs={{16,32},{48,64},{80,96},{112,128},{144,160},{176,192},{208,224},{2... | collective-permute-start | bytes 393224 | tf_op jit(solution)/shard_map/ppermute | solution.py:408
  7.8 9.8 %collective-permute-start.1 = (f32[2,2,16,256]{3,2,1,0:T(8,128)S(1)}, f32[2,2,16,256]{3,2,1,0:T(8,128)S(1)}, u32[]{:S(2)}, u32[]{:S(2)}) collective-permute-start(f32[2,2,16,256]{3,2,1,0:T(8,128)S(1)} %constant_dynamic-slice_fusion), channel_id=1, source_target_pairs={{0,32},{32,64},{64,96},{96,128},{128,160},{160,192},{192,224},{224... | collective-permute-start | bytes 196616 | tf_op jit(solution)/shard_map/ppermute | solution.py:411
  10.7 21.0 %copy-start.1 = (f32[2,256,256]{2,1,0:T(8,128)S(1)}, f32[2,256,256]{2,1,0:T(8,128)}, u32[]{:S(2)}) copy-start(f32[2,256,256]{2,1,0:T(8,128)} %q_ref.1) | copy-start | bytes 1572868
  18.8 12.9 %copy-start.2 = (f32[256,256]{1,0:T(8,128)S(1)}, f32[256,256]{1,0:T(8,128)}, u32[]{:S(2)}) copy-start(f32[256,256]{1,0:T(8,128)} %h_ref.1) | copy-start | bytes 786436
  18.9 24.2 %all-to-all-start = ((f32[32,16,128]{2,1,0:T(8,128)}), f32[32,16,128]{2,1,0:T(8,128)S(1)}, u32[]{:S(2)}, u32[]{:S(2)}) async-start(f32[32,16,128]{2,1,0:T(8,128)} %halo.1), calls=%async_computation | async-start | bytes 524288 | tf_op jit(solution)/shard_map/all_to_all | solution.py:416
  30.9 0.7 copy-start.4
  31.9 0.7 copy-start.3
  32.6 13.8 %collective-permute-start.2 = (f32[4,2,16,256]{3,2,1,0:T(8,128)S(1)}, f32[4,2,16,256]{3,2,1,0:T(8,128)S(1)}, u32[]{:S(2)}, u32[]{:S(2)}) collective-permute-start(f32[4,2,16,256]{3,2,1,0:T(8,128)S(1)} %copy-done), channel_id=1, source_target_pairs={{0,16},{32,48},{64,80},{96,112},{128,144},{160,176},{192,208},{224... | collective-permute-start | bytes 393224 | tf_op jit(solution)/shard_map/ppermute | solution.py:417
  34.8 11.7 %collective-permute-start.3 = (f32[2,2,16,256]{3,2,1,0:T(8,128)S(1)}, f32[2,2,16,256]{3,2,1,0:T(8,128)S(1)}, u32[]{:S(2)}, u32[]{:S(2)}) collective-permute-start(f32[2,2,16,256]{3,2,1,0:T(8,128)S(1)} %constant_dynamic-slice_fusion.1), channel_id=1, source_target_pairs={{32,0},{64,32},{96,64},{128,96},{160,128},{192,160},{224,192},{256... | collective-permute-start | bytes 196616 | tf_op jit(solution)/shard_map/ppermute | solution.py:418
  46.4 24.4 %all-to-all-start.1 = ((f32[32,32,128]{2,1,0:T(8,128)}), f32[32,32,128]{2,1,0:T(8,128)S(1)}, u32[]{:S(2)}, u32[]{:S(2)}) async-start(f32[32,32,128]{2,1,0:T(8,128)} %columns.1), calls=%async_computation.1 | async-start | bytes 1048576 | tf_op jit(solution)/shard_map/all_to_all | solution.py:421

commit v3 on v2

--- a/solution.py
+++ b/solution.py
@@ -149,12 +149,13 @@
 def halo_kernel(ints_ref, near_ref, far_ref, _, o_ref, s_ref, t_ref, sem):
     side = ints_ref[SIDE]
     count = jnp.where(side == 0, ints_ref[COUNTS + 1], ints_ref[COUNTS + 3])
+    farther = ints_ref[COUNTS]
     for i in range(4):
         at = i + jnp.where(side == 0, count - 4, 0)
         inside = jnp.where(side == 0, at >= 0, i < count)
-        other = jnp.where(side == 0, at + 2, i - count)
+        other = jnp.where(side == 0, at + farther, i - count)
         near = near_ref[jnp.clip(at, 0, 3)]
-        far = far_ref[jnp.clip(other, 0, 1)]
+        far = far_ref[jnp.clip(other, 0, 3)]
         s_ref[32 * i : 32 * i + 32, :] = jnp.where(inside, near, far).reshape(32, 256)
     t_ref[...] = s_ref[...].T.reshape(32, 8, 128)
     copy = pltpu.make_async_copy(t_ref, o_ref.at[:, 8:16], sem)
@@ -235,18 +236,18 @@
     nodes = Nodes(ints_ref, reals_ref, ints_ref[HERE_BEGIN])
     re, im = nodes.re, (-nodes.im[0], -nodes.im[1])
     up = ints_ref[SIDE]
-    below, own, above = ints_ref[COUNTS + 1], ints_ref[COUNTS + 2], ints_ref[COUNTS + 3]
+    farther, below, own, above = (ints_ref[COUNTS + i] for i in range(4))
     w_ref[8:12] = x_ref[...]
     w_ref[pl.ds(4 + 8 * up, 4)] = p1_ref[...]
-    w_ref[pl.ds(2 + 14 * up, 2)] = p2_ref[...]
+    w_ref[pl.ds(16 * up, 4)] = p2_ref[...]
     w_ref[pl.ds(12 - 8 * up, 4)] = p3_ref[...]
-    w_ref[pl.ds(16 - 14 * up, 2)] = p4_ref[...]
+    w_ref[pl.ds(16 - 16 * up, 4)] = p4_ref[...]
 
     def slot(p):
         j = p - 4
         if j < 0:
-            return 4 + j + below
-        return jnp.where(j < own, 8 + j, jnp.where(j < own + above, 12 + j - own, jnp.minimum(16 + j - own - above, 17)))
+            return jnp.where(j + below >= 0, 4 + j + below, farther + j + below)
+        return jnp.where(j < own, 8 + j, jnp.where(j < own + above, 12 + j - own, jnp.minimum(16 + j - own - above, 19)))
 
     x = []
     for p in range(12):
@@ -360,7 +361,7 @@
     struct((128, 256)),
     [SMEM] * 2 + [VMEM] * 7,
     [
-        pltpu.VMEM((18, 2, 16, 256), F32),
+        pltpu.VMEM((20, 2, 16, 256), F32),
         pltpu.VMEM((384, 768), BF),
         pltpu.VMEM((384, 768), BF),
         pltpu.VMEM((128, 768), BF),
@@ -406,19 +407,17 @@
     reals = jnp.concatenate([gamma, coeff.reshape(4), jnp.sqrt(jnp.arange(ROOTS, dtype=F32))])
     near, far, inner, back = swap_routes(node_count.shape[0])
     p1 = lax.ppermute(densities, hier, near)
-    tail = ints[COUNTS + 2] - 2
-    side = lax.axis_index("r")
-    p2 = lax.ppermute(lax.dynamic_slice_in_dim(densities, jnp.where(side == 0, tail, 0), 2, 0), hier, far)
+    p2 = lax.ppermute(densities, hier, far)
     part = own_call(densities.reshape(128, 256))
     vhi, vlo, hhi, hlo = weights_call(hamiltonian, couplings)
     sent = halo_call(ints, p1, p2, part)
     sent, again = lax.optimization_barrier((sent, densities))
     got = lax.all_to_all(sent, group, 0, 0, tiled=True)
     p3 = lax.ppermute(again, hier, inner)
-    p4 = lax.ppermute(lax.dynamic_slice_in_dim(again, jnp.where(side == 0, 0, tail), 2, 0), hier, back)
     back_sent = column_call(ints, reals, got, vhi, vlo)
-    back_sent, p3, p4 = lax.optimization_barrier((back_sent, p3, p4))
+    back_sent, p3, again = lax.optimization_barrier((back_sent, p3, densities))
     back_got = lax.all_to_all(back_sent, group, 0, 0, tiled=True)
+    p4 = lax.ppermute(again, hier, back)
     base = row_call(ints, reals, densities, p1, p2, p3, p4, vhi, vlo)
     out = finish_call(ints, back_got, base, hhi, hlo)
     return out.reshape(4, 2, 16, 256)

time: 73.1 us -> 68.3 us (0.934)
  the two profiles are of different devices: /device:TPU:30 before, /device:TPU:28 now
where the time goes in v3:
time: 68.3 us; the launch traced here: 67.6 us
  starting transfers between devices  33.5 us (49%)
  waiting for transfers between devices  22.8 us (33%)
  Pallas kernels  9.12 us (13%)
  local copies, waits for them, and re-layouts  1.67 us (2%)
    all_to_all x1, starting transfers between devices, on_device(): got = lax.all_to_all(sent, group, 0, 0, tiled=True)  14.8 us
    ppermute x1, waiting for transfers between devices, on_device(): p4 = lax.ppermute(again, hier, back)  10.5 us
    all_to_all x1, waiting for transfers between devices, on_device(): got = lax.all_to_all(sent, group, 0, 0, tiled=True)  8.35 us
    ppermute x1, starting transfers between devices, on_device(): p2 = lax.ppermute(densities, hier, far)  6.75 us
    all_to_all x1, starting transfers between devices, on_device(): back_got = lax.all_to_all(back_sent, group, 0, 0, tiled=True)  3.89 us
    all_to_all x1, waiting for transfers between devices, on_device(): back_got = lax.all_to_all(back_sent, group, 0, 0, tiled=True)  3.8 us
    ppermute x1, starting transfers between devices, on_device(): p3 = lax.ppermute(again, hier, inner)  3.7 us
    pallas_call x1, Pallas kernels, on_device(): back_sent = column_call(ints, reals, got, vhi, vlo)  3.41 us
  transfers between devices with their start and end apart: 6, of which 4 were waited for; matrix products, arithmetic and copies ran while one was open for 1% of the time, Pallas kernels for 9%

profile of v3, /device:TPU:28, one launch (start us, length us, event | category | flops | bytes accessed | tf_op | source)
XLA Modules:
  0.0 67.6 jit_solution(8381854061276137302)
XLA Ops:
  0.0 2.4 %collective-permute-start = (f32[4,2,16,256]{3,2,1,0:T(8,128)}, f32[4,2,16,256]{3,2,1,0:T(8,128)S(1)}, u32[]{:S(2)}, u32[]{:S(2)}) collective-permute-start(f32[4,2,16,256]{3,2,1,0:T(8,128)} %x_ref.1), channel_id=1, source_target_pairs={{16,32},{48,64},{80,96},{112,128},{144,160},{176,192},{208,224},{2... | collective-permute-start | bytes 393224 | tf_op jit(solution)/shard_map/ppermute | solution.py:409
  2.4 6.8 %collective-permute-start.1 = (f32[4,2,16,256]{3,2,1,0:T(8,128)}, f32[4,2,16,256]{3,2,1,0:T(8,128)S(1)}, u32[]{:S(2)}, u32[]{:S(2)}) collective-permute-start(f32[4,2,16,256]{3,2,1,0:T(8,128)} %x_ref.1), channel_id=1, source_target_pairs={{0,32},{32,64},{64,96},{96,128},{128,160},{160,192},{192,224},{224... | collective-permute-start | bytes 393224 | tf_op jit(solution)/shard_map/ppermute | solution.py:410
  9.3 0.9 %copy-done.2 = f32[4,2,16,256]{3,2,1,0:T(8,128)S(1)} copy-done((f32[4,2,16,256]{3,2,1,0:T(8,128)S(1)}, f32[4,2,16,256]{3,2,1,0:T(8,128)}, u32[]{:S(2)}) %copy-start.2) | copy-done | bytes 131096
  10.2 0.8 %own.1._ = f32[32,16,128]{2,1,0:T(8,128)} custom-call(f32[128,256]{1,0:T(8,128)S(1)} %bitcast.2), custom_call_target="tpu_custom_call" | custom-call | flops 1000000 | bytes 4000000 | tf_op jit(solution)/shard_map/own/pallas_call | solution.py:411
  11.0 0.0 copy-start.4
  11.0 0.6 copy-done.4
  11.6 0.2 select_reduce_fusion
  11.8 0.2 collective-permute-done.1.far_ref.p2_ref
  12.0 1.3 %halo.1 = f32[32,16,128]{2,1,0:T(8,128)} custom-call(s32[16]{0:T(128)S(1)} %fusion.2.ints_ref, f32[4,2,16,256]{3,2,1,0:T(8,128)S(1)} %collective-permute-done.near_ref.p1_ref, f32[4,2,16,256]{3,2,1,0:T(8,128)S(1)} %collective-permute-done.1.far_ref.p2_ref, f32[32,16,128]{2,1,0:T(8,128)} %own.1._), custom_call_target="tpu_custom_call", output_to_operand_aliasing={{}: (3, {})} | custom-call | flops 1000000 | bytes 4000000 | tf_op jit(solution)/shard_map/halo/pallas_call | solution.py:413
  13.3 0.0 copy-start.6
  13.4 0.0 copy-start.1
  13.4 14.8 %all-to-all-start = ((f32[32,16,128]{2,1,0:T(8,128)}), f32[32,16,128]{2,1,0:T(8,128)S(1)}, u32[]{:S(2)}, u32[]{:S(2)}) async-start(f32[32,16,128]{2,1,0:T(8,128)} %halo.1), calls=%async_computation | async-start | bytes 524288 | tf_op jit(solution)/shard_map/all_to_all | solution.py:415
  28.2 0.1 reshape.49
  28.3 3.7 %collective-permute-start.2 = (f32[4,2,16,256]{3,2,1,0:T(8,128)S(1)}, f32[4,2,16,256]{3,2,1,0:T(8,128)S(1)}, u32[]{:S(2)}, u32[]{:S(2)}) collective-permute-start(f32[4,2,16,256]{3,2,1,0:T(8,128)S(1)} %copy-done.3), channel_id=1, source_target_pairs={{0,16},{32,48},{64,80},{96,112},{128,144},{160,176},{192,208},{224... | collective-permute-start | bytes 393224 | tf_op jit(solution)/shard_map/ppermute | solution.py:416
  32.0 0.1 pad_maximum_fusion.reals_ref
  32.1 0.1 weights.1
  32.2 8.4 %all-to-all-done.got_ref = f32[32,16,128]{2,1,0:T(8,128)S(1)} async-done(((f32[32,16,128]{2,1,0:T(8,128)}), f32[32,16,128]{2,1,0:T(8,128)S(1)}, u32[]{:S(2)}, u32[]{:S(2)}) %all-to-all-start) | async-done | bytes 262176 | tf_op jit(solution)/shard_map/all_to_all | solution.py:415
  40.6 3.4 %columns.1 = f32[32,32,128]{2,1,0:T(8,128)} custom-call(s32[16]{0:T(128)S(1)} %fusion.2.ints_ref, f32[78]{0:T(128)S(1)} %pad_maximum_fusion.reals_ref, f32[32,16,128]{2,1,0:T(8,128)S(1)} %all-to-all-done.got_ref, bf16[768,256]{1,0:T(8,128)(2,1)S(1)} %get-tuple-element.15.ghi_ref, bf16[768,256]{1,0:T(8,128)(2,1)S(1)} %get-tuple-element.16.glo_ref), custom_call_target="tpu_custom_call" | custom-call | flops 1000000000 | bytes 4000000 | tf_op jit(solution)/shard_map/columns/pallas_call | solution.py:417
  44.0 3.9 %all-to-all-start.1 = ((f32[32,32,128]{2,1,0:T(8,128)}), f32[32,32,128]{2,1,0:T(8,128)S(1)}, u32[]{:S(2)}, u32[]{:S(2)}) async-start(f32[32,32,128]{2,1,0:T(8,128)} %columns.1), calls=%async_computation.1 | async-start | bytes 1048576 | tf_op jit(solution)/shard_map/all_to_all | solution.py:419
  47.9 1.9 %collective-permute-start.3 = (f32[4,2,16,256]{3,2,1,0:T(8,128)S(1)}, f32[4,2,16,256]{3,2,1,0:T(8,128)S(1)}, u32[]{:S(2)}, u32[]{:S(2)}) collective-permute-start(f32[4,2,16,256]{3,2,1,0:T(8,128)S(1)} %copy-done.3), channel_id=1, source_target_pairs={{32,0},{64,32},{96,64},{128,96},{160,128},{192,160},{224,192},{256... | collective-permute-start | bytes 393224 | tf_op jit(solution)/shard_map/ppermute | solution.py:420
  49.8 10.5 %collective-permute-done.3.p4_ref = f32[4,2,16,256]{3,2,1,0:T(8,128)S(1)} collective-permute-done((f32[4,2,16,256]{3,2,1,0:T(8,128)S(1)}, f32[4,2,16,256]{3,2,1,0:T(8,128)S(1)}, u32[]{:S(2)}, u32[]{:S(2)}) %collective-permute-start.3) | collective-permute-done | bytes 131104 | tf_op jit(solution)/shard_map/ppermute | solution.py:420
  60.3 1.7 %rows.1.base_ref = f32[128,256]{1,0:T(8,128)S(1)} custom-call(s32[16]{0:T(128)S(1)} %fusion.2.ints_ref, f32[78]{0:T(128)S(1)} %pad_maximum_fusion.reals_ref, f32[4,2,16,256]{3,2,1,0:T(8,128)S(1)} %copy-done.3, f32[4,2,16,256]{3,2,1,0:T(8,128)S(1)} %collective-permute-done.near_ref.p1_ref, f32[4,2,16,256]{3,2,1,0:T(8,128)S(1)} %collective-permute-done.1.far_ref.p2_ref, ...), custom_call_target="tpu_custom_call" | custom-call | flops 1000000000 | bytes 4000000 | tf_op jit(solution)/shard_map/rows/pallas_call | solution.py:421
  62.0 3.8 %all-to-all-done.1.got_ref = f32[32,32,128]{2,1,0:T(8,128)S(1)} async-done(((f32[32,32,128]{2,1,0:T(8,128)}), f32[32,32,128]{2,1,0:T(8,128)S(1)}, u32[]{:S(2)}, u32[]{:S(2)}) %all-to-all-start.1) | async-done | bytes 524320 | tf_op jit(solution)/shard_map/all_to_all | solution.py:419
  65.8 1.7 %finish.1 = f32[128,256]{1,0:T(8,128)} custom-call(s32[16]{0:T(128)S(1)} %fusion.2.ints_ref, f32[32,32,128]{2,1,0:T(8,128)S(1)} %all-to-all-done.1.got_ref, f32[128,256]{1,0:T(8,128)S(1)} %rows.1.base_ref, bf16[256,768]{1,0:T(8,128)(2,1)S(1)} %get-tuple-element.21.ghi_ref, bf16[256,768]{1,0:T(8,128)(2,1)S(1)} %get-tuple-element.22.glo_ref), custom_call_target="tpu_custom_call" | custom-call | flops 300000000 | bytes 4000000 | tf_op jit(solution)/shard_map/finish/pallas_call | solution.py:422
  (17 shorter events, 0.1 us)
Async XLA Ops:
  0.0 11.8 %collective-permute-start = (f32[4,2,16,256]{3,2,1,0:T(8,128)}, f32[4,2,16,256]{3,2,1,0:T(8,128)S(1)}, u32[]{:S(2)}, u32[]{:S(2)}) collective-permute-start(f32[4,2,16,256]{3,2,1,0:T(8,128)} %x_ref.1), channel_id=1, source_target_pairs={{16,32},{48,64},{80,96},{112,128},{144,160},{176,192},{208,224},{2... | collective-permute-start | bytes 393224 | tf_op jit(solution)/shard_map/ppermute | solution.py:409
  2.4 9.6 %collective-permute-start.1 = (f32[4,2,16,256]{3,2,1,0:T(8,128)}, f32[4,2,16,256]{3,2,1,0:T(8,128)S(1)}, u32[]{:S(2)}, u32[]{:S(2)}) collective-permute-start(f32[4,2,16,256]{3,2,1,0:T(8,128)} %x_ref.1), channel_id=1, source_target_pairs={{0,32},{32,64},{64,96},{96,128},{128,160},{160,192},{192,224},{224... | collective-permute-start | bytes 393224 | tf_op jit(solution)/shard_map/ppermute | solution.py:410
  9.3 0.9 %copy-start.2 = (f32[4,2,16,256]{3,2,1,0:T(8,128)S(1)}, f32[4,2,16,256]{3,2,1,0:T(8,128)}, u32[]{:S(2)}) copy-start(f32[4,2,16,256]{3,2,1,0:T(8,128)} %x_ref.1) | copy-start | bytes 393220
  11.0 0.7 copy-start.4
  11.8 20.2 %copy-start = (f32[2,256,256]{2,1,0:T(8,128)S(1)}, f32[2,256,256]{2,1,0:T(8,128)}, u32[]{:S(2)}) copy-start(f32[2,256,256]{2,1,0:T(8,128)} %q_ref.1) | copy-start | bytes 1572868
  13.3 14.8 %copy-start.6 = (f32[2,2]{1,0:T(2,128)S(1)}, f32[2,2]{1,0:T(2,128)}, u32[]{:S(2)}) copy-start(f32[2,2]{1,0:T(2,128)} %param.10) | copy-start | bytes 52
  13.3 14.9 %copy-start.3 = (f32[4,2,16,256]{3,2,1,0:T(8,128)S(1)}, f32[4,2,16,256]{3,2,1,0:T(8,128)}, u32[]{:S(2)}) copy-start(f32[4,2,16,256]{3,2,1,0:T(8,128)} %x_ref.1) | copy-start | bytes 393220
  13.4 18.7 %copy-start.1 = (f32[256,256]{1,0:T(8,128)S(1)}, f32[256,256]{1,0:T(8,128)}, u32[]{:S(2)}) copy-start(f32[256,256]{1,0:T(8,128)} %h_ref.1) | copy-start | bytes 786436
  13.4 27.2 %all-to-all-start = ((f32[32,16,128]{2,1,0:T(8,128)}), f32[32,16,128]{2,1,0:T(8,128)S(1)}, u32[]{:S(2)}, u32[]{:S(2)}) async-start(f32[32,16,128]{2,1,0:T(8,128)} %halo.1), calls=%async_computation | async-start | bytes 524288 | tf_op jit(solution)/shard_map/all_to_all | solution.py:415
  28.2 3.7 %copy-start.5 = (f32[2]{0:T(128)S(1)}, f32[2]{0:T(128)}, u32[]{:S(2)}) copy-start(f32[2]{0:T(128)} %param.9) | copy-start | bytes 28
  28.3 15.7 %collective-permute-start.2 = (f32[4,2,16,256]{3,2,1,0:T(8,128)S(1)}, f32[4,2,16,256]{3,2,1,0:T(8,128)S(1)}, u32[]{:S(2)}, u32[]{:S(2)}) collective-permute-start(f32[4,2,16,256]{3,2,1,0:T(8,128)S(1)} %copy-done.3), channel_id=1, source_target_pairs={{0,16},{32,48},{64,80},{96,112},{128,144},{160,176},{192,208},{224... | collective-permute-start | bytes 393224 | tf_op jit(solution)/shard_map/ppermute | solution.py:416
  44.0 21.9 %all-to-all-start.1 = ((f32[32,32,128]{2,1,0:T(8,128)}), f32[32,32,128]{2,1,0:T(8,128)S(1)}, u32[]{:S(2)}, u32[]{:S(2)}) async-start(f32[32,32,128]{2,1,0:T(8,128)} %columns.1), calls=%async_computation.1 | async-start | bytes 1048576 | tf_op jit(solution)/shard_map/all_to_all | solution.py:419
  47.9 12.4 %collective-permute-start.3 = (f32[4,2,16,256]{3,2,1,0:T(8,128)S(1)}, f32[4,2,16,256]{3,2,1,0:T(8,128)S(1)}, u32[]{:S(2)}, u32[]{:S(2)}) collective-permute-start(f32[4,2,16,256]{3,2,1,0:T(8,128)S(1)} %copy-done.3), channel_id=1, source_target_pairs={{32,0},{64,32},{96,64},{128,96},{160,128},{192,160},{224,192},{256... | collective-permute-start | bytes 393224 | tf_op jit(solution)/shard_map/ppermute | solution.py:420

commit v4 on v3

--- a/solution.py
+++ b/solution.py
@@ -25,20 +25,27 @@
 
 def granules(vs):
     lane = lax.broadcasted_iota(jnp.int32, vs[0].shape, 1) // 16
-    for bit in (4, 2, 1):
-        low = (lane & bit) == 0
-        out = list(vs)
-        for a in range(8):
-            if not a & bit:
-                b = a | bit
-                out[a] = jnp.where(low, vs[a], pltpu.roll(vs[b], 16 * bit, 1))
-                out[b] = jnp.where(low, pltpu.roll(vs[a], 128 - 16 * bit, 1), vs[b])
-        vs = out
-    return vs
+    turned = [vs[0]] + [pltpu.roll(vs[k], 16 * k, 1) for k in range(1, 8)]
+    cur = [turned[-k % 8] for k in range(8)]
+    for bit in (1, 2, 4):
+        pick = (lane & bit) != 0
+        cur = [jnp.where(pick, cur[(m - bit) % 8], cur[m]) for m in range(8)]
+    return [cur[0]] + [pltpu.roll(cur[m], 128 - 16 * m, 1) for m in range(1, 8)]
+
+
+def once(method):
+    def cached(self, p):
+        key = (method.__name__, p)
+        if key not in self.memo:
+            self.memo[key] = method(self, p)
+        return self.memo[key]
+
+    return cached
 
 
 class Nodes:
     def __init__(self, ints_ref, reals_ref, begin):
+        self.memo = {}
         self.live = (ints_ref[TOTAL] >> 1) << 1
         self.begin = begin
         self.base = begin - 4
@@ -50,14 +57,17 @@
     def root(self, n):
         return self.reals[jnp.clip(n, 0, ROOTS - 1) + 6]
 
+    @once
     def up(self, p):
         g = self.base + p
         return jnp.where((g >= 0) & (g + 2 < self.live), self.root((g >> 1) + 1), 0.0)
 
+    @once
     def down(self, p):
         g = self.base + p
         return jnp.where((g >= 2) & (g < self.live), self.root(g >> 1), 0.0)
 
+    @once
     def middle(self, p):
         g = self.base + p
         n = (g >> 1).astype(F32)
@@ -65,14 +75,17 @@
         upper = jnp.where(ok & (g + 2 < self.live), n + 1.0, 0.0)
         return upper + jnp.where(ok & (g >= 2), n, 0.0)
 
+    @once
     def even(self, p):
         g = self.base + p
         return jnp.where((g >= 0) & (g < self.live) & ((g & 1) == 0), 1.0, 0.0).astype(F32)
 
+    @once
     def odd(self, p):
         g = self.base + p
         return jnp.where((g >= 0) & (g < self.live) & ((g & 1) == 1), 1.0, 0.0).astype(F32)
 
+    @once
     def damp(self, p):
         g = self.base + p
         n0 = (g >> 1).astype(F32)
@@ -146,27 +159,35 @@
     copy.wait()
 
 
-def halo_kernel(ints_ref, near_ref, far_ref, _, o_ref, s_ref, t_ref, sem):
-    side = ints_ref[SIDE]
-    count = jnp.where(side == 0, ints_ref[COUNTS + 1], ints_ref[COUNTS + 3])
-    farther = ints_ref[COUNTS]
-    for i in range(4):
-        at = i + jnp.where(side == 0, count - 4, 0)
-        inside = jnp.where(side == 0, at >= 0, i < count)
-        other = jnp.where(side == 0, at + farther, i - count)
-        near = near_ref[jnp.clip(at, 0, 3)]
-        far = far_ref[jnp.clip(other, 0, 3)]
-        s_ref[32 * i : 32 * i + 32, :] = jnp.where(inside, near, far).reshape(32, 256)
-    t_ref[...] = s_ref[...].T.reshape(32, 8, 128)
-    copy = pltpu.make_async_copy(t_ref, o_ref.at[:, 8:16], sem)
+def fetch(pairs, sem):
+    copies = [pltpu.make_async_copy(source, target, sem.at[i]) for i, (source, target) in enumerate(pairs)]
+    for copy in copies:
+        copy.start()
+    return copies
+
+
+def halo_kernel(ints_in, far_ref, near_ref, _, o_ref, t_ref, ints_ref, sem, out_sem):
+    fetched = fetch([(ints_in, ints_ref)], sem)
+    near = near_ref[...].reshape(128, 256).T
+    far = far_ref[...].reshape(128, 256).T
+    lane = lax.broadcasted_iota(jnp.int32, near.shape, 1)
+    for copy in fetched:
+        copy.wait()
+    lower = ints_ref[SIDE] == 0
+    count = jnp.where(lower, ints_ref[COUNTS + 1], ints_ref[COUNTS + 3])
+    near = pltpu.roll(near, jnp.where(lower, 4 - count, 0) * 32, 1)
+    far = pltpu.roll(far, ((jnp.where(lower, 8 - count - ints_ref[COUNTS], count)) & 3) * 32, 1)
+    inside = (lane >= jnp.where(lower, 4 - count, 0) * 32) & (lane < jnp.where(lower, 4, count) * 32)
+    t_ref[...] = jnp.where(inside, near, far).reshape(32, 8, 128)
+    copy = pltpu.make_async_copy(t_ref, o_ref.at[:, 8:16], out_sem)
     copy.start()
     copy.wait()
 
 
-def column_kernel(ints_ref, reals_ref, got_ref, ghi_ref, glo_ref, o_ref, y_ref, hi_ref, lo_ref, hi2_ref, lo2_ref, z_ref):
-    nodes = Nodes(ints_ref, reals_ref, ints_ref[TEAM_BEGIN])
-    own, other = ints_ref[COUNTS + 2 - ints_ref[SIDE]], ints_ref[COUNTS + 3 - ints_ref[SIDE]]
-    re, im = nodes.re, nodes.im
+def column_kernel(
+    ints_in, reals_in, got_ref, ghi_ref, glo_ref, o_ref, y_ref, hi_ref, lo_ref, hi2_ref, lo2_ref, z_ref, send_ref, ints_ref, reals_ref, sem, out_sem
+):
+    fetched = fetch([(ints_in, ints_ref), (reals_in, reals_ref)], sem)
     places = ((1, 0), (0, 0), (0, 1), (1, 1))
     for i, (g, r) in enumerate(places):
         vs = []
@@ -174,6 +195,11 @@
             vs.append(jnp.concatenate([got_ref[(8 * high + low) * 2 + r, 8 * g : 8 * g + 8, :] for high in range(2)], axis=0))
         for m, v in enumerate(granules(vs)):
             y_ref[SLOTS * i + m // 2, m % 2] = jnp.concatenate([v[:8], v[8:]], axis=1)
+    for copy in fetched:
+        copy.wait()
+    nodes = Nodes(ints_ref, reals_ref, ints_ref[TEAM_BEGIN])
+    own, other = ints_ref[COUNTS + 2 - ints_ref[SIDE]], ints_ref[COUNTS + 3 - ints_ref[SIDE]]
+    re, im = nodes.re, nodes.im
 
     def slot(p):
         j = p - 4
@@ -218,8 +244,8 @@
         z_ref[1, j] = (2.0 * HALF2) * sums[16 * j : 16 * j + 16].reshape(2, 8, 256)
         z_ref[2, j] = HALF2 * sums[384 + 16 * j : 400 + 16 * j].reshape(2, 8, 256)
         z_ref[3, j] = HALF2 * sums[512 + 16 * j : 528 + 16 * j].reshape(2, 8, 256)
-    z_ref[0] = times_weights(hi2_ref, lo2_ref, ghi_ref, glo_ref).reshape(8, 2, 8, 256)
-    for z in range(4):
+
+    def send(z):
         for r in range(2):
             vs = []
             for m in range(8):
@@ -227,7 +253,16 @@
                 vs.append(jnp.concatenate([v[:, :128], v[:, 128:]], axis=0))
             for low, v in enumerate(granules(vs)):
                 for high in range(2):
-                    o_ref[(8 * high + low) * 2 + r, 8 * z : 8 * z + 8, :] = v[8 * high : 8 * high + 8]
+                    send_ref[z, (8 * high + low) * 2 + r] = v[8 * high : 8 * high + 8]
+        copy = pltpu.make_async_copy(send_ref.at[z], o_ref.at[:, 8 * z : 8 * z + 8], out_sem.at[z])
+        copy.start()
+        return copy
+
+    last = times_weights(hi2_ref, lo2_ref, ghi_ref, glo_ref)
+    copies = [send(z) for z in range(1, 4)]
+    z_ref[0] = last.reshape(8, 2, 8, 256)
+    for copy in [*copies, send(0)]:
+        copy.wait()
 
 
 def row_kernel(
@@ -283,8 +318,8 @@
         o_ref[32 * j : 32 * j + 32, :] = jnp.where(live, keep * old + right[32 * j : 32 * j + 32], old)
 
 
-def finish_kernel(ints_ref, got_ref, base_ref, ghi_ref, glo_ref, o_ref):
-    own, begin, limit = ints_ref[COUNTS + 2], ints_ref[HERE_BEGIN], (ints_ref[TOTAL] >> 1) << 1
+def finish_kernel(ints_in, got_ref, base_ref, ghi_ref, glo_ref, o_ref, ints_ref, sem):
+    fetched = fetch([(ints_in, ints_ref)], sem)
     his, los = [], []
     for z in range(1, 4):
         hi, lo = split(got_ref[:, 8 * z : 8 * z + 8, :].reshape(256, 128))
@@ -294,6 +329,9 @@
     g = ghi_ref[...]
     out = dot(g, hi) + dot(g, lo) + dot(glo_ref[...], hi) + got_ref[:, :8, :].reshape(256, 128)
     out = out.T
+    for copy in fetched:
+        copy.wait()
+    own, begin, limit = ints_ref[COUNTS + 2], ints_ref[HERE_BEGIN], (ints_ref[TOTAL] >> 1) << 1
     for j in range(4):
         live = (j < own) & (begin + j < limit)
         rows = slice(32 * j, 32 * j + 32)
@@ -332,11 +370,12 @@
 own_call = call(
     own_kernel, struct((32, 16, 128)), [VMEM], [pltpu.VMEM((32, 8, 128), F32), pltpu.SemaphoreType.DMA], out_specs=ANY, name="own"
 )
+INTS = pltpu.SMEM((16,), jnp.int32)
 halo_call = call(
     halo_kernel,
     struct((32, 16, 128)),
-    [SMEM] + [VMEM] * 2 + [ANY],
-    [pltpu.VMEM((128, 256), F32), pltpu.VMEM((32, 8, 128), F32), pltpu.SemaphoreType.DMA],
+    [ANY] + [VMEM] * 2 + [ANY],
+    [pltpu.VMEM((32, 8, 128), F32), INTS, pltpu.SemaphoreType.DMA((1,)), pltpu.SemaphoreType.DMA],
     out_specs=ANY,
     aliases={3: 0},
     name="halo",
@@ -344,7 +383,7 @@
 column_call = call(
     column_kernel,
     struct((32, 32, 128)),
-    [SMEM] * 2 + [VMEM] * 3,
+    [ANY] * 2 + [VMEM] * 3,
     [
         pltpu.VMEM((16, 2, 8, 256), F32),
         pltpu.VMEM((640, 768), BF),
@@ -352,8 +391,14 @@
         pltpu.VMEM((128, 768), BF),
         pltpu.VMEM((128, 768), BF),
         pltpu.VMEM((4, 8, 2, 8, 256), F32),
+        pltpu.VMEM((4, 32, 8, 128), F32),
+        INTS,
+        pltpu.SMEM((6 + ROOTS,), F32),
+        pltpu.SemaphoreType.DMA((2,)),
+        pltpu.SemaphoreType.DMA((4,)),
     ],
     flops=1_000_000_000,
+    out_specs=ANY,
     name="columns",
 )
 row_call = call(
@@ -370,7 +415,9 @@
     flops=1_000_000_000,
     name="rows",
 )
-finish_call = call(finish_kernel, struct((128, 256)), [SMEM] + [VMEM] * 4, flops=300_000_000, name="finish")
+finish_call = call(
+    finish_kernel, struct((128, 256)), [ANY] + [VMEM] * 4, [INTS, pltpu.SemaphoreType.DMA((1,))], flops=300_000_000, name="finish"
+)
 
 
 def swap_routes(shards):
@@ -406,11 +453,11 @@
     ints = integers(node_count)
     reals = jnp.concatenate([gamma, coeff.reshape(4), jnp.sqrt(jnp.arange(ROOTS, dtype=F32))])
     near, far, inner, back = swap_routes(node_count.shape[0])
+    p2 = lax.ppermute(densities, hier, far)
     p1 = lax.ppermute(densities, hier, near)
-    p2 = lax.ppermute(densities, hier, far)
     part = own_call(densities.reshape(128, 256))
     vhi, vlo, hhi, hlo = weights_call(hamiltonian, couplings)
-    sent = halo_call(ints, p1, p2, part)
+    sent = halo_call(ints, p2, p1, part)
     sent, again = lax.optimization_barrier((sent, densities))
     got = lax.all_to_all(sent, group, 0, 0, tiled=True)
     p3 = lax.ppermute(again, hier, inner)

time: 68.3 us -> 66.6 us (0.975)
  the two profiles are of different devices: /device:TPU:28 before, /device:TPU:34 now
where the time goes in v4:
time: 66.6 us; the launch traced here: 66.2 us
  starting transfers between devices  29.2 us (44%)
  waiting for transfers between devices  26.5 us (40%)
  Pallas kernels  8.29 us (12%)
  local copies, waits for them, and re-layouts  1.67 us (3%)
    all_to_all x1, starting transfers between devices, on_device(): got = lax.all_to_all(sent, group, 0, 0, tiled=True)  14.8 us
    ppermute x1, waiting for transfers between devices, on_device(): p4 = lax.ppermute(again, hier, back)  10 us
    all_to_all x1, waiting for transfers between devices, on_device(): got = lax.all_to_all(sent, group, 0, 0, tiled=True)  9.58 us
    all_to_all x1, starting transfers between devices, on_device(): back_got = lax.all_to_all(back_sent, group, 0, 0, tiled=True)  4.12 us
    ppermute x1, starting transfers between devices, on_device(): p2 = lax.ppermute(densities, hier, far)  3.91 us
    all_to_all x1, waiting for transfers between devices, on_device(): back_got = lax.all_to_all(back_sent, group, 0, 0, tiled=True)  3.84 us
    pallas_call x1, Pallas kernels, on_device(): back_sent = column_call(ints, reals, got, vhi, vlo)  2.97 us
    ppermute x1, waiting for transfers between devices, on_device(): p1 = lax.ppermute(densities, hier, near)  2.74 us
  transfers between devices with their start and end apart: 6, of which 5 were waited for; matrix products, arithmetic and copies ran while one was open for 1% of the time, Pallas kernels for 8%

profile of v4, /device:TPU:34, one launch (start us, length us, event | category | flops | bytes accessed | tf_op | source)
XLA Modules:
  0.0 66.2 jit_solution(5879873984665019734)
XLA Ops:
  0.0 3.9 %collective-permute-start = (f32[4,2,16,256]{3,2,1,0:T(8,128)}, f32[4,2,16,256]{3,2,1,0:T(8,128)S(1)}, u32[]{:S(2)}, u32[]{:S(2)}) collective-permute-start(f32[4,2,16,256]{3,2,1,0:T(8,128)} %x_ref.1), channel_id=1, source_target_pairs={{0,32},{32,64},{64,96},{96,128},{128,160},{160,192},{192,224},{224... | collective-permute-start | bytes 393224 | tf_op jit(solution)/shard_map/ppermute | solution.py:456
  3.9 2.0 %collective-permute-start.1 = (f32[4,2,16,256]{3,2,1,0:T(8,128)}, f32[4,2,16,256]{3,2,1,0:T(8,128)S(1)}, u32[]{:S(2)}, u32[]{:S(2)}) collective-permute-start(f32[4,2,16,256]{3,2,1,0:T(8,128)} %x_ref.1), channel_id=1, source_target_pairs={{16,32},{48,64},{80,96},{112,128},{144,160},{176,192},{208,224},{2... | collective-permute-start | bytes 393224 | tf_op jit(solution)/shard_map/ppermute | solution.py:457
  6.0 0.0 copy-start.2
  6.0 0.9 %copy-done.2 = f32[4,2,16,256]{3,2,1,0:T(8,128)S(1)} copy-done((f32[4,2,16,256]{3,2,1,0:T(8,128)S(1)}, f32[4,2,16,256]{3,2,1,0:T(8,128)}, u32[]{:S(2)}) %copy-start.2) | copy-done | bytes 131096
  6.9 0.8 %own.1._ = f32[32,16,128]{2,1,0:T(8,128)} custom-call(f32[128,256]{1,0:T(8,128)S(1)} %bitcast.2), custom_call_target="tpu_custom_call" | custom-call | flops 1000000 | bytes 4000000 | tf_op jit(solution)/shard_map/own/pallas_call | solution.py:458
  7.7 0.6 copy-done.4
  8.4 0.2 select_reduce_fusion
  8.6 0.0 copy-start
  8.6 0.3 collective-permute-done.far_ref.p2_ref
  8.9 2.7 %collective-permute-done.1.near_ref.p1_ref = f32[4,2,16,256]{3,2,1,0:T(8,128)S(1)} collective-permute-done((f32[4,2,16,256]{3,2,1,0:T(8,128)}, f32[4,2,16,256]{3,2,1,0:T(8,128)S(1)}, u32[]{:S(2)}, u32[]{:S(2)}) %collective-permute-start.1) | collective-permute-done | bytes 131104 | tf_op jit(solution)/shard_map/ppermute | solution.py:457
  11.6 1.3 %halo.1 = f32[32,16,128]{2,1,0:T(8,128)} custom-call(s32[16]{0:T(128)S(1)} %fusion.2.ints_in.ints_ref, f32[4,2,16,256]{3,2,1,0:T(8,128)S(1)} %collective-permute-done.far_ref.p2_ref, f32[4,2,16,256]{3,2,1,0:T(8,128)S(1)} %collective-permute-done.1.near_ref.p1_ref, f32[32,16,128]{2,1,0:T(8,128)} %own.1._), custom_call_target="tpu_custom_call", output_to_operand_aliasing={{}: (3, {})} | custom-call | flops 1000000 | bytes 4000000 | tf_op jit(solution)/shard_map/halo/pallas_call | solution.py:460
  13.0 14.8 %all-to-all-start = ((f32[32,16,128]{2,1,0:T(8,128)}), f32[32,16,128]{2,1,0:T(8,128)S(1)}, u32[]{:S(2)}, u32[]{:S(2)}) async-start(f32[32,16,128]{2,1,0:T(8,128)} %halo.1), calls=%async_computation | async-start | bytes 524288 | tf_op jit(solution)/shard_map/all_to_all | solution.py:462
  27.9 0.1 reshape.49
  28.0 2.1 %collective-permute-start.2 = (f32[4,2,16,256]{3,2,1,0:T(8,128)S(1)}, f32[4,2,16,256]{3,2,1,0:T(8,128)S(1)}, u32[]{:S(2)}, u32[]{:S(2)}) collective-permute-start(f32[4,2,16,256]{3,2,1,0:T(8,128)S(1)} %copy-done.3), channel_id=1, source_target_pairs={{0,16},{32,48},{64,80},{96,112},{128,144},{160,176},{192,208},{224... | collective-permute-start | bytes 393224 | tf_op jit(solution)/shard_map/ppermute | solution.py:463
  30.2 0.1 pad_maximum_fusion.reals_in.reals_ref
  30.2 0.1 weights.1
  30.4 9.6 %all-to-all-done.got_ref = f32[32,16,128]{2,1,0:T(8,128)S(1)} async-done(((f32[32,16,128]{2,1,0:T(8,128)}), f32[32,16,128]{2,1,0:T(8,128)S(1)}, u32[]{:S(2)}, u32[]{:S(2)}) %all-to-all-start) | async-done | bytes 262176 | tf_op jit(solution)/shard_map/all_to_all | solution.py:462
  40.0 3.0 %columns.1 = f32[32,32,128]{2,1,0:T(8,128)} custom-call(s32[16]{0:T(128)S(1)} %fusion.2.ints_in.ints_ref, f32[78]{0:T(128)S(1)} %pad_maximum_fusion.reals_in.reals_ref, f32[32,16,128]{2,1,0:T(8,128)S(1)} %all-to-all-done.got_ref, bf16[768,256]{1,0:T(8,128)(2,1)S(1)} %get-tuple-element.15.ghi_ref, bf16[768,256]{1,0:T(8,128)(2,1)S(1)} %get-tuple-element.16.glo_ref), custom_call_target="tpu_custom_call" | custom-call | flops 1000000000 | bytes 4000000 | tf_op jit(solution)/shard_map/columns/pallas_call | solution.py:464
  43.0 4.1 %all-to-all-start.1 = ((f32[32,32,128]{2,1,0:T(8,128)}), f32[32,32,128]{2,1,0:T(8,128)S(1)}, u32[]{:S(2)}, u32[]{:S(2)}) async-start(f32[32,32,128]{2,1,0:T(8,128)} %columns.1), calls=%async_computation.1 | async-start | bytes 1048576 | tf_op jit(solution)/shard_map/all_to_all | solution.py:466
  47.1 2.2 %collective-permute-start.3 = (f32[4,2,16,256]{3,2,1,0:T(8,128)S(1)}, f32[4,2,16,256]{3,2,1,0:T(8,128)S(1)}, u32[]{:S(2)}, u32[]{:S(2)}) collective-permute-start(f32[4,2,16,256]{3,2,1,0:T(8,128)S(1)} %copy-done.3), channel_id=1, source_target_pairs={{32,0},{64,32},{96,64},{128,96},{160,128},{192,160},{224,192},{256... | collective-permute-start | bytes 393224 | tf_op jit(solution)/shard_map/ppermute | solution.py:467
  49.3 10.0 %collective-permute-done.3.p4_ref = f32[4,2,16,256]{3,2,1,0:T(8,128)S(1)} collective-permute-done((f32[4,2,16,256]{3,2,1,0:T(8,128)S(1)}, f32[4,2,16,256]{3,2,1,0:T(8,128)S(1)}, u32[]{:S(2)}, u32[]{:S(2)}) %collective-permute-start.3) | collective-permute-done | bytes 131104 | tf_op jit(solution)/shard_map/ppermute | solution.py:467
  59.3 1.7 %rows.1.base_ref = f32[128,256]{1,0:T(8,128)S(1)} custom-call(s32[16]{0:T(128)S(1)} %fusion.2.ints_in.ints_ref, f32[78]{0:T(128)S(1)} %pad_maximum_fusion.reals_in.reals_ref, f32[4,2,16,256]{3,2,1,0:T(8,128)S(1)} %copy-done.3, f32[4,2,16,256]{3,2,1,0:T(8,128)S(1)} %collective-permute-done.1.near_ref.p1_ref, ...), custom_call_target="tpu_custom_call" | custom-call | flops 1000000000 | bytes 4000000 | tf_op jit(solution)/shard_map/rows/pallas_call | solution.py:468
  61.0 3.8 %all-to-all-done.1.got_ref = f32[32,32,128]{2,1,0:T(8,128)S(1)} async-done(((f32[32,32,128]{2,1,0:T(8,128)}), f32[32,32,128]{2,1,0:T(8,128)S(1)}, u32[]{:S(2)}, u32[]{:S(2)}) %all-to-all-start.1) | async-done | bytes 524320 | tf_op jit(solution)/shard_map/all_to_all | solution.py:466
  64.9 1.3 %finish.1 = f32[128,256]{1,0:T(8,128)} custom-call(s32[16]{0:T(128)S(1)} %fusion.2.ints_in.ints_ref, f32[32,32,128]{2,1,0:T(8,128)S(1)} %all-to-all-done.1.got_ref, f32[128,256]{1,0:T(8,128)S(1)} %rows.1.base_ref, bf16[256,768]{1,0:T(8,128)(2,1)S(1)} %get-tuple-element.21.ghi_ref, bf16[256,768]{1,0:T(8,128)(2,1)S(1)} %get-tuple-element.22.glo_ref), custom_call_target="tpu_custom_call" | custom-call | flops 300000000 | bytes 4000000 | tf_op jit(solution)/shard_map/finish/pallas_call | solution.py:469
  (17 shorter events, 0.1 us)
Async XLA Ops:
  0.0 8.9 %collective-permute-start = (f32[4,2,16,256]{3,2,1,0:T(8,128)}, f32[4,2,16,256]{3,2,1,0:T(8,128)S(1)}, u32[]{:S(2)}, u32[]{:S(2)}) collective-permute-start(f32[4,2,16,256]{3,2,1,0:T(8,128)} %x_ref.1), channel_id=1, source_target_pairs={{0,32},{32,64},{64,96},{96,128},{128,160},{160,192},{192,224},{224... | collective-permute-start | bytes 393224 | tf_op jit(solution)/shard_map/ppermute | solution.py:456
  3.9 7.7 %collective-permute-start.1 = (f32[4,2,16,256]{3,2,1,0:T(8,128)}, f32[4,2,16,256]{3,2,1,0:T(8,128)S(1)}, u32[]{:S(2)}, u32[]{:S(2)}) collective-permute-start(f32[4,2,16,256]{3,2,1,0:T(8,128)} %x_ref.1), channel_id=1, source_target_pairs={{16,32},{48,64},{80,96},{112,128},{144,160},{176,192},{208,224},{2... | collective-permute-start | bytes 393224 | tf_op jit(solution)/shard_map/ppermute | solution.py:457
  6.0 0.9 %copy-start.2 = (f32[4,2,16,256]{3,2,1,0:T(8,128)S(1)}, f32[4,2,16,256]{3,2,1,0:T(8,128)}, u32[]{:S(2)}) copy-start(f32[4,2,16,256]{3,2,1,0:T(8,128)} %x_ref.1) | copy-start | bytes 393220
  7.7 0.7 copy-start.4
  8.6 21.7 %copy-start = (f32[2,256,256]{2,1,0:T(8,128)S(1)}, f32[2,256,256]{2,1,0:T(8,128)}, u32[]{:S(2)}) copy-start(f32[2,256,256]{2,1,0:T(8,128)} %q_ref.1) | copy-start | bytes 1572868
  13.0 14.9 %copy-start.6 = (f32[2,2]{1,0:T(2,128)S(1)}, f32[2,2]{1,0:T(2,128)}, u32[]{:S(2)}) copy-start(f32[2,2]{1,0:T(2,128)} %param.10) | copy-start | bytes 52
  13.0 15.0 %copy-start.3 = (f32[4,2,16,256]{3,2,1,0:T(8,128)S(1)}, f32[4,2,16,256]{3,2,1,0:T(8,128)}, u32[]{:S(2)}) copy-start(f32[4,2,16,256]{3,2,1,0:T(8,128)} %x_ref.1) | copy-start | bytes 393220
  13.0 17.2 %copy-start.1 = (f32[256,256]{1,0:T(8,128)S(1)}, f32[256,256]{1,0:T(8,128)}, u32[]{:S(2)}) copy-start(f32[256,256]{1,0:T(8,128)} %h_ref.1) | copy-start | bytes 786436
  13.0 26.9 %all-to-all-start = ((f32[32,16,128]{2,1,0:T(8,128)}), f32[32,16,128]{2,1,0:T(8,128)S(1)}, u32[]{:S(2)}, u32[]{:S(2)}) async-start(f32[32,16,128]{2,1,0:T(8,128)} %halo.1), calls=%async_computation | async-start | bytes 524288 | tf_op jit(solution)/shard_map/all_to_all | solution.py:462
  28.0 2.2 %copy-start.5 = (f32[2]{0:T(128)S(1)}, f32[2]{0:T(128)}, u32[]{:S(2)}) copy-start(f32[2]{0:T(128)} %param.9) | copy-start | bytes 28
  28.0 15.0 %collective-permute-start.2 = (f32[4,2,16,256]{3,2,1,0:T(8,128)S(1)}, f32[4,2,16,256]{3,2,1,0:T(8,128)S(1)}, u32[]{:S(2)}, u32[]{:S(2)}) collective-permute-start(f32[4,2,16,256]{3,2,1,0:T(8,128)S(1)} %copy-done.3), channel_id=1, source_target_pairs={{0,16},{32,48},{64,80},{96,112},{128,144},{160,176},{192,208},{224... | collective-permute-start | bytes 393224 | tf_op jit(solution)/shard_map/ppermute | solution.py:463
  43.0 21.9 %all-to-all-start.1 = ((f32[32,32,128]{2,1,0:T(8,128)}), f32[32,32,128]{2,1,0:T(8,128)S(1)}, u32[]{:S(2)}, u32[]{:S(2)}) async-start(f32[32,32,128]{2,1,0:T(8,128)} %columns.1), calls=%async_computation.1 | async-start | bytes 1048576 | tf_op jit(solution)/shard_map/all_to_all | solution.py:466
  47.1 12.2 %collective-permute-start.3 = (f32[4,2,16,256]{3,2,1,0:T(8,128)S(1)}, f32[4,2,16,256]{3,2,1,0:T(8,128)S(1)}, u32[]{:S(2)}, u32[]{:S(2)}) collective-permute-start(f32[4,2,16,256]{3,2,1,0:T(8,128)S(1)} %copy-done.3), channel_id=1, source_target_pairs={{32,0},{64,32},{96,64},{128,96},{160,128},{192,160},{224,192},{256... | collective-permute-start | bytes 393224 | tf_op jit(solution)/shard_map/ppermute | solution.py:467

commit v5 on v4

--- a/solution.py
+++ b/solution.py
@@ -166,22 +166,35 @@
     return copies
 
 
-def halo_kernel(ints_in, far_ref, near_ref, _, o_ref, t_ref, ints_ref, sem, out_sem):
-    fetched = fetch([(ints_in, ints_ref)], sem)
-    near = near_ref[...].reshape(128, 256).T
-    far = far_ref[...].reshape(128, 256).T
-    lane = lax.broadcasted_iota(jnp.int32, near.shape, 1)
-    for copy in fetched:
-        copy.wait()
-    lower = ints_ref[SIDE] == 0
-    count = jnp.where(lower, ints_ref[COUNTS + 1], ints_ref[COUNTS + 3])
-    near = pltpu.roll(near, jnp.where(lower, 4 - count, 0) * 32, 1)
-    far = pltpu.roll(far, ((jnp.where(lower, 8 - count - ints_ref[COUNTS], count)) & 3) * 32, 1)
-    inside = (lane >= jnp.where(lower, 4 - count, 0) * 32) & (lane < jnp.where(lower, 4, count) * 32)
-    t_ref[...] = jnp.where(inside, near, far).reshape(32, 8, 128)
-    copy = pltpu.make_async_copy(t_ref, o_ref.at[:, 8:16], out_sem)
+def halo_kernel(wide_ref, far_ref, near_ref, _, o_ref, t_ref, sem):
+    def row(i):
+        return wide_ref[i : i + 1, :]
+
+    def turned(v, by, choices):
+        out = v
+        for k in range(1, choices):
+            out = jnp.where(by == k, pltpu.roll(v, 32 * k, 1), out)
+        return out
+
+    side = row(SIDE)
+    lower = 1 - side
+    count = lower * row(COUNTS + 1) + side * row(COUNTS + 3)
+    by_near = jnp.broadcast_to(lower * (4 - count), (256, 128))
+    by_far = jnp.broadcast_to((lower * (8 - count - row(COUNTS)) + side * count) & 3, (256, 128))
+    begin = jnp.broadcast_to(lower * (4 - count), (256, 128))
+    end = jnp.broadcast_to(lower * 4 + side * count, (256, 128))
+    near = turned(near_ref[...].reshape(128, 256).T, by_near, 3)
+    far = turned(far_ref[...].reshape(128, 256).T, by_far, 4)
+    node = lax.broadcasted_iota(jnp.int32, (256, 128), 1) // 32
+    t_ref[...] = jnp.where(node >= begin, jnp.where(node < end, near, far), far).reshape(32, 8, 128)
+    copy = pltpu.make_async_copy(t_ref, o_ref.at[:, 8:16], sem)
     copy.start()
     copy.wait()
+
+
+def pair_kernel(ints_ref, x_ref, near_ref, o_ref):
+    o_ref[0:4] = x_ref[...]
+    o_ref[4:6] = near_ref[pl.ds(jnp.where(ints_ref[SIDE] == 0, ints_ref[COUNTS + 1] - 2, 0), 2)]
 
 
 def column_kernel(
@@ -266,7 +279,7 @@
 
 
 def row_kernel(
-    ints_ref, reals_ref, x_ref, p1_ref, p2_ref, p3_ref, p4_ref, ghi_ref, glo_ref, o_ref, w_ref, hi_ref, lo_ref, hi2_ref, lo2_ref
+    ints_ref, reals_ref, x_ref, p1_ref, p2_ref, pair_ref, ghi_ref, glo_ref, o_ref, w_ref, hi_ref, lo_ref, hi2_ref, lo2_ref
 ):
     nodes = Nodes(ints_ref, reals_ref, ints_ref[HERE_BEGIN])
     re, im = nodes.re, (-nodes.im[0], -nodes.im[1])
@@ -275,8 +288,8 @@
     w_ref[8:12] = x_ref[...]
     w_ref[pl.ds(4 + 8 * up, 4)] = p1_ref[...]
     w_ref[pl.ds(16 * up, 4)] = p2_ref[...]
-    w_ref[pl.ds(12 - 8 * up, 4)] = p3_ref[...]
-    w_ref[pl.ds(16 - 16 * up, 4)] = p4_ref[...]
+    w_ref[pl.ds(12 - 8 * up, 4)] = pair_ref[0:4]
+    w_ref[pl.ds(jnp.where(up == 0, 16, farther - 2), 2)] = pair_ref[4:6]
 
     def slot(p):
         j = p - 4
@@ -374,12 +387,13 @@
 halo_call = call(
     halo_kernel,
     struct((32, 16, 128)),
-    [ANY] + [VMEM] * 2 + [ANY],
-    [pltpu.VMEM((32, 8, 128), F32), INTS, pltpu.SemaphoreType.DMA((1,)), pltpu.SemaphoreType.DMA],
+    [VMEM] * 3 + [ANY],
+    [pltpu.VMEM((32, 8, 128), F32), pltpu.SemaphoreType.DMA],
     out_specs=ANY,
     aliases={3: 0},
     name="halo",
 )
+pair_call = call(pair_kernel, struct((6, 2, 16, 256)), [SMEM] + [VMEM] * 2, name="pair")
 column_call = call(
     column_kernel,
     struct((32, 32, 128)),
@@ -404,7 +418,7 @@
 row_call = call(
     row_kernel,
     struct((128, 256)),
-    [SMEM] * 2 + [VMEM] * 7,
+    [SMEM] * 2 + [VMEM] * 6,
     [
         pltpu.VMEM((20, 2, 16, 256), F32),
         pltpu.VMEM((384, 768), BF),
@@ -420,14 +434,12 @@
 )
 
 
-def swap_routes(shards):
+def routes(shards):
     pairs = [(i, i + 1) for i in range(1, shards - 1, 2)]
     near = pairs + [(b, a) for a, b in pairs]
     far = [(i, i + 2) for i in range(0, shards - 2, 2)] + [(i, i - 2) for i in range(3, shards, 2)]
     pairs = [(i, i + 1) for i in range(0, shards, 2)]
-    inner = pairs + [(b, a) for a, b in pairs]
-    back = [(i, i - 2) for i in range(2, shards, 2)] + [(i, i + 2) for i in range(1, shards - 2, 2)]
-    return near, far, inner, back
+    return near, far, pairs + [(b, a) for a, b in pairs]
 
 
 def integers(node_count):
@@ -452,20 +464,20 @@
     group = ("col", "r")
     ints = integers(node_count)
     reals = jnp.concatenate([gamma, coeff.reshape(4), jnp.sqrt(jnp.arange(ROOTS, dtype=F32))])
-    near, far, inner, back = swap_routes(node_count.shape[0])
+    near, far, inner = routes(node_count.shape[0])
     p2 = lax.ppermute(densities, hier, far)
     p1 = lax.ppermute(densities, hier, near)
     part = own_call(densities.reshape(128, 256))
     vhi, vlo, hhi, hlo = weights_call(hamiltonian, couplings)
-    sent = halo_call(ints, p2, p1, part)
-    sent, again = lax.optimization_barrier((sent, densities))
+    sent = halo_call(jnp.broadcast_to(ints[:, None], (16, 128)), p2, p1, part)
+    sent, x, p1 = lax.optimization_barrier((sent, densities, p1))
     got = lax.all_to_all(sent, group, 0, 0, tiled=True)
-    p3 = lax.ppermute(again, hier, inner)
+    pair = pair_call(ints, x, p1)
     back_sent = column_call(ints, reals, got, vhi, vlo)
-    back_sent, p3, again = lax.optimization_barrier((back_sent, p3, densities))
+    back_sent, pair = lax.optimization_barrier((back_sent, pair))
     back_got = lax.all_to_all(back_sent, group, 0, 0, tiled=True)
-    p4 = lax.ppermute(again, hier, back)
-    base = row_call(ints, reals, densities, p1, p2, p3, p4, vhi, vlo)
+    pair = lax.ppermute(pair, hier, inner)
+    base = row_call(ints, reals, x, p1, p2, pair, vhi, vlo)
     out = finish_call(ints, back_got, base, hhi, hlo)
     return out.reshape(4, 2, 16, 256)
 

time: 66.6 us -> 66.3 us (level)
  starting transfers between devices: 29.2 us -> 27.1 us
  waiting for transfers between devices: 26.5 us -> 27.4 us
  local copies, waits for them, and re-layouts: 1.67 us -> 2.38 us
    ppermute x2 -> x1, starting transfers between devices: 4.32 us -> 2.26 us  [on_device(): pair = lax.ppermute(pair, hier, inner)]
    all_to_all x1, waiting for transfers between devices: 9.58 us -> 10.5 us  [on_device(): got = lax.all_to_all(sent, group, 0, 0, tiled=True)]
    ppermute x2 -> x1, waiting for transfers between devices: 10 us -> 9.67 us  [on_device(): pair = lax.ppermute(pair, hier, inner)]
    pallas_call x2 -> x3, Pallas kernels: 3.07 us -> 3.25 us  [the longest x1 1.7 us: on_device(): base = row_call(ints, reals, x, p1, p2, pair, vhi, vlo)]
  transfers between devices with their start and end apart: 6 -> 5, of which waited for: 5 -> 5; matrix products, arithmetic and copies ran while one was open for 1% -> 1% of each run, Pallas kernels for 8% -> 5%
where the time goes in v5:
time: 66.3 us; the launch traced here: 65.8 us
  waiting for transfers between devices  27.4 us (41%)
  starting transfers between devices  27.1 us (41%)
  Pallas kernels  8.45 us (13%)
  local copies, waits for them, and re-layouts  2.38 us (4%)
    all_to_all x1, starting transfers between devices, on_device(): got = lax.all_to_all(sent, group, 0, 0, tiled=True)  14.8 us
    all_to_all x1, waiting for transfers between devices, on_device(): got = lax.all_to_all(sent, group, 0, 0, tiled=True)  10.5 us
    ppermute x1, waiting for transfers between devices, on_device(): pair = lax.ppermute(pair, hier, inner)  9.67 us
    all_to_all x1, waiting for transfers between devices, on_device(): back_got = lax.all_to_all(back_sent, group, 0, 0, tiled=True)  4.14 us
    all_to_all x1, starting transfers between devices, on_device(): back_got = lax.all_to_all(back_sent, group, 0, 0, tiled=True)  4.11 us
    ppermute x1, starting transfers between devices, on_device(): p2 = lax.ppermute(densities, hier, far)  3.91 us
    pallas_call x1, Pallas kernels, on_device(): back_sent = column_call(ints, reals, got, vhi, vlo)  2.94 us
    ppermute x1, waiting for transfers between devices, on_device(): p1 = lax.ppermute(densities, hier, near)  2.74 us
  transfers between devices with their start and end apart: 5, of which 5 were waited for; matrix products, arithmetic and copies ran while one was open for 1% of the time, Pallas kernels for 5%

profile of v5, /device:TPU:34, one launch (start us, length us, event | category | flops | bytes accessed | tf_op | source)
XLA Modules:
  0.0 65.8 jit_solution(622748830576181996)
XLA Ops:
  0.0 3.9 %collective-permute-start = (f32[4,2,16,256]{3,2,1,0:T(8,128)}, f32[4,2,16,256]{3,2,1,0:T(8,128)S(1)}, u32[]{:S(2)}, u32[]{:S(2)}) collective-permute-start(f32[4,2,16,256]{3,2,1,0:T(8,128)} %x_ref.1), channel_id=1, source_target_pairs={{0,32},{32,64},{64,96},{96,128},{128,160},{160,192},{192,224},{224... | collective-permute-start | bytes 393224 | tf_op jit(solution)/shard_map/ppermute | solution.py:468
  3.9 2.0 %collective-permute-start.1 = (f32[4,2,16,256]{3,2,1,0:T(8,128)}, f32[4,2,16,256]{3,2,1,0:T(8,128)S(1)}, u32[]{:S(2)}, u32[]{:S(2)}) collective-permute-start(f32[4,2,16,256]{3,2,1,0:T(8,128)} %x_ref.1), channel_id=1, source_target_pairs={{16,32},{48,64},{80,96},{112,128},{144,160},{176,192},{208,224},{2... | collective-permute-start | bytes 393224 | tf_op jit(solution)/shard_map/ppermute | solution.py:469
  6.0 0.9 %copy-done.1 = f32[4,2,16,256]{3,2,1,0:T(8,128)S(1)} copy-done((f32[4,2,16,256]{3,2,1,0:T(8,128)S(1)}, f32[4,2,16,256]{3,2,1,0:T(8,128)}, u32[]{:S(2)}) %copy-start.1) | copy-done | bytes 131096
  6.9 0.8 %own.1._ = f32[32,16,128]{2,1,0:T(8,128)} custom-call(f32[128,256]{1,0:T(8,128)S(1)} %bitcast.2), custom_call_target="tpu_custom_call" | custom-call | flops 1000000 | bytes 4000000 | tf_op jit(solution)/shard_map/own/pallas_call | solution.py:470
  7.7 0.6 copy-done.4
  8.4 0.2 select_reduce_fusion
  8.6 0.3 collective-permute-done.far_ref.p2_ref
  8.9 2.7 %collective-permute-done.1.near_ref.p1_ref = f32[4,2,16,256]{3,2,1,0:T(8,128)S(1)} collective-permute-done((f32[4,2,16,256]{3,2,1,0:T(8,128)}, f32[4,2,16,256]{3,2,1,0:T(8,128)S(1)}, u32[]{:S(2)}, u32[]{:S(2)}) %collective-permute-start.1) | collective-permute-done | bytes 131104 | tf_op jit(solution)/shard_map/ppermute | solution.py:469
  11.6 0.1 broadcast_in_dim.30.wide_ref
  11.7 1.0 %halo.1 = f32[32,16,128]{2,1,0:T(8,128)} custom-call(s32[16,128]{1,0:T(8,128)S(1)} %broadcast_in_dim.30.wide_ref, f32[4,2,16,256]{3,2,1,0:T(8,128)S(1)} %collective-permute-done.far_ref.p2_ref, f32[4,2,16,256]{3,2,1,0:T(8,128)S(1)} %collective-permute-done.1.near_ref.p1_ref, f32[32,16,128]{2,1,0:T(8,128)} %own.1._), custom_call_target="tpu_custom_call", output_to_operand_aliasing={{}: (3, {})} | custom-call | flops 1000000 | bytes 4000000 | tf_op jit(solution)/shard_map/halo/pallas_call | solution.py:472
  12.7 14.8 %all-to-all-start = ((f32[32,16,128]{2,1,0:T(8,128)}), f32[32,16,128]{2,1,0:T(8,128)S(1)}, u32[]{:S(2)}, u32[]{:S(2)}) async-start(f32[32,16,128]{2,1,0:T(8,128)} %halo.1), calls=%async_computation | async-start | bytes 524288 | tf_op jit(solution)/shard_map/all_to_all | solution.py:474
  27.6 0.1 reshape.57
  27.7 0.1 weights.1
  27.9 0.6 copy-done.5
  28.5 0.1 pad_maximum_fusion.reals_in.reals_ref
  28.6 0.6 pair.1
  29.1 10.5 %all-to-all-done.got_ref = f32[32,16,128]{2,1,0:T(8,128)S(1)} async-done(((f32[32,16,128]{2,1,0:T(8,128)}), f32[32,16,128]{2,1,0:T(8,128)S(1)}, u32[]{:S(2)}, u32[]{:S(2)}) %all-to-all-start) | async-done | bytes 262176 | tf_op jit(solution)/shard_map/all_to_all | solution.py:474
  39.7 2.9 %columns.1 = f32[32,32,128]{2,1,0:T(8,128)} custom-call(s32[16]{0:T(128)S(1)} %fusion.2.ints_in.ints_ref, f32[78]{0:T(128)S(1)} %pad_maximum_fusion.reals_in.reals_ref, f32[32,16,128]{2,1,0:T(8,128)S(1)} %all-to-all-done.got_ref, bf16[768,256]{1,0:T(8,128)(2,1)S(1)} %get-tuple-element.15.ghi_ref, bf16[768,256]{1,0:T(8,128)(2,1)S(1)} %get-tuple-element.16.glo_ref), custom_call_target="tpu_custom_call" | custom-call | flops 1000000000 | bytes 4000000 | tf_op jit(solution)/shard_map/columns/pallas_call | solution.py:476
  42.6 4.1 %all-to-all-start.1 = ((f32[32,32,128]{2,1,0:T(8,128)}), f32[32,32,128]{2,1,0:T(8,128)S(1)}, u32[]{:S(2)}, u32[]{:S(2)}) async-start(f32[32,32,128]{2,1,0:T(8,128)} %columns.1), calls=%async_computation.1 | async-start | bytes 1048576 | tf_op jit(solution)/shard_map/all_to_all | solution.py:478
  46.7 2.3 %collective-permute-start.2 = (f32[6,2,16,256]{3,2,1,0:T(8,128)S(1)}, f32[6,2,16,256]{3,2,1,0:T(8,128)S(1)}, u32[]{:S(2)}, u32[]{:S(2)}) collective-permute-start(f32[6,2,16,256]{3,2,1,0:T(8,128)S(1)} %pair.1), channel_id=1, source_target_pairs={{0,16},{32,48},{64,80},{96,112},{128,144},{160,176},{192,208},{224... | collective-permute-start | bytes 589832 | tf_op jit(solution)/shard_map/ppermute | solution.py:479
  49.0 9.7 %collective-permute-done.2.pair_ref = f32[6,2,16,256]{3,2,1,0:T(8,128)S(1)} collective-permute-done((f32[6,2,16,256]{3,2,1,0:T(8,128)S(1)}, f32[6,2,16,256]{3,2,1,0:T(8,128)S(1)}, u32[]{:S(2)}, u32[]{:S(2)}) %collective-permute-start.2) | collective-permute-done | bytes 196640 | tf_op jit(solution)/shard_map/ppermute | solution.py:479
  58.7 1.7 %rows.1.base_ref = f32[128,256]{1,0:T(8,128)S(1)} custom-call(s32[16]{0:T(128)S(1)} %fusion.2.ints_in.ints_ref, f32[78]{0:T(128)S(1)} %pad_maximum_fusion.reals_in.reals_ref, f32[4,2,16,256]{3,2,1,0:T(8,128)S(1)} %copy-done.2, f32[4,2,16,256]{3,2,1,0:T(8,128)S(1)} %collective-permute-done.1.near_ref.p1_ref, ...), custom_call_target="tpu_custom_call" | custom-call | flops 1000000000 | bytes 4000000 | tf_op jit(solution)/shard_map/rows/pallas_call | solution.py:480
  60.4 4.1 %all-to-all-done.1.got_ref = f32[32,32,128]{2,1,0:T(8,128)S(1)} async-done(((f32[32,32,128]{2,1,0:T(8,128)}), f32[32,32,128]{2,1,0:T(8,128)S(1)}, u32[]{:S(2)}, u32[]{:S(2)}) %all-to-all-start.1) | async-done | bytes 524320 | tf_op jit(solution)/shard_map/all_to_all | solution.py:478
  64.5 1.3 %finish.1 = f32[128,256]{1,0:T(8,128)} custom-call(s32[16]{0:T(128)S(1)} %fusion.2.ints_in.ints_ref, f32[32,32,128]{2,1,0:T(8,128)S(1)} %all-to-all-done.1.got_ref, f32[128,256]{1,0:T(8,128)S(1)} %rows.1.base_ref, bf16[256,768]{1,0:T(8,128)(2,1)S(1)} %get-tuple-element.21.ghi_ref, bf16[256,768]{1,0:T(8,128)(2,1)S(1)} %get-tuple-element.22.glo_ref), custom_call_target="tpu_custom_call" | custom-call | flops 300000000 | bytes 4000000 | tf_op jit(solution)/shard_map/finish/pallas_call | solution.py:481
  (17 shorter events, 0.1 us)
Async XLA Ops:
  0.0 8.9 %collective-permute-start = (f32[4,2,16,256]{3,2,1,0:T(8,128)}, f32[4,2,16,256]{3,2,1,0:T(8,128)S(1)}, u32[]{:S(2)}, u32[]{:S(2)}) collective-permute-start(f32[4,2,16,256]{3,2,1,0:T(8,128)} %x_ref.1), channel_id=1, source_target_pairs={{0,32},{32,64},{64,96},{96,128},{128,160},{160,192},{192,224},{224... | collective-permute-start | bytes 393224 | tf_op jit(solution)/shard_map/ppermute | solution.py:468
  3.9 7.7 %collective-permute-start.1 = (f32[4,2,16,256]{3,2,1,0:T(8,128)}, f32[4,2,16,256]{3,2,1,0:T(8,128)S(1)}, u32[]{:S(2)}, u32[]{:S(2)}) collective-permute-start(f32[4,2,16,256]{3,2,1,0:T(8,128)} %x_ref.1), channel_id=1, source_target_pairs={{16,32},{48,64},{80,96},{112,128},{144,160},{176,192},{208,224},{2... | collective-permute-start | bytes 393224 | tf_op jit(solution)/shard_map/ppermute | solution.py:469
  6.0 0.9 %copy-start.1 = (f32[4,2,16,256]{3,2,1,0:T(8,128)S(1)}, f32[4,2,16,256]{3,2,1,0:T(8,128)}, u32[]{:S(2)}) copy-start(f32[4,2,16,256]{3,2,1,0:T(8,128)} %x_ref.1) | copy-start | bytes 393220
  7.7 0.7 copy-start.4
  11.7 16.0 %copy-start = (f32[2,256,256]{2,1,0:T(8,128)S(1)}, f32[2,256,256]{2,1,0:T(8,128)}, u32[]{:S(2)}) copy-start(f32[2,256,256]{2,1,0:T(8,128)} %q_ref.1) | copy-start | bytes 1572868
  12.7 14.9 %copy-start.6 = (f32[2,2]{1,0:T(2,128)S(1)}, f32[2,2]{1,0:T(2,128)}, u32[]{:S(2)}) copy-start(f32[2,2]{1,0:T(2,128)} %param.10) | copy-start | bytes 52
  12.7 14.9 %copy-start.3 = (f32[256,256]{1,0:T(8,128)S(1)}, f32[256,256]{1,0:T(8,128)}, u32[]{:S(2)}) copy-start(f32[256,256]{1,0:T(8,128)} %h_ref.1) | copy-start | bytes 786436
  12.7 26.9 %all-to-all-start = ((f32[32,16,128]{2,1,0:T(8,128)}), f32[32,16,128]{2,1,0:T(8,128)S(1)}, u32[]{:S(2)}, u32[]{:S(2)}) async-start(f32[32,16,128]{2,1,0:T(8,128)} %halo.1), calls=%async_computation | async-start | bytes 524288 | tf_op jit(solution)/shard_map/all_to_all | solution.py:474
  27.7 0.9 %copy-start.2 = (f32[4,2,16,256]{3,2,1,0:T(8,128)S(1)}, f32[4,2,16,256]{3,2,1,0:T(8,128)}, u32[]{:S(2)}) copy-start(f32[4,2,16,256]{3,2,1,0:T(8,128)} %x_ref.1) | copy-start | bytes 393220
  27.8 0.7 copy-start.5
  42.6 21.9 %all-to-all-start.1 = ((f32[32,32,128]{2,1,0:T(8,128)}), f32[32,32,128]{2,1,0:T(8,128)S(1)}, u32[]{:S(2)}, u32[]{:S(2)}) async-start(f32[32,32,128]{2,1,0:T(8,128)} %columns.1), calls=%async_computation.1 | async-start | bytes 1048576 | tf_op jit(solution)/shard_map/all_to_all | solution.py:478
  46.7 11.9 %collective-permute-start.2 = (f32[6,2,16,256]{3,2,1,0:T(8,128)S(1)}, f32[6,2,16,256]{3,2,1,0:T(8,128)S(1)}, u32[]{:S(2)}, u32[]{:S(2)}) collective-permute-start(f32[6,2,16,256]{3,2,1,0:T(8,128)S(1)} %pair.1), channel_id=1, source_target_pairs={{0,16},{32,48},{64,80},{96,112},{128,144},{160,176},{192,208},{224... | collective-permute-start | bytes 589832 | tf_op jit(solution)/shard_map/ppermute | solution.py:479

commit v6 on v5

--- a/solution.py
+++ b/solution.py
@@ -8,7 +8,7 @@
 STEP = 0.2
 HALF2 = 0.5 * STEP * STEP
 SLOTS = 4
-TOTAL, TEAM_BEGIN, HERE_BEGIN, SIDE, COUNTS = 0, 1, 2, 3, 4
+TOTAL, TEAM_BEGIN, HERE_BEGIN, SIDE, COUNTS, ODD = 0, 1, 2, 3, 4, 9
 ROOTS = 72
 BF = jnp.bfloat16
 F32 = jnp.float32
@@ -152,11 +152,8 @@
         hlo[:, 256 * b : 256 * b + 256] = lo
 
 
-def own_kernel(x_ref, o_ref, t_ref, sem):
-    t_ref[...] = x_ref[...].T.reshape(32, 8, 128)
-    copy = pltpu.make_async_copy(t_ref, o_ref.at[:, 0:8], sem)
-    copy.start()
-    copy.wait()
+def own_kernel(x_ref, o_ref):
+    o_ref[...] = x_ref[...].T.reshape(32, 8, 128)
 
 
 def fetch(pairs, sem):
@@ -166,30 +163,32 @@
     return copies
 
 
-def halo_kernel(wide_ref, far_ref, near_ref, _, o_ref, t_ref, sem):
-    def row(i):
-        return wide_ref[i : i + 1, :]
-
-    def turned(v, by, choices):
-        out = v
-        for k in range(1, choices):
-            out = jnp.where(by == k, pltpu.roll(v, 32 * k, 1), out)
-        return out
-
-    side = row(SIDE)
-    lower = 1 - side
-    count = lower * row(COUNTS + 1) + side * row(COUNTS + 3)
-    by_near = jnp.broadcast_to(lower * (4 - count), (256, 128))
-    by_far = jnp.broadcast_to((lower * (8 - count - row(COUNTS)) + side * count) & 3, (256, 128))
-    begin = jnp.broadcast_to(lower * (4 - count), (256, 128))
-    end = jnp.broadcast_to(lower * 4 + side * count, (256, 128))
-    near = turned(near_ref[...].reshape(128, 256).T, by_near, 3)
-    far = turned(far_ref[...].reshape(128, 256).T, by_far, 4)
-    node = lax.broadcasted_iota(jnp.int32, (256, 128), 1) // 32
-    t_ref[...] = jnp.where(node >= begin, jnp.where(node < end, near, far), far).reshape(32, 8, 128)
-    copy = pltpu.make_async_copy(t_ref, o_ref.at[:, 8:16], sem)
-    copy.start()
-    copy.wait()
+def team_counts(ints_ref):
+    side = ints_ref[SIDE]
+    return ints_ref[COUNTS + 2 - side], ints_ref[COUNTS + 3 - side]
+
+
+def edge_kernel(ints_in, got_ref, own_ref, first_ref, last_ref, y_ref, ints_ref, sem):
+    fetched = fetch([(ints_in, ints_ref)], sem)
+    for place in range(2):
+        vs = []
+        for low in range(8):
+            vs.append(jnp.concatenate([got_ref[(8 * high + low) * 2 + place] for high in range(2)], axis=0))
+        for m, v in enumerate(granules(vs)):
+            y_ref[SLOTS * place + m // 2, m % 2] = jnp.concatenate([v[:8], v[8:]], axis=1)
+    for copy in fetched:
+        copy.wait()
+    own, other = team_counts(ints_ref)
+    odd = ints_ref[ODD]
+
+    def node(j):
+        return y_ref[jnp.where(j < own, SLOTS * odd + j, SLOTS * (1 - odd) + jnp.minimum(j - own, SLOTS - 1))]
+
+    for j in range(8):
+        own_ref[j] = node(j)
+    for j in range(4):
+        first_ref[j] = own_ref[j]
+        last_ref[j] = own_ref[own + other - 4 + j]
 
 
 def pair_kernel(ints_ref, x_ref, near_ref, o_ref):
@@ -198,31 +197,22 @@
 
 
 def column_kernel(
-    ints_in, reals_in, got_ref, ghi_ref, glo_ref, o_ref, y_ref, hi_ref, lo_ref, hi2_ref, lo2_ref, z_ref, send_ref, ints_ref, reals_ref, sem, out_sem
+    ints_in, reals_in, own_ref, below_ref, above_ref, ghi_ref, glo_ref, o_ref, y_ref, hi_ref, lo_ref, hi2_ref, lo2_ref, z_ref, send_ref, ints_ref, reals_ref, sem, out_sem
 ):
     fetched = fetch([(ints_in, ints_ref), (reals_in, reals_ref)], sem)
-    places = ((1, 0), (0, 0), (0, 1), (1, 1))
-    for i, (g, r) in enumerate(places):
-        vs = []
-        for low in range(8):
-            vs.append(jnp.concatenate([got_ref[(8 * high + low) * 2 + r, 8 * g : 8 * g + 8, :] for high in range(2)], axis=0))
-        for m, v in enumerate(granules(vs)):
-            y_ref[SLOTS * i + m // 2, m % 2] = jnp.concatenate([v[:8], v[8:]], axis=1)
+    y_ref[0:4] = below_ref[...]
+    y_ref[4:12] = own_ref[...]
+    y_ref[12:16] = above_ref[...]
     for copy in fetched:
         copy.wait()
     nodes = Nodes(ints_ref, reals_ref, ints_ref[TEAM_BEGIN])
-    own, other = ints_ref[COUNTS + 2 - ints_ref[SIDE]], ints_ref[COUNTS + 3 - ints_ref[SIDE]]
+    own, other = team_counts(ints_ref)
+    odd = ints_ref[ODD]
     re, im = nodes.re, nodes.im
-
-    def slot(p):
-        j = p - 4
-        if j < 0:
-            return p
-        return jnp.where(j < own, 4 + j, jnp.where(j < own + other, 8 + j - own, jnp.minimum(12 + j - own - other, 15)))
-
+    y_ref[pl.ds(4 + own + other, 4)] = above_ref[...]
     x = []
     for p in range(16):
-        v = y_ref[slot(p)]
+        v = y_ref[p]
         x.append((v[0], v[1]))
     a2, b2 = {}, {}
     for p in range(2, 14):
@@ -266,7 +256,7 @@
                 vs.append(jnp.concatenate([v[:, :128], v[:, 128:]], axis=0))
             for low, v in enumerate(granules(vs)):
                 for high in range(2):
-                    send_ref[z, (8 * high + low) * 2 + r] = v[8 * high : 8 * high + 8]
+                    send_ref[z, (8 * high + low) * 2 + (odd if r == 0 else 1 - odd)] = v[8 * high : 8 * high + 8]
         copy = pltpu.make_async_copy(send_ref.at[z], o_ref.at[:, 8 * z : 8 * z + 8], out_sem.at[z])
         copy.start()
         return copy
@@ -380,24 +370,20 @@
     [VMEM] * 2,
     name="weights",
 )
-own_call = call(
-    own_kernel, struct((32, 16, 128)), [VMEM], [pltpu.VMEM((32, 8, 128), F32), pltpu.SemaphoreType.DMA], out_specs=ANY, name="own"
-)
+own_call = call(own_kernel, struct((32, 8, 128)), [VMEM], name="own")
 INTS = pltpu.SMEM((16,), jnp.int32)
-halo_call = call(
-    halo_kernel,
-    struct((32, 16, 128)),
-    [VMEM] * 3 + [ANY],
-    [pltpu.VMEM((32, 8, 128), F32), pltpu.SemaphoreType.DMA],
-    out_specs=ANY,
-    aliases={3: 0},
-    name="halo",
+edge_call = call(
+    edge_kernel,
+    (struct((8, 2, 8, 256)), struct((4, 2, 8, 256)), struct((4, 2, 8, 256))),
+    [ANY, VMEM],
+    [pltpu.VMEM((8, 2, 8, 256), F32), INTS, pltpu.SemaphoreType.DMA((1,))],
+    name="edge",
 )
 pair_call = call(pair_kernel, struct((6, 2, 16, 256)), [SMEM] + [VMEM] * 2, name="pair")
 column_call = call(
     column_kernel,
     struct((32, 32, 128)),
-    [ANY] * 2 + [VMEM] * 3,
+    [ANY] * 2 + [VMEM] * 5,
     [
         pltpu.VMEM((16, 2, 8, 256), F32),
         pltpu.VMEM((640, 768), BF),
@@ -439,7 +425,15 @@
     near = pairs + [(b, a) for a, b in pairs]
     far = [(i, i + 2) for i in range(0, shards - 2, 2)] + [(i, i - 2) for i in range(3, shards, 2)]
     pairs = [(i, i + 1) for i in range(0, shards, 2)]
-    return near, far, pairs + [(b, a) for a, b in pairs]
+    inner = pairs + [(b, a) for a, b in pairs]
+    onward = [(i, (i // 2 + 1) * 2 + 1 - i % 2) for i in range(shards - 2)]
+    return near, far, inner, onward, [(b, a) for a, b in onward]
+
+
+def groups(shards, columns):
+    return [
+        [(2 * team + (side ^ team % 2)) * columns + c for c in range(columns) for side in range(2)] for team in range(shards // 2)
+    ]
 
 
 def integers(node_count):
@@ -453,29 +447,38 @@
         (row == TOTAL)
         | ((row == TEAM_BEGIN) & (column < 2 * team))
         | ((row == HERE_BEGIN) & (column < here))
-        | ((row >= COUNTS) & (column == near))
+        | ((row >= COUNTS) & (row < ODD) & (column == near))
     )
     sums = jnp.sum(jnp.where(wanted, node_count[None, :], 0), axis=1)
-    return sums + jnp.where(row[:, 0] == SIDE, side, 0)
+    return sums + jnp.where(row[:, 0] == SIDE, side, 0) + jnp.where(row[:, 0] == ODD, team & 1, 0)
 
 
 def on_device(densities, hamiltonian, couplings, gamma, coeff, node_count):
     hier = ("team", "r")
-    group = ("col", "r")
+    shards = node_count.shape[0]
+    everyone = ("team", "r", "col")
+    lists = groups(shards, lax.axis_size("col"))
+    near, far, inner, onward, backward = routes(shards)
+
+    def exchange(v):
+        return lax.all_to_all(v, everyone, 0, 0, axis_index_groups=lists, tiled=True)
+
     ints = integers(node_count)
     reals = jnp.concatenate([gamma, coeff.reshape(4), jnp.sqrt(jnp.arange(ROOTS, dtype=F32))])
-    near, far, inner = routes(node_count.shape[0])
-    p2 = lax.ppermute(densities, hier, far)
-    p1 = lax.ppermute(densities, hier, near)
-    part = own_call(densities.reshape(128, 256))
     vhi, vlo, hhi, hlo = weights_call(hamiltonian, couplings)
-    sent = halo_call(jnp.broadcast_to(ints[:, None], (16, 128)), p2, p1, part)
-    sent, x, p1 = lax.optimization_barrier((sent, densities, p1))
-    got = lax.all_to_all(sent, group, 0, 0, tiled=True)
+    sent, x = lax.optimization_barrier((own_call(densities.reshape(128, 256)), densities))
+    got = exchange(sent)
+    p1 = lax.ppermute(x, hier, near)
+    p2 = lax.ppermute(x, hier, far)
+    own, first, last = edge_call(ints, got)
+    below = lax.ppermute(last, hier, onward)
+    above = lax.ppermute(first, hier, backward)
+    own, p1, p2, x = lax.optimization_barrier((own, p1, p2, x))
     pair = pair_call(ints, x, p1)
-    back_sent = column_call(ints, reals, got, vhi, vlo)
+    own, pair = lax.optimization_barrier((own, pair))
+    back_sent = column_call(ints, reals, own, below, above, vhi, vlo)
     back_sent, pair = lax.optimization_barrier((back_sent, pair))
-    back_got = lax.all_to_all(back_sent, group, 0, 0, tiled=True)
+    back_got = exchange(back_sent)
     pair = lax.ppermute(pair, hier, inner)
     base = row_call(ints, reals, x, p1, p2, pair, vhi, vlo)
     out = finish_call(ints, back_got, base, hhi, hlo)

time: 66.3 us -> 73.7 us (1.11)
  the two profiles are of different devices: /device:TPU:34 before, /device:TPU:28 now
where the time goes in v6:
time: 73.7 us; the launch traced here: 73.2 us
  starting transfers between devices  35.3 us (48%)
  waiting for transfers between devices  25.2 us (34%)
  Pallas kernels  9.82 us (13%)
  local copies, waits for them, and re-layouts  2.36 us (3%)
    all_to_all x2, starting transfers between devices, exchange(): lax.all_to_all(v, everyone, 0, 0, axis_index_groups=lists, tiled=True)  17.9 us
    all_to_all x2, waiting for transfers between devices, exchange(): lax.all_to_all(v, everyone, 0, 0, axis_index_groups=lists, tiled=True)  10.2 us
    ppermute x1, waiting for transfers between devices, on_device(): pair = lax.ppermute(pair, hier, inner)  9.67 us
    ppermute x1, starting transfers between devices, on_device(): p2 = lax.ppermute(x, hier, far)  6.75 us
    ppermute x1, waiting for transfers between devices, on_device(): above = lax.ppermute(first, hier, backward)  5.3 us
    ppermute x1, starting transfers between devices, on_device(): below = lax.ppermute(last, hier, onward)  4 us
    pallas_call x1, Pallas kernels, on_device(): back_sent = column_call(ints, reals, own, below, above, vhi, vlo)  2.94 us
    ppermute x1, starting transfers between devices, on_device(): p1 = lax.ppermute(x, hier, near)  2.43 us
  transfers between devices with their start and end apart: 7, of which 4 were waited for; matrix products, arithmetic and copies ran while one was open for 1% of the time, Pallas kernels for 5%

profile of v6, /device:TPU:28, one launch (start us, length us, event | category | flops | bytes accessed | tf_op | source)
XLA Modules:
  0.0 73.2 jit_solution(5953217115894458280)
XLA Ops:
  0.0 1.7 %own.1 = f32[32,8,128]{2,1,0:T(8,128)} custom-call(f32[128,256]{1,0:T(8,128)} %bitcast.x_ref), custom_call_target="tpu_custom_call" | custom-call | flops 1000000 | bytes 4000000 | tf_op jit(solution)/shard_map/own/pallas_call | solution.py:469
  1.7 2.4 %collective-permute-start = (f32[4,2,16,256]{3,2,1,0:T(8,128)}, f32[4,2,16,256]{3,2,1,0:T(8,128)S(1)}, u32[]{:S(2)}, u32[]{:S(2)}) collective-permute-start(f32[4,2,16,256]{3,2,1,0:T(8,128)} %x_ref.1), channel_id=1, source_target_pairs={{16,32},{48,64},{80,96},{112,128},{144,160},{176,192},{208,224},{2... | collective-permute-start | bytes 393224 | tf_op jit(solution)/shard_map/ppermute | solution.py:471
  4.2 6.8 %collective-permute-start.1 = (f32[4,2,16,256]{3,2,1,0:T(8,128)}, f32[4,2,16,256]{3,2,1,0:T(8,128)S(1)}, u32[]{:S(2)}, u32[]{:S(2)}) collective-permute-start(f32[4,2,16,256]{3,2,1,0:T(8,128)} %x_ref.1), channel_id=1, source_target_pairs={{0,32},{32,64},{64,96},{96,128},{128,160},{160,192},{192,224},{224... | collective-permute-start | bytes 393224 | tf_op jit(solution)/shard_map/ppermute | solution.py:472
  10.9 11.9 %all-to-all-start = ((f32[32,8,128]{2,1,0:T(8,128)}), f32[32,8,128]{2,1,0:T(8,128)S(1)}, u32[]{:S(2)}, u32[]{:S(2)}) async-start(f32[32,8,128]{2,1,0:T(8,128)} %own.1), calls=%async_computation | async-start | bytes 262144 | tf_op jit(solution)/shard_map/all_to_all | solution.py:464
  22.9 0.6 copy-done.2
  23.6 0.2 select_reduce_fusion
  23.8 0.7 copy-done.4
  24.5 0.1 reshape.55
  24.6 0.9 %copy-done.1 = f32[256,256]{1,0:T(8,128)S(1)} copy-done((f32[256,256]{1,0:T(8,128)S(1)}, f32[256,256]{1,0:T(8,128)}, u32[]{:S(2)}) %copy-start.1) | copy-done | bytes 262168
  25.5 0.1 weights.1
  25.7 6.5 %all-to-all-done.got_ref = f32[32,8,128]{2,1,0:T(8,128)S(1)} async-done(((f32[32,8,128]{2,1,0:T(8,128)}), f32[32,8,128]{2,1,0:T(8,128)S(1)}, u32[]{:S(2)}, u32[]{:S(2)}) %all-to-all-start) | async-done | bytes 131104 | tf_op jit(solution)/shard_map/all_to_all | solution.py:464
  32.1 0.7 edge.1
  32.9 4.0 %collective-permute-start.2 = (f32[4,2,8,256]{3,2,1,0:T(8,128)S(1)}, f32[4,2,8,256]{3,2,1,0:T(8,128)S(1)}, u32[]{:S(2)}, u32[]{:S(2)}) collective-permute-start(f32[4,2,8,256]{3,2,1,0:T(8,128)S(1)} %get-tuple-element.29), channel_id=1, source_target_pairs={{0,48},{16,32},{32,80},{48,64},{64,112},{80,96},{96,144},{112,128}... | collective-permute-start | bytes 196616 | tf_op jit(solution)/shard_map/ppermute | solution.py:474
  36.9 1.9 %collective-permute-start.3 = (f32[4,2,8,256]{3,2,1,0:T(8,128)S(1)}, f32[4,2,8,256]{3,2,1,0:T(8,128)S(1)}, u32[]{:S(2)}, u32[]{:S(2)}) collective-permute-start(f32[4,2,8,256]{3,2,1,0:T(8,128)S(1)} %get-tuple-element.30), channel_id=1, source_target_pairs={{48,0},{32,16},{80,32},{64,48},{112,64},{96,80},{144,96},{128,112}... | collective-permute-start | bytes 196616 | tf_op jit(solution)/shard_map/ppermute | solution.py:475
  38.8 0.1 pad_maximum_fusion.reals_in.reals_ref
  38.9 0.9 %pair.1 = f32[6,2,16,256]{3,2,1,0:T(8,128)S(1)} custom-call(s32[16]{0:T(128)S(1)} %fusion.3.ints_in.ints_ref, f32[4,2,16,256]{3,2,1,0:T(8,128)} %x_ref.1, f32[4,2,16,256]{3,2,1,0:T(8,128)S(1)} %collective-permute-done.near_ref.p1_ref), custom_call_target="tpu_custom_call" | custom-call | flops 1000000 | bytes 4000000 | tf_op jit(solution)/shard_map/pair/pallas_call | solution.py:477
  39.8 5.3 %collective-permute-done.3.above_ref = f32[4,2,8,256]{3,2,1,0:T(8,128)S(1)} collective-permute-done((f32[4,2,8,256]{3,2,1,0:T(8,128)S(1)}, f32[4,2,8,256]{3,2,1,0:T(8,128)S(1)}, u32[]{:S(2)}, u32[]{:S(2)}) %collective-permute-start.3) | collective-permute-done | bytes 65568 | tf_op jit(solution)/shard_map/ppermute | solution.py:475
  45.1 2.9 %columns.1 = f32[32,32,128]{2,1,0:T(8,128)} custom-call(s32[16]{0:T(128)S(1)} %fusion.3.ints_in.ints_ref, f32[78]{0:T(128)S(1)} %pad_maximum_fusion.reals_in.reals_ref, f32[8,2,8,256]{3,2,1,0:T(8,128)S(1)} %get-tuple-element.28.own_ref, f32[4,2,8,256]{3,2,1,0:T(8,128)S(1)} %collective-permute-done.2.below_ref, ...), custom_call_target="tpu_custom_call" | custom-call | flops 1000000000 | bytes 4000000 | tf_op jit(solution)/shard_map/columns/pallas_call | solution.py:479
  48.1 6.0 %all-to-all-start.1 = ((f32[32,32,128]{2,1,0:T(8,128)}), f32[32,32,128]{2,1,0:T(8,128)S(1)}, u32[]{:S(2)}, u32[]{:S(2)}) async-start(f32[32,32,128]{2,1,0:T(8,128)} %columns.1), calls=%async_computation.1 | async-start | bytes 1048576 | tf_op jit(solution)/shard_map/all_to_all | solution.py:464
  54.1 2.3 %collective-permute-start.4 = (f32[6,2,16,256]{3,2,1,0:T(8,128)S(1)}, f32[6,2,16,256]{3,2,1,0:T(8,128)S(1)}, u32[]{:S(2)}, u32[]{:S(2)}) collective-permute-start(f32[6,2,16,256]{3,2,1,0:T(8,128)S(1)} %pair.1), channel_id=1, source_target_pairs={{0,16},{32,48},{64,80},{96,112},{128,144},{160,176},{192,208},{224... | collective-permute-start | bytes 589832 | tf_op jit(solution)/shard_map/ppermute | solution.py:482
  56.4 9.7 %collective-permute-done.4.pair_ref = f32[6,2,16,256]{3,2,1,0:T(8,128)S(1)} collective-permute-done((f32[6,2,16,256]{3,2,1,0:T(8,128)S(1)}, f32[6,2,16,256]{3,2,1,0:T(8,128)S(1)}, u32[]{:S(2)}, u32[]{:S(2)}) %collective-permute-start.4) | collective-permute-done | bytes 196640 | tf_op jit(solution)/shard_map/ppermute | solution.py:482
  66.0 2.1 %rows.1.base_ref = f32[128,256]{1,0:T(8,128)S(1)} custom-call(s32[16]{0:T(128)S(1)} %fusion.3.ints_in.ints_ref, f32[78]{0:T(128)S(1)} %pad_maximum_fusion.reals_in.reals_ref, f32[4,2,16,256]{3,2,1,0:T(8,128)} %x_ref.1, f32[4,2,16,256]{3,2,1,0:T(8,128)S(1)} %collective-permute-done.near_ref.p1_ref, f32[4,2,16,256]{3,2,1,0:T(8,128)S(1)} %collective-permute-done.1.p2_ref, ...), custom_call_target="tpu_custom_call" | custom-call | flops 1000000000 | bytes 4000000 | tf_op jit(solution)/shard_map/rows/pallas_call | solution.py:483
  68.1 3.8 %all-to-all-done.1.got_ref = f32[32,32,128]{2,1,0:T(8,128)S(1)} async-done(((f32[32,32,128]{2,1,0:T(8,128)}), f32[32,32,128]{2,1,0:T(8,128)S(1)}, u32[]{:S(2)}, u32[]{:S(2)}) %all-to-all-start.1) | async-done | bytes 524320 | tf_op jit(solution)/shard_map/all_to_all | solution.py:464
  71.9 1.3 %finish.1 = f32[128,256]{1,0:T(8,128)} custom-call(s32[16]{0:T(128)S(1)} %fusion.3.ints_in.ints_ref, f32[32,32,128]{2,1,0:T(8,128)S(1)} %all-to-all-done.1.got_ref, f32[128,256]{1,0:T(8,128)S(1)} %rows.1.base_ref, bf16[256,768]{1,0:T(8,128)(2,1)S(1)} %get-tuple-element.37.ghi_ref, bf16[256,768]{1,0:T(8,128)(2,1)S(1)} %get-tuple-element.38.glo_ref), custom_call_target="tpu_custom_call" | custom-call | flops 300000000 | bytes 4000000 | tf_op jit(solution)/shard_map/finish/pallas_call | solution.py:484
  (16 shorter events, 0.1 us)
Async XLA Ops:
  0.0 24.6 %copy-start = (f32[2,256,256]{2,1,0:T(8,128)S(1)}, f32[2,256,256]{2,1,0:T(8,128)}, u32[]{:S(2)}) copy-start(f32[2,256,256]{2,1,0:T(8,128)} %q_ref.1) | copy-start | bytes 1572868
  1.7 37.2 %collective-permute-start = (f32[4,2,16,256]{3,2,1,0:T(8,128)}, f32[4,2,16,256]{3,2,1,0:T(8,128)S(1)}, u32[]{:S(2)}, u32[]{:S(2)}) collective-permute-start(f32[4,2,16,256]{3,2,1,0:T(8,128)} %x_ref.1), channel_id=1, source_target_pairs={{16,32},{48,64},{80,96},{112,128},{144,160},{176,192},{208,224},{2... | collective-permute-start | bytes 393224 | tf_op jit(solution)/shard_map/ppermute | solution.py:471
  4.2 34.7 %collective-permute-start.1 = (f32[4,2,16,256]{3,2,1,0:T(8,128)}, f32[4,2,16,256]{3,2,1,0:T(8,128)S(1)}, u32[]{:S(2)}, u32[]{:S(2)}) collective-permute-start(f32[4,2,16,256]{3,2,1,0:T(8,128)} %x_ref.1), channel_id=1, source_target_pairs={{0,32},{32,64},{64,96},{96,128},{128,160},{160,192},{192,224},{224... | collective-permute-start | bytes 393224 | tf_op jit(solution)/shard_map/ppermute | solution.py:472
  10.9 21.2 %all-to-all-start = ((f32[32,8,128]{2,1,0:T(8,128)}), f32[32,8,128]{2,1,0:T(8,128)S(1)}, u32[]{:S(2)}, u32[]{:S(2)}) async-start(f32[32,8,128]{2,1,0:T(8,128)} %own.1), calls=%async_computation | async-start | bytes 262144 | tf_op jit(solution)/shard_map/all_to_all | solution.py:464
  22.9 0.7 copy-start.2
  23.8 0.7 copy-start.4
  24.6 1.0 %copy-start.1 = (f32[256,256]{1,0:T(8,128)S(1)}, f32[256,256]{1,0:T(8,128)}, u32[]{:S(2)}) copy-start(f32[256,256]{1,0:T(8,128)} %h_ref.1) | copy-start | bytes 786436
  32.8 6.0 %copy-start.3 = (f32[2]{0:T(128)S(1)}, f32[2]{0:T(128)}, u32[]{:S(2)}) copy-start(f32[2]{0:T(128)} %param.9) | copy-start | bytes 28
  32.9 7.0 %collective-permute-start.2 = (f32[4,2,8,256]{3,2,1,0:T(8,128)S(1)}, f32[4,2,8,256]{3,2,1,0:T(8,128)S(1)}, u32[]{:S(2)}, u32[]{:S(2)}) collective-permute-start(f32[4,2,8,256]{3,2,1,0:T(8,128)S(1)} %get-tuple-element.29), channel_id=1, source_target_pairs={{0,48},{16,32},{32,80},{48,64},{64,112},{80,96},{96,144},{112,128}... | collective-permute-start | bytes 196616 | tf_op jit(solution)/shard_map/ppermute | solution.py:474
  36.9 8.3 %collective-permute-start.3 = (f32[4,2,8,256]{3,2,1,0:T(8,128)S(1)}, f32[4,2,8,256]{3,2,1,0:T(8,128)S(1)}, u32[]{:S(2)}, u32[]{:S(2)}) collective-permute-start(f32[4,2,8,256]{3,2,1,0:T(8,128)S(1)} %get-tuple-element.30), channel_id=1, source_target_pairs={{48,0},{32,16},{80,32},{64,48},{112,64},{96,80},{144,96},{128,112}... | collective-permute-start | bytes 196616 | tf_op jit(solution)/shard_map/ppermute | solution.py:475
  48.1 23.8 %all-to-all-start.1 = ((f32[32,32,128]{2,1,0:T(8,128)}), f32[32,32,128]{2,1,0:T(8,128)S(1)}, u32[]{:S(2)}, u32[]{:S(2)}) async-start(f32[32,32,128]{2,1,0:T(8,128)} %columns.1), calls=%async_computation.1 | async-start | bytes 1048576 | tf_op jit(solution)/shard_map/all_to_all | solution.py:464
  54.1 11.9 %collective-permute-start.4 = (f32[6,2,16,256]{3,2,1,0:T(8,128)S(1)}, f32[6,2,16,256]{3,2,1,0:T(8,128)S(1)}, u32[]{:S(2)}, u32[]{:S(2)}) collective-permute-start(f32[6,2,16,256]{3,2,1,0:T(8,128)S(1)} %pair.1), channel_id=1, source_target_pairs={{0,16},{32,48},{64,80},{96,112},{128,144},{160,176},{192,208},{224... | collective-permute-start | bytes 589832 | tf_op jit(solution)/shard_map/ppermute | solution.py:482

commit v7 on v6

--- a/solution.py
+++ b/solution.py
@@ -191,7 +191,8 @@
         last_ref[j] = own_ref[own + other - 4 + j]
 
 
-def pair_kernel(ints_ref, x_ref, near_ref, o_ref):
+def pair_kernel(ints_ref, x_ref, near_ref, o_ref, far_ref):
+    far_ref[...] = x_ref[pl.ds(jnp.where(ints_ref[SIDE] == 0, ints_ref[COUNTS + 2] - 2, 0), 2)]
     o_ref[0:4] = x_ref[...]
     o_ref[4:6] = near_ref[pl.ds(jnp.where(ints_ref[SIDE] == 0, ints_ref[COUNTS + 1] - 2, 0), 2)]
 
@@ -277,7 +278,7 @@
     farther, below, own, above = (ints_ref[COUNTS + i] for i in range(4))
     w_ref[8:12] = x_ref[...]
     w_ref[pl.ds(4 + 8 * up, 4)] = p1_ref[...]
-    w_ref[pl.ds(16 * up, 4)] = p2_ref[...]
+    w_ref[pl.ds(jnp.where(up == 0, farther - 2, 16), 2)] = p2_ref[...]
     w_ref[pl.ds(12 - 8 * up, 4)] = pair_ref[0:4]
     w_ref[pl.ds(jnp.where(up == 0, 16, farther - 2), 2)] = pair_ref[4:6]
 
@@ -379,7 +380,7 @@
     [pltpu.VMEM((8, 2, 8, 256), F32), INTS, pltpu.SemaphoreType.DMA((1,))],
     name="edge",
 )
-pair_call = call(pair_kernel, struct((6, 2, 16, 256)), [SMEM] + [VMEM] * 2, name="pair")
+pair_call = call(pair_kernel, (struct((6, 2, 16, 256)), struct((2, 2, 16, 256))), [SMEM] + [VMEM] * 2, name="pair")
 column_call = call(
     column_kernel,
     struct((32, 32, 128)),
@@ -469,16 +470,16 @@
     sent, x = lax.optimization_barrier((own_call(densities.reshape(128, 256)), densities))
     got = exchange(sent)
     p1 = lax.ppermute(x, hier, near)
-    p2 = lax.ppermute(x, hier, far)
     own, first, last = edge_call(ints, got)
     below = lax.ppermute(last, hier, onward)
     above = lax.ppermute(first, hier, backward)
-    own, p1, p2, x = lax.optimization_barrier((own, p1, p2, x))
-    pair = pair_call(ints, x, p1)
-    own, pair = lax.optimization_barrier((own, pair))
+    own, p1, x = lax.optimization_barrier((own, p1, x))
+    pair, edge = pair_call(ints, x, p1)
+    own, pair, edge = lax.optimization_barrier((own, pair, edge))
     back_sent = column_call(ints, reals, own, below, above, vhi, vlo)
-    back_sent, pair = lax.optimization_barrier((back_sent, pair))
+    back_sent, pair, edge = lax.optimization_barrier((back_sent, pair, edge))
     back_got = exchange(back_sent)
+    p2 = lax.ppermute(edge, hier, far)
     pair = lax.ppermute(pair, hier, inner)
     base = row_call(ints, reals, x, p1, p2, pair, vhi, vlo)
     out = finish_call(ints, back_got, base, hhi, hlo)

time: 73.7 us -> 65.7 us (0.89)
  waiting for transfers between devices: 25.2 us -> 21.3 us
  starting transfers between devices: 35.3 us -> 31.9 us
  Pallas kernels: 9.82 us -> 8.11 us
  local copies, waits for them, and re-layouts: 2.36 us -> 3.33 us
    ppermute x1, waiting for transfers between devices: 9.67 us -> 1.07 us  [on_device(): pair = lax.ppermute(pair, hier, inner)]
    ppermute x1, waiting for transfers between devices: 0.01 us -> 8.09 us  [on_device(): p2 = lax.ppermute(edge, hier, far)]
    ppermute x1, starting transfers between devices: 6.75 us -> 2.2 us  [on_device(): p2 = lax.ppermute(edge, hier, far)]
    all_to_all x2, waiting for transfers between devices: 10.2 us -> 6.49 us  [exchange(): lax.all_to_all(v, everyone, 0, 0, axis_index_groups=lists, tiled=True)]
    unnamed x10 -> x14, local copies, waits for them, and re-layouts: 2.27 us -> 3.24 us
    pallas_call x1, Pallas kernels: 1.72 us -> 0.75 us  [on_device(): own_call(densities.reshape(128, 256))]
  transfers between devices with their start and end apart: 7 -> 7, of which waited for: 4 -> 5; matrix products, arithmetic and copies ran while one was open for 1% -> 1% of each run, Pallas kernels for 5% -> 5%
where the time goes in v7:
time: 65.7 us; the launch traced here: 65.2 us
  starting transfers between devices  31.9 us (49%)
  waiting for transfers between devices  21.3 us (32%)
  Pallas kernels  8.11 us (12%)
  local copies, waits for them, and re-layouts  3.33 us (5%)
    all_to_all x2, starting transfers between devices, exchange(): lax.all_to_all(v, everyone, 0, 0, axis_index_groups=lists, tiled=True)  18.6 us
    ppermute x1, waiting for transfers between devices, on_device(): p2 = lax.ppermute(edge, hier, far)  8.09 us
    all_to_all x2, waiting for transfers between devices, exchange(): lax.all_to_all(v, everyone, 0, 0, axis_index_groups=lists, tiled=True)  6.49 us
    ppermute x1, waiting for transfers between devices, on_device(): above = lax.ppermute(first, hier, backward)  5.67 us
    ppermute x1, starting transfers between devices, on_device(): below = lax.ppermute(last, hier, onward)  4.67 us
    unnamed x14, local copies, waits for them, and re-layouts  3.24 us
    pallas_call x1, Pallas kernels, on_device(): back_sent = column_call(ints, reals, own, below, above, vhi, vlo)  2.93 us
    ppermute x1, starting transfers between devices, on_device(): p1 = lax.ppermute(x, hier, near)  2.44 us
  transfers between devices with their start and end apart: 7, of which 5 were waited for; matrix products, arithmetic and copies ran while one was open for 1% of the time, Pallas kernels for 5%

profile of v7, /device:TPU:28, one launch (start us, length us, event | category | flops | bytes accessed | tf_op | source)
XLA Modules:
  0.0 65.2 jit_solution(11175405567134809357)
XLA Ops:
  0.0 1.0 %copy-done.1 = f32[4,2,16,256]{3,2,1,0:T(8,128)S(1)} copy-done((f32[4,2,16,256]{3,2,1,0:T(8,128)S(1)}, f32[4,2,16,256]{3,2,1,0:T(8,128)}, u32[]{:S(2)}) %copy-start.1) | copy-done | bytes 131096
  1.0 0.8 %own.1 = f32[32,8,128]{2,1,0:T(8,128)} custom-call(f32[128,256]{1,0:T(8,128)S(1)} %bitcast.2), custom_call_target="tpu_custom_call" | custom-call | flops 1000000 | bytes 4000000 | tf_op jit(solution)/shard_map/own/pallas_call | solution.py:470
  1.7 11.9 %all-to-all-start = ((f32[32,8,128]{2,1,0:T(8,128)}), f32[32,8,128]{2,1,0:T(8,128)S(1)}, u32[]{:S(2)}, u32[]{:S(2)}) async-start(f32[32,8,128]{2,1,0:T(8,128)} %own.1), calls=%async_computation | async-start | bytes 262144 | tf_op jit(solution)/shard_map/all_to_all | solution.py:465
  13.7 2.4 %collective-permute-start = (f32[4,2,16,256]{3,2,1,0:T(8,128)}, f32[4,2,16,256]{3,2,1,0:T(8,128)S(1)}, u32[]{:S(2)}, u32[]{:S(2)}) collective-permute-start(f32[4,2,16,256]{3,2,1,0:T(8,128)} %x_ref.1), channel_id=1, source_target_pairs={{16,32},{48,64},{80,96},{112,128},{144,160},{176,192},{208,224},{2... | collective-permute-start | bytes 393224 | tf_op jit(solution)/shard_map/ppermute | solution.py:472
  16.2 0.6 copy-done.4
  16.8 0.2 select_reduce_fusion
  17.1 0.7 %copy-done.6 = f32[2,2]{1,0:T(2,128)S(1)} copy-done((f32[2,2]{1,0:T(2,128)S(1)}, f32[2,2]{1,0:T(2,128)}, u32[]{:S(2)}) %copy-start.6) | copy-done | bytes 40
  17.8 0.9 %copy-done.3 = f32[256,256]{1,0:T(8,128)S(1)} copy-done((f32[256,256]{1,0:T(8,128)S(1)}, f32[256,256]{1,0:T(8,128)}, u32[]{:S(2)}) %copy-start.3) | copy-done | bytes 262168
  18.8 0.1 weights.1
  18.9 4.0 %all-to-all-done.got_ref = f32[32,8,128]{2,1,0:T(8,128)S(1)} async-done(((f32[32,8,128]{2,1,0:T(8,128)}), f32[32,8,128]{2,1,0:T(8,128)S(1)}, u32[]{:S(2)}, u32[]{:S(2)}) %all-to-all-start) | async-done | bytes 131104 | tf_op jit(solution)/shard_map/all_to_all | solution.py:465
  22.9 0.7 %edge.1 = (f32[8,2,8,256]{3,2,1,0:T(8,128)S(1)}, f32[4,2,8,256]{3,2,1,0:T(8,128)S(1)}, f32[4,2,8,256]{3,2,1,0:T(8,128)S(1)}) custom-call(s32[16]{0:T(128)S(1)} %fusion.3.ints_in.ints_ref, f32[32,8,128]{2,1,0:T(8,128)S(1)} %all-to-all-done.got_ref), custom_call_target="tpu_custom_call" | custom-call | flops 1000000 | bytes 4000000 | tf_op jit(solution)/shard_map/edge/pallas_call | solution.py:473
  23.6 4.7 %collective-permute-start.1 = (f32[4,2,8,256]{3,2,1,0:T(8,128)S(1)}, f32[4,2,8,256]{3,2,1,0:T(8,128)S(1)}, u32[]{:S(2)}, u32[]{:S(2)}) collective-permute-start(f32[4,2,8,256]{3,2,1,0:T(8,128)S(1)} %get-tuple-element.34), channel_id=1, source_target_pairs={{0,48},{16,32},{32,80},{48,64},{64,112},{80,96},{96,144},{112,128}... | collective-permute-start | bytes 196616 | tf_op jit(solution)/shard_map/ppermute | solution.py:474
  28.3 1.9 %collective-permute-start.2 = (f32[4,2,8,256]{3,2,1,0:T(8,128)S(1)}, f32[4,2,8,256]{3,2,1,0:T(8,128)S(1)}, u32[]{:S(2)}, u32[]{:S(2)}) collective-permute-start(f32[4,2,8,256]{3,2,1,0:T(8,128)S(1)} %get-tuple-element.35), channel_id=1, source_target_pairs={{48,0},{32,16},{80,32},{64,48},{112,64},{96,80},{144,96},{128,112}... | collective-permute-start | bytes 196616 | tf_op jit(solution)/shard_map/ppermute | solution.py:475
  30.3 0.6 pair.1
  30.9 5.7 %collective-permute-done.2.above_ref = f32[4,2,8,256]{3,2,1,0:T(8,128)S(1)} collective-permute-done((f32[4,2,8,256]{3,2,1,0:T(8,128)S(1)}, f32[4,2,8,256]{3,2,1,0:T(8,128)S(1)}, u32[]{:S(2)}, u32[]{:S(2)}) %collective-permute-start.2) | collective-permute-done | bytes 65568 | tf_op jit(solution)/shard_map/ppermute | solution.py:475
  36.6 2.9 %columns.1 = f32[32,32,128]{2,1,0:T(8,128)} custom-call(s32[16]{0:T(128)S(1)} %fusion.3.ints_in.ints_ref, f32[78]{0:T(128)S(1)} %pad_maximum_fusion.reals_in.reals_ref, f32[8,2,8,256]{3,2,1,0:T(8,128)S(1)} %get-tuple-element.33.own_ref, f32[4,2,8,256]{3,2,1,0:T(8,128)S(1)} %collective-permute-done.1.below_ref, ...), custom_call_target="tpu_custom_call" | custom-call | flops 1000000000 | bytes 4000000 | tf_op jit(solution)/shard_map/columns/pallas_call | solution.py:479
  39.5 6.6 %all-to-all-start.1 = ((f32[32,32,128]{2,1,0:T(8,128)}), f32[32,32,128]{2,1,0:T(8,128)S(1)}, u32[]{:S(2)}, u32[]{:S(2)}) async-start(f32[32,32,128]{2,1,0:T(8,128)} %columns.1), calls=%async_computation.1 | async-start | bytes 1048576 | tf_op jit(solution)/shard_map/all_to_all | solution.py:465
  46.2 2.1 %collective-permute-start.4 = (f32[6,2,16,256]{3,2,1,0:T(8,128)S(1)}, f32[6,2,16,256]{3,2,1,0:T(8,128)S(1)}, u32[]{:S(2)}, u32[]{:S(2)}) collective-permute-start(f32[6,2,16,256]{3,2,1,0:T(8,128)S(1)} %get-tuple-element.42), channel_id=1, source_target_pairs={{0,16},{32,48},{64,80},{96,112},{128,144},{160,176},{192,208},{224... | collective-permute-start | bytes 589832 | tf_op jit(solution)/shard_map/ppermute | solution.py:483
  48.3 2.2 %collective-permute-start.3 = (f32[2,2,16,256]{3,2,1,0:T(8,128)S(1)}, f32[2,2,16,256]{3,2,1,0:T(8,128)S(1)}, u32[]{:S(2)}, u32[]{:S(2)}) collective-permute-start(f32[2,2,16,256]{3,2,1,0:T(8,128)S(1)} %get-tuple-element.41), channel_id=1, source_target_pairs={{0,32},{32,64},{64,96},{96,128},{128,160},{160,192},{192,224},{224... | collective-permute-start | bytes 196616 | tf_op jit(solution)/shard_map/ppermute | solution.py:482
  50.5 8.1 %collective-permute-done.3.p2_ref = f32[2,2,16,256]{3,2,1,0:T(8,128)S(1)} collective-permute-done((f32[2,2,16,256]{3,2,1,0:T(8,128)S(1)}, f32[2,2,16,256]{3,2,1,0:T(8,128)S(1)}, u32[]{:S(2)}, u32[]{:S(2)}) %collective-permute-start.3) | collective-permute-done | bytes 65568 | tf_op jit(solution)/shard_map/ppermute | solution.py:482
  58.6 1.1 %collective-permute-done.4.pair_ref = f32[6,2,16,256]{3,2,1,0:T(8,128)S(1)} collective-permute-done((f32[6,2,16,256]{3,2,1,0:T(8,128)S(1)}, f32[6,2,16,256]{3,2,1,0:T(8,128)S(1)}, u32[]{:S(2)}, u32[]{:S(2)}) %collective-permute-start.4) | collective-permute-done | bytes 196640 | tf_op jit(solution)/shard_map/ppermute | solution.py:483
  59.7 1.7 %rows.1.base_ref = f32[128,256]{1,0:T(8,128)S(1)} custom-call(s32[16]{0:T(128)S(1)} %fusion.3.ints_in.ints_ref, f32[78]{0:T(128)S(1)} %pad_maximum_fusion.reals_in.reals_ref, f32[4,2,16,256]{3,2,1,0:T(8,128)S(1)} %copy-done.2, f32[4,2,16,256]{3,2,1,0:T(8,128)S(1)} %collective-permute-done.near_ref.p1_ref, ...), custom_call_target="tpu_custom_call" | custom-call | flops 1000000000 | bytes 4000000 | tf_op jit(solution)/shard_map/rows/pallas_call | solution.py:484
  61.4 2.5 %all-to-all-done.1.got_ref = f32[32,32,128]{2,1,0:T(8,128)S(1)} async-done(((f32[32,32,128]{2,1,0:T(8,128)}), f32[32,32,128]{2,1,0:T(8,128)S(1)}, u32[]{:S(2)}, u32[]{:S(2)}) %all-to-all-start.1) | async-done | bytes 524320 | tf_op jit(solution)/shard_map/all_to_all | solution.py:465
  63.9 1.3 %finish.1 = f32[128,256]{1,0:T(8,128)} custom-call(s32[16]{0:T(128)S(1)} %fusion.3.ints_in.ints_ref, f32[32,32,128]{2,1,0:T(8,128)S(1)} %all-to-all-done.1.got_ref, f32[128,256]{1,0:T(8,128)S(1)} %rows.1.base_ref, bf16[256,768]{1,0:T(8,128)(2,1)S(1)} %get-tuple-element.43.ghi_ref, bf16[256,768]{1,0:T(8,128)(2,1)S(1)} %get-tuple-element.44.glo_ref), custom_call_target="tpu_custom_call" | custom-call | flops 300000000 | bytes 4000000 | tf_op jit(solution)/shard_map/finish/pallas_call | solution.py:485
  (20 shorter events, 0.2 us)
Async XLA Ops:
  0.0 17.8 %copy-start = (f32[2,256,256]{2,1,0:T(8,128)S(1)}, f32[2,256,256]{2,1,0:T(8,128)}, u32[]{:S(2)}) copy-start(f32[2,256,256]{2,1,0:T(8,128)} %q_ref.1) | copy-start | bytes 1572868
  0.0 1.0 %copy-start.1 = (f32[4,2,16,256]{3,2,1,0:T(8,128)S(1)}, f32[4,2,16,256]{3,2,1,0:T(8,128)}, u32[]{:S(2)}) copy-start(f32[4,2,16,256]{3,2,1,0:T(8,128)} %x_ref.1) | copy-start | bytes 393220
  1.7 21.2 %all-to-all-start = ((f32[32,8,128]{2,1,0:T(8,128)}), f32[32,8,128]{2,1,0:T(8,128)S(1)}, u32[]{:S(2)}, u32[]{:S(2)}) async-start(f32[32,8,128]{2,1,0:T(8,128)} %own.1), calls=%async_computation | async-start | bytes 262144 | tf_op jit(solution)/shard_map/all_to_all | solution.py:465
  13.7 16.7 %collective-permute-start = (f32[4,2,16,256]{3,2,1,0:T(8,128)}, f32[4,2,16,256]{3,2,1,0:T(8,128)S(1)}, u32[]{:S(2)}, u32[]{:S(2)}) collective-permute-start(f32[4,2,16,256]{3,2,1,0:T(8,128)} %x_ref.1), channel_id=1, source_target_pairs={{16,32},{48,64},{80,96},{112,128},{144,160},{176,192},{208,224},{2... | collective-permute-start | bytes 393224 | tf_op jit(solution)/shard_map/ppermute | solution.py:472
  16.2 0.7 %copy-start.4 = (s32[32]{0:T(128)S(1)}, s32[32]{0:T(128)}, u32[]{:S(2)}) copy-start(s32[32]{0:T(128)} %param.11) | copy-start | bytes 388
  17.0 0.7 %copy-start.6 = (f32[2,2]{1,0:T(2,128)S(1)}, f32[2,2]{1,0:T(2,128)}, u32[]{:S(2)}) copy-start(f32[2,2]{1,0:T(2,128)} %param.10) | copy-start | bytes 52
  17.8 1.0 %copy-start.3 = (f32[256,256]{1,0:T(8,128)S(1)}, f32[256,256]{1,0:T(8,128)}, u32[]{:S(2)}) copy-start(f32[256,256]{1,0:T(8,128)} %h_ref.1) | copy-start | bytes 786436
  18.9 11.4 %copy-start.2 = (f32[4,2,16,256]{3,2,1,0:T(8,128)S(1)}, f32[4,2,16,256]{3,2,1,0:T(8,128)}, u32[]{:S(2)}) copy-start(f32[4,2,16,256]{3,2,1,0:T(8,128)} %x_ref.1) | copy-start | bytes 393220
  23.6 6.6 %copy-start.5 = (f32[2]{0:T(128)S(1)}, f32[2]{0:T(128)}, u32[]{:S(2)}) copy-start(f32[2]{0:T(128)} %param.9) | copy-start | bytes 28
  23.6 7.3 %collective-permute-start.1 = (f32[4,2,8,256]{3,2,1,0:T(8,128)S(1)}, f32[4,2,8,256]{3,2,1,0:T(8,128)S(1)}, u32[]{:S(2)}, u32[]{:S(2)}) collective-permute-start(f32[4,2,8,256]{3,2,1,0:T(8,128)S(1)} %get-tuple-element.34), channel_id=1, source_target_pairs={{0,48},{16,32},{32,80},{48,64},{64,112},{80,96},{96,144},{112,128}... | collective-permute-start | bytes 196616 | tf_op jit(solution)/shard_map/ppermute | solution.py:474
  28.3 8.3 %collective-permute-start.2 = (f32[4,2,8,256]{3,2,1,0:T(8,128)S(1)}, f32[4,2,8,256]{3,2,1,0:T(8,128)S(1)}, u32[]{:S(2)}, u32[]{:S(2)}) collective-permute-start(f32[4,2,8,256]{3,2,1,0:T(8,128)S(1)} %get-tuple-element.35), channel_id=1, source_target_pairs={{48,0},{32,16},{80,32},{64,48},{112,64},{96,80},{144,96},{128,112}... | collective-permute-start | bytes 196616 | tf_op jit(solution)/shard_map/ppermute | solution.py:475
  39.5 24.3 %all-to-all-start.1 = ((f32[32,32,128]{2,1,0:T(8,128)}), f32[32,32,128]{2,1,0:T(8,128)S(1)}, u32[]{:S(2)}, u32[]{:S(2)}) async-start(f32[32,32,128]{2,1,0:T(8,128)} %columns.1), calls=%async_computation.1 | async-start | bytes 1048576 | tf_op jit(solution)/shard_map/all_to_all | solution.py:465
  46.2 13.5 %collective-permute-start.4 = (f32[6,2,16,256]{3,2,1,0:T(8,128)S(1)}, f32[6,2,16,256]{3,2,1,0:T(8,128)S(1)}, u32[]{:S(2)}, u32[]{:S(2)}) collective-permute-start(f32[6,2,16,256]{3,2,1,0:T(8,128)S(1)} %get-tuple-element.42), channel_id=1, source_target_pairs={{0,16},{32,48},{64,80},{96,112},{128,144},{160,176},{192,208},{224... | collective-permute-start | bytes 589832 | tf_op jit(solution)/shard_map/ppermute | solution.py:483
  48.3 10.3 %collective-permute-start.3 = (f32[2,2,16,256]{3,2,1,0:T(8,128)S(1)}, f32[2,2,16,256]{3,2,1,0:T(8,128)S(1)}, u32[]{:S(2)}, u32[]{:S(2)}) collective-permute-start(f32[2,2,16,256]{3,2,1,0:T(8,128)S(1)} %get-tuple-element.41), channel_id=1, source_target_pairs={{0,32},{32,64},{64,96},{96,128},{128,160},{160,192},{192,224},{224... | collective-permute-start | bytes 196616 | tf_op jit(solution)/shard_map/ppermute | solution.py:482

commit v8 on v7

--- a/solution.py
+++ b/solution.py
@@ -44,28 +44,25 @@
 
 
 class Nodes:
-    def __init__(self, ints_ref, reals_ref, begin):
+    def __init__(self, total, begin, reals, root):
         self.memo = {}
-        self.live = (ints_ref[TOTAL] >> 1) << 1
+        self.live = (total >> 1) << 1
         self.begin = begin
         self.base = begin - 4
-        self.reals = reals_ref
-        self.gamma = (reals_ref[0], reals_ref[1])
-        self.re = (reals_ref[2], reals_ref[4])
-        self.im = (reals_ref[3], reals_ref[5])
-
-    def root(self, n):
-        return self.reals[jnp.clip(n, 0, ROOTS - 1) + 6]
+        self.gamma = (reals[0], reals[1])
+        self.re = (reals[2], reals[4])
+        self.im = (reals[3], reals[5])
+        self.root = root
 
     @once
     def up(self, p):
         g = self.base + p
-        return jnp.where((g >= 0) & (g + 2 < self.live), self.root((g >> 1) + 1), 0.0)
+        return self.root((g >> 1) + 1) * jnp.where((g >= 0) & (g + 2 < self.live), 1.0, 0.0)
 
     @once
     def down(self, p):
         g = self.base + p
-        return jnp.where((g >= 2) & (g < self.live), self.root(g >> 1), 0.0)
+        return self.root(g >> 1) * jnp.where((g >= 2) & (g < self.live), 1.0, 0.0)
 
     @once
     def middle(self, p):
@@ -198,18 +195,22 @@
 
 
 def column_kernel(
-    ints_in, reals_in, own_ref, below_ref, above_ref, ghi_ref, glo_ref, o_ref, y_ref, hi_ref, lo_ref, hi2_ref, lo2_ref, z_ref, send_ref, ints_ref, reals_ref, sem, out_sem
+    wide_ref, reals_ref, own_ref, below_ref, above_ref, ghi_ref, glo_ref, o_ref, y_ref, hi_ref, lo_ref, hi2_ref, lo2_ref, z_ref, send_ref, out_sem
 ):
-    fetched = fetch([(ints_in, ints_ref), (reals_in, reals_ref)], sem)
+    total, begin, side, before, here, after, odd = (
+        wide_ref[i : i + 1, 0:1][0, 0] for i in (TOTAL, TEAM_BEGIN, SIDE, COUNTS + 1, COUNTS + 2, COUNTS + 3, ODD)
+    )
+    reals = [reals_ref[i : i + 1, 0:1][0, 0] for i in range(6)]
+    own, other = jnp.where(side == 0, here, before), jnp.where(side == 0, after, here)
+
+    def root(n):
+        return jnp.sqrt(jnp.full((8, 256), jnp.maximum(n, 0).astype(F32)))
+
+    nodes = Nodes(total, begin, reals, root)
+    re, im = nodes.re, nodes.im
     y_ref[0:4] = below_ref[...]
     y_ref[4:12] = own_ref[...]
     y_ref[12:16] = above_ref[...]
-    for copy in fetched:
-        copy.wait()
-    nodes = Nodes(ints_ref, reals_ref, ints_ref[TEAM_BEGIN])
-    own, other = team_counts(ints_ref)
-    odd = ints_ref[ODD]
-    re, im = nodes.re, nodes.im
     y_ref[pl.ds(4 + own + other, 4)] = above_ref[...]
     x = []
     for p in range(16):
@@ -272,7 +273,11 @@
 def row_kernel(
     ints_ref, reals_ref, x_ref, p1_ref, p2_ref, pair_ref, ghi_ref, glo_ref, o_ref, w_ref, hi_ref, lo_ref, hi2_ref, lo2_ref
 ):
-    nodes = Nodes(ints_ref, reals_ref, ints_ref[HERE_BEGIN])
+
+    def root(n):
+        return reals_ref[jnp.clip(n, 0, ROOTS - 1) + 6]
+
+    nodes = Nodes(ints_ref[TOTAL], ints_ref[HERE_BEGIN], [reals_ref[i] for i in range(6)], root)
     re, im = nodes.re, (-nodes.im[0], -nodes.im[1])
     up = ints_ref[SIDE]
     farther, below, own, above = (ints_ref[COUNTS + i] for i in range(4))
@@ -384,7 +389,7 @@
 column_call = call(
     column_kernel,
     struct((32, 32, 128)),
-    [ANY] * 2 + [VMEM] * 5,
+    [VMEM] * 7,
     [
         pltpu.VMEM((16, 2, 8, 256), F32),
         pltpu.VMEM((640, 768), BF),
@@ -393,9 +398,6 @@
         pltpu.VMEM((128, 768), BF),
         pltpu.VMEM((4, 8, 2, 8, 256), F32),
         pltpu.VMEM((4, 32, 8, 128), F32),
-        INTS,
-        pltpu.SMEM((6 + ROOTS,), F32),
-        pltpu.SemaphoreType.DMA((2,)),
         pltpu.SemaphoreType.DMA((4,)),
     ],
     flops=1_000_000_000,
@@ -466,17 +468,19 @@
 
     ints = integers(node_count)
     reals = jnp.concatenate([gamma, coeff.reshape(4), jnp.sqrt(jnp.arange(ROOTS, dtype=F32))])
-    vhi, vlo, hhi, hlo = weights_call(hamiltonian, couplings)
     sent, x = lax.optimization_barrier((own_call(densities.reshape(128, 256)), densities))
     got = exchange(sent)
     p1 = lax.ppermute(x, hier, near)
     own, first, last = edge_call(ints, got)
     below = lax.ppermute(last, hier, onward)
     above = lax.ppermute(first, hier, backward)
-    own, p1, x = lax.optimization_barrier((own, p1, x))
+    own, p1, x, hamiltonian, couplings = lax.optimization_barrier((own, p1, x, hamiltonian, couplings))
+    vhi, vlo, hhi, hlo = weights_call(hamiltonian, couplings)
+    wide = jnp.broadcast_to(ints[:, None], (16, 128))
+    wide_reals = jnp.broadcast_to(reals[:8, None], (8, 128))
     pair, edge = pair_call(ints, x, p1)
     own, pair, edge = lax.optimization_barrier((own, pair, edge))
-    back_sent = column_call(ints, reals, own, below, above, vhi, vlo)
+    back_sent = column_call(wide, wide_reals, own, below, above, vhi, vlo)
     back_sent, pair, edge = lax.optimization_barrier((back_sent, pair, edge))
     back_got = exchange(back_sent)
     p2 = lax.ppermute(edge, hier, far)

time: 65.7 us -> 64.8 us (0.986)
  local copies, waits for them, and re-layouts: 3.33 us -> 1.22 us
  waiting for transfers between devices: 21.3 us -> 23.2 us
    all_to_all x2, waiting for transfers between devices: 6.49 us -> 8.77 us  [exchange(): lax.all_to_all(v, everyone, 0, 0, axis_index_groups=lists, tiled=True)]
    unnamed x14, local copies, waits for them, and re-layouts: 3.24 us -> 0.99 us
    ppermute x1, waiting for transfers between devices: 8.09 us -> 6.53 us  [on_device(): p2 = lax.ppermute(edge, hier, far)]
    ppermute x1, waiting for transfers between devices: 1.07 us -> 2.37 us  [on_device(): pair = lax.ppermute(pair, hier, inner)]
where the time goes in v8:
time: 64.8 us; the launch traced here: 64.4 us
  starting transfers between devices  31.9 us (49%)
  waiting for transfers between devices  23.2 us (36%)
  Pallas kernels  7.61 us (12%)
  local copies, waits for them, and re-layouts  1.22 us (2%)
    all_to_all x2, starting transfers between devices, exchange(): lax.all_to_all(v, everyone, 0, 0, axis_index_groups=lists, tiled=True)  18.1 us
    all_to_all x2, waiting for transfers between devices, exchange(): lax.all_to_all(v, everyone, 0, 0, axis_index_groups=lists, tiled=True)  8.77 us
    ppermute x1, waiting for transfers between devices, on_device(): p2 = lax.ppermute(edge, hier, far)  6.53 us
    ppermute x1, waiting for transfers between devices, on_device(): above = lax.ppermute(first, hier, backward)  5.49 us
    ppermute x1, starting transfers between devices, on_device(): below = lax.ppermute(last, hier, onward)  4.67 us
    ppermute x1, starting transfers between devices, on_device(): p1 = lax.ppermute(x, hier, near)  2.58 us
    pallas_call x1, Pallas kernels, on_device(): back_sent = column_call(wide, wide_reals, own, below, above, vhi, vlo)  2.43 us
    ppermute x1, starting transfers between devices, on_device(): p2 = lax.ppermute(edge, hier, far)  2.4 us
  transfers between devices with their start and end apart: 7, of which 5 were waited for; matrix products, arithmetic and copies ran while one was open for 1% of the time, Pallas kernels for 5%

profile of v8, /device:TPU:28, one launch (start us, length us, event | category | flops | bytes accessed | tf_op | source)
XLA Modules:
  0.0 64.4 jit_solution(6821561276816379132)
XLA Ops:
  0.0 1.0 %copy-done.1 = f32[4,2,16,256]{3,2,1,0:T(8,128)S(1)} copy-done((f32[4,2,16,256]{3,2,1,0:T(8,128)S(1)}, f32[4,2,16,256]{3,2,1,0:T(8,128)}, u32[]{:S(2)}) %copy-start.1) | copy-done | bytes 131096
  1.0 0.8 %own.1 = f32[32,8,128]{2,1,0:T(8,128)} custom-call(f32[128,256]{1,0:T(8,128)S(1)} %bitcast.3), custom_call_target="tpu_custom_call" | custom-call | flops 1000000 | bytes 4000000 | tf_op jit(solution)/shard_map/own/pallas_call | solution.py:471
  1.7 12.1 %all-to-all-start = ((f32[32,8,128]{2,1,0:T(8,128)}), f32[32,8,128]{2,1,0:T(8,128)S(1)}, u32[]{:S(2)}, u32[]{:S(2)}) async-start(f32[32,8,128]{2,1,0:T(8,128)} %own.1), calls=%async_computation | async-start | bytes 262144 | tf_op jit(solution)/shard_map/all_to_all | solution.py:467
  13.8 2.6 %collective-permute-start = (f32[4,2,16,256]{3,2,1,0:T(8,128)}, f32[4,2,16,256]{3,2,1,0:T(8,128)S(1)}, u32[]{:S(2)}, u32[]{:S(2)}) collective-permute-start(f32[4,2,16,256]{3,2,1,0:T(8,128)} %x_ref.1), channel_id=1, source_target_pairs={{16,32},{48,64},{80,96},{112,128},{144,160},{176,192},{208,224},{2... | collective-permute-start | bytes 393224 | tf_op jit(solution)/shard_map/ppermute | solution.py:473
  16.5 0.2 select_reduce_fusion
  16.7 0.1 reshape.68
  16.8 6.3 %all-to-all-done.got_ref = f32[32,8,128]{2,1,0:T(8,128)S(1)} async-done(((f32[32,8,128]{2,1,0:T(8,128)}), f32[32,8,128]{2,1,0:T(8,128)S(1)}, u32[]{:S(2)}, u32[]{:S(2)}) %all-to-all-start) | async-done | bytes 131104 | tf_op jit(solution)/shard_map/all_to_all | solution.py:467
  23.1 0.7 %edge.1 = (f32[8,2,8,256]{3,2,1,0:T(8,128)S(1)}, f32[4,2,8,256]{3,2,1,0:T(8,128)S(1)}, f32[4,2,8,256]{3,2,1,0:T(8,128)S(1)}) custom-call(s32[16]{0:T(128)S(1)} %fusion.3.ints_in.ints_ref, f32[32,8,128]{2,1,0:T(8,128)S(1)} %all-to-all-done.got_ref), custom_call_target="tpu_custom_call" | custom-call | flops 1000000 | bytes 4000000 | tf_op jit(solution)/shard_map/edge/pallas_call | solution.py:474
  23.8 4.7 %collective-permute-start.1 = (f32[4,2,8,256]{3,2,1,0:T(8,128)S(1)}, f32[4,2,8,256]{3,2,1,0:T(8,128)S(1)}, u32[]{:S(2)}, u32[]{:S(2)}) collective-permute-start(f32[4,2,8,256]{3,2,1,0:T(8,128)S(1)} %get-tuple-element.36), channel_id=1, source_target_pairs={{0,48},{16,32},{32,80},{48,64},{64,112},{80,96},{96,144},{112,128}... | collective-permute-start | bytes 196616 | tf_op jit(solution)/shard_map/ppermute | solution.py:475
  28.4 1.9 %collective-permute-start.2 = (f32[4,2,8,256]{3,2,1,0:T(8,128)S(1)}, f32[4,2,8,256]{3,2,1,0:T(8,128)S(1)}, u32[]{:S(2)}, u32[]{:S(2)}) collective-permute-start(f32[4,2,8,256]{3,2,1,0:T(8,128)S(1)} %get-tuple-element.37), channel_id=1, source_target_pairs={{48,0},{32,16},{80,32},{64,48},{112,64},{96,80},{144,96},{128,112}... | collective-permute-start | bytes 196616 | tf_op jit(solution)/shard_map/ppermute | solution.py:476
  30.4 0.1 pad_maximum_fusion.reals_ref
  30.5 0.6 pair.1
  31.1 0.1 weights.1
  31.2 5.5 %collective-permute-done.2.above_ref = f32[4,2,8,256]{3,2,1,0:T(8,128)S(1)} collective-permute-done((f32[4,2,8,256]{3,2,1,0:T(8,128)S(1)}, f32[4,2,8,256]{3,2,1,0:T(8,128)S(1)}, u32[]{:S(2)}, u32[]{:S(2)}) %collective-permute-start.2) | collective-permute-done | bytes 65568 | tf_op jit(solution)/shard_map/ppermute | solution.py:476
  36.7 0.1 broadcast_in_dim.41.wide_ref
  36.9 2.4 %columns.1 = f32[32,32,128]{2,1,0:T(8,128)} custom-call(s32[16,128]{1,0:T(8,128)S(1)} %broadcast_in_dim.41.wide_ref, f32[8,128]{1,0:T(8,128)S(1)} %broadcast_in_dim.42.reals_ref, f32[8,2,8,256]{3,2,1,0:T(8,128)S(1)} %get-tuple-element.35.own_ref, f32[4,2,8,256]{3,2,1,0:T(8,128)S(1)} %collective-permute-done.1.below_ref, ...), custom_call_target="tpu_custom_call" | custom-call | flops 1000000000 | bytes 4000000 | tf_op jit(solution)/shard_map/columns/pallas_call | solution.py:483
  39.3 6.0 %all-to-all-start.1 = ((f32[32,32,128]{2,1,0:T(8,128)}), f32[32,32,128]{2,1,0:T(8,128)S(1)}, u32[]{:S(2)}, u32[]{:S(2)}) async-start(f32[32,32,128]{2,1,0:T(8,128)} %columns.1), calls=%async_computation.1 | async-start | bytes 1048576 | tf_op jit(solution)/shard_map/all_to_all | solution.py:467
  45.3 2.3 %collective-permute-start.4 = (f32[6,2,16,256]{3,2,1,0:T(8,128)S(1)}, f32[6,2,16,256]{3,2,1,0:T(8,128)S(1)}, u32[]{:S(2)}, u32[]{:S(2)}) collective-permute-start(f32[6,2,16,256]{3,2,1,0:T(8,128)S(1)} %get-tuple-element.46), channel_id=1, source_target_pairs={{0,16},{32,48},{64,80},{96,112},{128,144},{160,176},{192,208},{224... | collective-permute-start | bytes 589832 | tf_op jit(solution)/shard_map/ppermute | solution.py:487
  47.6 2.4 %collective-permute-start.3 = (f32[2,2,16,256]{3,2,1,0:T(8,128)S(1)}, f32[2,2,16,256]{3,2,1,0:T(8,128)S(1)}, u32[]{:S(2)}, u32[]{:S(2)}) collective-permute-start(f32[2,2,16,256]{3,2,1,0:T(8,128)S(1)} %get-tuple-element.45), channel_id=1, source_target_pairs={{0,32},{32,64},{64,96},{96,128},{128,160},{160,192},{192,224},{224... | collective-permute-start | bytes 196616 | tf_op jit(solution)/shard_map/ppermute | solution.py:486
  50.0 6.5 %collective-permute-done.3.p2_ref = f32[2,2,16,256]{3,2,1,0:T(8,128)S(1)} collective-permute-done((f32[2,2,16,256]{3,2,1,0:T(8,128)S(1)}, f32[2,2,16,256]{3,2,1,0:T(8,128)S(1)}, u32[]{:S(2)}, u32[]{:S(2)}) %collective-permute-start.3) | collective-permute-done | bytes 65568 | tf_op jit(solution)/shard_map/ppermute | solution.py:486
  56.5 2.4 %collective-permute-done.4.pair_ref = f32[6,2,16,256]{3,2,1,0:T(8,128)S(1)} collective-permute-done((f32[6,2,16,256]{3,2,1,0:T(8,128)S(1)}, f32[6,2,16,256]{3,2,1,0:T(8,128)S(1)}, u32[]{:S(2)}, u32[]{:S(2)}) %collective-permute-start.4) | collective-permute-done | bytes 196640 | tf_op jit(solution)/shard_map/ppermute | solution.py:487
  58.9 1.7 %rows.1.base_ref = f32[128,256]{1,0:T(8,128)S(1)} custom-call(s32[16]{0:T(128)S(1)} %fusion.3.ints_in.ints_ref, f32[78]{0:T(128)S(1)} %pad_maximum_fusion.reals_ref, f32[4,2,16,256]{3,2,1,0:T(8,128)S(1)} %copy-done.2, f32[4,2,16,256]{3,2,1,0:T(8,128)S(1)} %collective-permute-done.near_ref.p1_ref, f32[2,2,16,256]{3,2,1,0:T(8,128)S(1)} %collective-permute-done.3.p2_ref, ...), custom_call_target="tpu_custom_call" | custom-call | flops 1000000000 | bytes 4000000 | tf_op jit(solution)/shard_map/rows/pallas_call | solution.py:488
  60.6 2.5 %all-to-all-done.1.got_ref = f32[32,32,128]{2,1,0:T(8,128)S(1)} async-done(((f32[32,32,128]{2,1,0:T(8,128)}), f32[32,32,128]{2,1,0:T(8,128)S(1)}, u32[]{:S(2)}, u32[]{:S(2)}) %all-to-all-start.1) | async-done | bytes 524320 | tf_op jit(solution)/shard_map/all_to_all | solution.py:467
  63.1 1.3 %finish.1 = f32[128,256]{1,0:T(8,128)} custom-call(s32[16]{0:T(128)S(1)} %fusion.3.ints_in.ints_ref, f32[32,32,128]{2,1,0:T(8,128)S(1)} %all-to-all-done.1.got_ref, f32[128,256]{1,0:T(8,128)S(1)} %rows.1.base_ref, bf16[256,768]{1,0:T(8,128)(2,1)S(1)} %get-tuple-element.47.ghi_ref, bf16[256,768]{1,0:T(8,128)(2,1)S(1)} %get-tuple-element.48.glo_ref), custom_call_target="tpu_custom_call" | custom-call | flops 300000000 | bytes 4000000 | tf_op jit(solution)/shard_map/finish/pallas_call | solution.py:489
  (22 shorter events, 0.1 us)
Async XLA Ops:
  0.0 31.0 %copy-start = (f32[2,256,256]{2,1,0:T(8,128)S(1)}, f32[2,256,256]{2,1,0:T(8,128)}, u32[]{:S(2)}) copy-start(f32[2,256,256]{2,1,0:T(8,128)} %q_ref) | copy-start | bytes 1572868
  0.0 1.0 %copy-start.1 = (f32[4,2,16,256]{3,2,1,0:T(8,128)S(1)}, f32[4,2,16,256]{3,2,1,0:T(8,128)}, u32[]{:S(2)}) copy-start(f32[4,2,16,256]{3,2,1,0:T(8,128)} %x_ref.1) | copy-start | bytes 393220
  1.7 14.8 %copy-start.4 = (s32[32]{0:T(128)S(1)}, s32[32]{0:T(128)}, u32[]{:S(2)}) copy-start(s32[32]{0:T(128)} %param.11) | copy-start | bytes 388
  1.7 15.0 %copy-start.6 = (f32[2,2]{1,0:T(2,128)S(1)}, f32[2,2]{1,0:T(2,128)}, u32[]{:S(2)}) copy-start(f32[2,2]{1,0:T(2,128)} %param.10) | copy-start | bytes 52
  1.7 28.6 %copy-start.5 = (f32[2]{0:T(128)S(1)}, f32[2]{0:T(128)}, u32[]{:S(2)}) copy-start(f32[2]{0:T(128)} %param.9) | copy-start | bytes 28
  1.7 21.3 %all-to-all-start = ((f32[32,8,128]{2,1,0:T(8,128)}), f32[32,8,128]{2,1,0:T(8,128)S(1)}, u32[]{:S(2)}, u32[]{:S(2)}) async-start(f32[32,8,128]{2,1,0:T(8,128)} %own.1), calls=%async_computation | async-start | bytes 262144 | tf_op jit(solution)/shard_map/all_to_all | solution.py:467
  13.8 16.7 %copy-start.2 = (f32[4,2,16,256]{3,2,1,0:T(8,128)S(1)}, f32[4,2,16,256]{3,2,1,0:T(8,128)}, u32[]{:S(2)}) copy-start(f32[4,2,16,256]{3,2,1,0:T(8,128)} %x_ref.1) | copy-start | bytes 393220
  13.8 17.2 %copy-start.3 = (f32[256,256]{1,0:T(8,128)S(1)}, f32[256,256]{1,0:T(8,128)}, u32[]{:S(2)}) copy-start(f32[256,256]{1,0:T(8,128)} %h_ref) | copy-start | bytes 786436
  13.8 16.6 %collective-permute-start = (f32[4,2,16,256]{3,2,1,0:T(8,128)}, f32[4,2,16,256]{3,2,1,0:T(8,128)S(1)}, u32[]{:S(2)}, u32[]{:S(2)}) collective-permute-start(f32[4,2,16,256]{3,2,1,0:T(8,128)} %x_ref.1), channel_id=1, source_target_pairs={{16,32},{48,64},{80,96},{112,128},{144,160},{176,192},{208,224},{2... | collective-permute-start | bytes 393224 | tf_op jit(solution)/shard_map/ppermute | solution.py:473
  23.8 7.4 %collective-permute-start.1 = (f32[4,2,8,256]{3,2,1,0:T(8,128)S(1)}, f32[4,2,8,256]{3,2,1,0:T(8,128)S(1)}, u32[]{:S(2)}, u32[]{:S(2)}) collective-permute-start(f32[4,2,8,256]{3,2,1,0:T(8,128)S(1)} %get-tuple-element.36), channel_id=1, source_target_pairs={{0,48},{16,32},{32,80},{48,64},{64,112},{80,96},{96,144},{112,128}... | collective-permute-start | bytes 196616 | tf_op jit(solution)/shard_map/ppermute | solution.py:475
  28.4 8.3 %collective-permute-start.2 = (f32[4,2,8,256]{3,2,1,0:T(8,128)S(1)}, f32[4,2,8,256]{3,2,1,0:T(8,128)S(1)}, u32[]{:S(2)}, u32[]{:S(2)}) collective-permute-start(f32[4,2,8,256]{3,2,1,0:T(8,128)S(1)} %get-tuple-element.37), channel_id=1, source_target_pairs={{48,0},{32,16},{80,32},{64,48},{112,64},{96,80},{144,96},{128,112}... | collective-permute-start | bytes 196616 | tf_op jit(solution)/shard_map/ppermute | solution.py:476
  39.3 23.8 %all-to-all-start.1 = ((f32[32,32,128]{2,1,0:T(8,128)}), f32[32,32,128]{2,1,0:T(8,128)S(1)}, u32[]{:S(2)}, u32[]{:S(2)}) async-start(f32[32,32,128]{2,1,0:T(8,128)} %columns.1), calls=%async_computation.1 | async-start | bytes 1048576 | tf_op jit(solution)/shard_map/all_to_all | solution.py:467
  45.3 13.6 %collective-permute-start.4 = (f32[6,2,16,256]{3,2,1,0:T(8,128)S(1)}, f32[6,2,16,256]{3,2,1,0:T(8,128)S(1)}, u32[]{:S(2)}, u32[]{:S(2)}) collective-permute-start(f32[6,2,16,256]{3,2,1,0:T(8,128)S(1)} %get-tuple-element.46), channel_id=1, source_target_pairs={{0,16},{32,48},{64,80},{96,112},{128,144},{160,176},{192,208},{224... | collective-permute-start | bytes 589832 | tf_op jit(solution)/shard_map/ppermute | solution.py:487
  47.6 8.9 %collective-permute-start.3 = (f32[2,2,16,256]{3,2,1,0:T(8,128)S(1)}, f32[2,2,16,256]{3,2,1,0:T(8,128)S(1)}, u32[]{:S(2)}, u32[]{:S(2)}) collective-permute-start(f32[2,2,16,256]{3,2,1,0:T(8,128)S(1)} %get-tuple-element.45), channel_id=1, source_target_pairs={{0,32},{32,64},{64,96},{96,128},{128,160},{160,192},{192,224},{224... | collective-permute-start | bytes 196616 | tf_op jit(solution)/shard_map/ppermute | solution.py:486

commit v9 on v8

--- a/solution.py
+++ b/solution.py
@@ -65,12 +65,11 @@
         return self.root(g >> 1) * jnp.where((g >= 2) & (g < self.live), 1.0, 0.0)
 
     @once
-    def middle(self, p):
+    def twist(self, p):
         g = self.base + p
         n = (g >> 1).astype(F32)
         ok = (g >= 0) & (g < self.live)
-        upper = jnp.where(ok & (g + 2 < self.live), n + 1.0, 0.0)
-        return upper + jnp.where(ok & (g >= 2), n, 0.0)
+        return jnp.where(ok & (g + 2 < self.live), n + 1.0, 0.0) - jnp.where(ok & (g >= 2), n, 0.0)
 
     @once
     def even(self, p):
@@ -128,16 +127,19 @@
     return zero, one, two
 
 
-def put(hi_ref, lo_ref, block, col, j, rows, v):
+def put(hi_ref, lo_ref, col, j, rows, v):
     hi, lo = split(jnp.concatenate([v[0], v[1]], axis=0))
-    at = pl.ds(block * 128 + j * rows, rows)
+    at = pl.ds(j * rows, rows)
     hi_ref[at, 256 * col : 256 * col + 256] = hi
     lo_ref[at, 256 * col : 256 * col + 256] = lo
 
 
+def product(hi, lo, ghi, glo):
+    return dot(hi, ghi) + dot(lo, ghi) + dot(hi, glo)
+
+
 def times_weights(hi_ref, lo_ref, ghi_ref, glo_ref):
-    hi, g = hi_ref[...], ghi_ref[...]
-    return dot(hi, g) + dot(lo_ref[...], g) + dot(hi, glo_ref[...])
+    return product(hi_ref[...], lo_ref[...], ghi_ref[...], glo_ref[...])
 
 
 def weights_kernel(h_ref, q_ref, vhi, vlo, hhi, hlo):
@@ -160,32 +162,28 @@
     return copies
 
 
-def team_counts(ints_ref):
-    side = ints_ref[SIDE]
-    return ints_ref[COUNTS + 2 - side], ints_ref[COUNTS + 3 - side]
-
-
-def edge_kernel(ints_in, got_ref, own_ref, first_ref, last_ref, y_ref, ints_ref, sem):
-    fetched = fetch([(ints_in, ints_ref)], sem)
+def taken(ref, i):
+    return ref[i : i + 1, 0:1][0, 0]
+
+
+def edge_kernel(wide_ref, got_ref, own_ref, first_ref, last_ref, y_ref):
+    side, before, here, after, odd = (taken(wide_ref, i) for i in (SIDE, COUNTS + 1, COUNTS + 2, COUNTS + 3, ODD))
+    own, other = jnp.where(side == 0, here, before), jnp.where(side == 0, after, here)
     for place in range(2):
         vs = []
         for low in range(8):
             vs.append(jnp.concatenate([got_ref[(8 * high + low) * 2 + place] for high in range(2)], axis=0))
         for m, v in enumerate(granules(vs)):
             y_ref[SLOTS * place + m // 2, m % 2] = jnp.concatenate([v[:8], v[8:]], axis=1)
-    for copy in fetched:
-        copy.wait()
-    own, other = team_counts(ints_ref)
-    odd = ints_ref[ODD]
 
     def node(j):
-        return y_ref[jnp.where(j < own, SLOTS * odd + j, SLOTS * (1 - odd) + jnp.minimum(j - own, SLOTS - 1))]
+        return y_ref[jnp.where(j < own, SLOTS * odd + j, SLOTS * (1 - odd) + jnp.clip(j - own, 0, SLOTS - 1))]
 
     for j in range(8):
         own_ref[j] = node(j)
     for j in range(4):
-        first_ref[j] = own_ref[j]
-        last_ref[j] = own_ref[own + other - 4 + j]
+        first_ref[j] = node(j)
+        last_ref[j] = node(own + other - 4 + j)
 
 
 def pair_kernel(ints_ref, x_ref, near_ref, o_ref, far_ref):
@@ -198,9 +196,9 @@
     wide_ref, reals_ref, own_ref, below_ref, above_ref, ghi_ref, glo_ref, o_ref, y_ref, hi_ref, lo_ref, hi2_ref, lo2_ref, z_ref, send_ref, out_sem
 ):
     total, begin, side, before, here, after, odd = (
-        wide_ref[i : i + 1, 0:1][0, 0] for i in (TOTAL, TEAM_BEGIN, SIDE, COUNTS + 1, COUNTS + 2, COUNTS + 3, ODD)
+        taken(wide_ref, i) for i in (TOTAL, TEAM_BEGIN, SIDE, COUNTS + 1, COUNTS + 2, COUNTS + 3, ODD)
     )
-    reals = [reals_ref[i : i + 1, 0:1][0, 0] for i in range(6)]
+    reals = [taken(reals_ref, i) for i in range(6)]
     own, other = jnp.where(side == 0, here, before), jnp.where(side == 0, after, here)
 
     def root(n):
@@ -216,39 +214,24 @@
     for p in range(16):
         v = y_ref[p]
         x.append((v[0], v[1]))
-    a2, b2 = {}, {}
     for p in range(2, 14):
-        a2[p], b2[p] = both1(nodes, x, p, re[1], im[1])
+        put(hi_ref, lo_ref, 0, p - 2, 16, x[p])
+        put(hi_ref, lo_ref, 1, p - 2, 16, both(nodes, x, p, re[0], im[0])[0])
+        put(hi_ref, lo_ref, 2, p - 2, 16, both1(nodes, x, p, re[1], im[1])[0])
+    sums = times_weights(hi_ref, lo_ref, ghi_ref, glo_ref)
+    hi, lo = hi_ref[32:160, :256], lo_ref[32:160, :256]
+    alone = [product(hi, lo, ghi_ref[256 * b : 256 * b + 256, :], glo_ref[256 * b : 256 * b + 256, :]) for b in (1, 2)]
+    s = {p: (sums[16 * p - 32 : 16 * p - 24], sums[16 * p - 24 : 16 * p - 16]) for p in range(2, 14)}
     for j in range(8):
         p = j + 4
-        a1, b1 = both(nodes, x, p, re[0], im[0])
-        a12, b1a2 = both(nodes, a2, p, re[0], im[0])
-        a1b2, _ = both(nodes, b2, p, re[0], im[0])
-        far = scaled(nodes.up(p) * nodes.up(p + 2), x[p + 4])
-        low = scaled(nodes.down(p) * nodes.down(p - 2), x[p - 4])
-        mid = nodes.middle(p)
-        here = scaled(mid, x[p])
-        a11 = plus(plus(far, times(re[0], im[0], here)), times(re[0] * re[0] - im[0] * im[0], 2.0 * re[0] * im[0], low))
-        s11 = plus(plus(scaled(2.0, far), scaled(2.0 * re[0], here)), scaled(2.0 * (re[0] * re[0] + im[0] * im[0]), low))
-        rows = (
-            (x[p], a1, a2[p]),
-            (a1, a11, a12),
-            (a2[p], a12, times(re[1], im[1], x[p])),
-            (scaled(2.0, b1), s11, scaled(2.0, b1a2)),
-            (scaled(2.0, b2[p]), scaled(2.0, a1b2), scaled(2.0 * re[1], x[p])),
-        )
-        for block, row in enumerate(rows):
-            for col, v in enumerate(row):
-                put(hi_ref, lo_ref, block, col, j, 16, v)
-    sums = times_weights(hi_ref, lo_ref, ghi_ref, glo_ref)
-    for j in range(8):
-        p = j + 4
-        for block, v in enumerate(first_order(nodes, x, p, re, im)):
-            s = sums[block * 128 + 16 * j : block * 128 + 16 * j + 16]
-            put(hi2_ref, lo2_ref, 0, block, j, 16, (v[1] - HALF2 * s[:8], -v[0] - HALF2 * s[8:]))
-        z_ref[1, j] = (2.0 * HALF2) * sums[16 * j : 16 * j + 16].reshape(2, 8, 256)
-        z_ref[2, j] = HALF2 * sums[384 + 16 * j : 400 + 16 * j].reshape(2, 8, 256)
-        z_ref[3, j] = HALF2 * sums[512 + 16 * j : 528 + 16 * j].reshape(2, 8, 256)
+        left, right = zip(both(nodes, s, p, re[0], im[0]), both1(nodes, s, p, re[1], im[1]))
+        for col, (v, t) in enumerate(zip(first_order(nodes, x, p, re, im), (s[p], *left))):
+            put(hi2_ref, lo2_ref, col, j, 16, (v[1] - HALF2 * t[0], -v[0] - HALF2 * t[1]))
+        z_ref[1, j] = (2.0 * HALF2) * sums[16 * j + 32 : 16 * j + 48].reshape(2, 8, 256)
+        for b, twist in enumerate((nodes.twist(p), nodes.even(p) - nodes.odd(p))):
+            by = im[b] * twist
+            z_ref[2 + b, j, 0] = (2.0 * HALF2) * (right[b][0] + by * alone[b][16 * j + 8 : 16 * j + 16])
+            z_ref[2 + b, j, 1] = (2.0 * HALF2) * (right[b][1] - by * alone[b][16 * j : 16 * j + 8])
 
     def send(z):
         for r in range(2):
@@ -297,27 +280,17 @@
     for p in range(12):
         v = w_ref[slot(p)]
         x.append((v[0], v[1]))
-    b2 = {}
     for p in range(2, 10):
-        b2[p], _ = both1(nodes, x, p, re[1], im[1])
+        put(hi_ref, lo_ref, 0, p - 2, 32, x[p])
+        put(hi_ref, lo_ref, 1, p - 2, 32, both(nodes, x, p, re[0], im[0])[0])
+        put(hi_ref, lo_ref, 2, p - 2, 32, both1(nodes, x, p, re[1], im[1])[0])
+    sums = times_weights(hi_ref, lo_ref, ghi_ref, glo_ref)
+    s = {p: (sums[32 * p - 64 : 32 * p - 48], sums[32 * p - 48 : 32 * p - 32]) for p in range(2, 10)}
     for j in range(4):
         p = j + 4
-        b1, _ = both(nodes, x, p, re[0], im[0])
-        b12, _ = both(nodes, b2, p, re[0], im[0])
-        far = scaled(nodes.up(p) * nodes.up(p + 2), x[p + 4])
-        low = scaled(nodes.down(p) * nodes.down(p - 2), x[p - 4])
-        here = scaled(nodes.middle(p), x[p])
-        b11 = plus(plus(far, times(re[0], im[0], here)), times(re[0] * re[0] - im[0] * im[0], 2.0 * re[0] * im[0], low))
-        rows = ((x[p], b1, b2[p]), (b1, b11, b12), (b2[p], b12, times(re[1], im[1], x[p])))
-        for block, row in enumerate(rows):
-            for col, v in enumerate(row):
-                put(hi_ref, lo_ref, block, col, j, 32, v)
-    sums = times_weights(hi_ref, lo_ref, ghi_ref, glo_ref)
-    for j in range(4):
-        p = j + 4
-        for block, v in enumerate(first_order(nodes, x, p, re, im)):
-            s = sums[block * 128 + 32 * j : block * 128 + 32 * j + 32]
-            put(hi2_ref, lo2_ref, 0, block, j, 32, (-v[1] - HALF2 * s[:16], v[0] - HALF2 * s[16:]))
+        mixed = (s[p], both(nodes, s, p, re[0], im[0])[0], both1(nodes, s, p, re[1], im[1])[0])
+        for col, (v, t) in enumerate(zip(first_order(nodes, x, p, re, im), mixed)):
+            put(hi2_ref, lo2_ref, col, j, 32, (-v[1] - HALF2 * t[0], v[0] - HALF2 * t[1]))
     right = times_weights(hi2_ref, lo2_ref, ghi_ref, glo_ref)
     for j in range(4):
         d = nodes.damp(j + 4)
@@ -381,8 +354,8 @@
 edge_call = call(
     edge_kernel,
     (struct((8, 2, 8, 256)), struct((4, 2, 8, 256)), struct((4, 2, 8, 256))),
-    [ANY, VMEM],
-    [pltpu.VMEM((8, 2, 8, 256), F32), INTS, pltpu.SemaphoreType.DMA((1,))],
+    [VMEM] * 2,
+    [pltpu.VMEM((8, 2, 8, 256), F32)],
     name="edge",
 )
 pair_call = call(pair_kernel, (struct((6, 2, 16, 256)), struct((2, 2, 16, 256))), [SMEM] + [VMEM] * 2, name="pair")
@@ -392,8 +365,8 @@
     [VMEM] * 7,
     [
         pltpu.VMEM((16, 2, 8, 256), F32),
-        pltpu.VMEM((640, 768), BF),
-        pltpu.VMEM((640, 768), BF),
+        pltpu.VMEM((192, 768), BF),
+        pltpu.VMEM((192, 768), BF),
         pltpu.VMEM((128, 768), BF),
         pltpu.VMEM((128, 768), BF),
         pltpu.VMEM((4, 8, 2, 8, 256), F32),
@@ -410,8 +383,8 @@
     [SMEM] * 2 + [VMEM] * 6,
     [
         pltpu.VMEM((20, 2, 16, 256), F32),
-        pltpu.VMEM((384, 768), BF),
-        pltpu.VMEM((384, 768), BF),
+        pltpu.VMEM((256, 768), BF),
+        pltpu.VMEM((256, 768), BF),
         pltpu.VMEM((128, 768), BF),
         pltpu.VMEM((128, 768), BF),
     ],
@@ -467,16 +440,16 @@
         return lax.all_to_all(v, everyone, 0, 0, axis_index_groups=lists, tiled=True)
 
     ints = integers(node_count)
+    wide = jnp.broadcast_to(ints[:, None], (16, 128))
     reals = jnp.concatenate([gamma, coeff.reshape(4), jnp.sqrt(jnp.arange(ROOTS, dtype=F32))])
     sent, x = lax.optimization_barrier((own_call(densities.reshape(128, 256)), densities))
     got = exchange(sent)
     p1 = lax.ppermute(x, hier, near)
-    own, first, last = edge_call(ints, got)
+    own, first, last = edge_call(wide, got)
     below = lax.ppermute(last, hier, onward)
     above = lax.ppermute(first, hier, backward)
     own, p1, x, hamiltonian, couplings = lax.optimization_barrier((own, p1, x, hamiltonian, couplings))
     vhi, vlo, hhi, hlo = weights_call(hamiltonian, couplings)
-    wide = jnp.broadcast_to(ints[:, None], (16, 128))
     wide_reals = jnp.broadcast_to(reals[:8, None], (8, 128))
     pair, edge = pair_call(ints, x, p1)
     own, pair, edge = lax.optimization_barrier((own, pair, edge))

time: 64.8 us -> 63.9 us (0.986)
  Pallas kernels: 7.61 us -> 6.68 us
  transfers between devices with their start and end apart: 7 -> 7, of which waited for: 5 -> 5; matrix products, arithmetic and copies ran while one was open for 1% -> 1% of each run, Pallas kernels for 5% -> 4%
where the time goes in v9:
time: 63.9 us; the launch traced here: 63.5 us
  starting transfers between devices  31.9 us (50%)
  waiting for transfers between devices  23.2 us (36%)
  Pallas kernels  6.68 us (10%)
  local copies, waits for them, and re-layouts  1.22 us (2%)
    all_to_all x2, starting transfers between devices, exchange(): lax.all_to_all(v, everyone, 0, 0, axis_index_groups=lists, tiled=True)  18.1 us
    all_to_all x2, waiting for transfers between devices, exchange(): lax.all_to_all(v, everyone, 0, 0, axis_index_groups=lists, tiled=True)  8.81 us
    ppermute x1, waiting for transfers between devices, on_device(): p2 = lax.ppermute(edge, hier, far)  6.52 us
    ppermute x1, waiting for transfers between devices, on_device(): above = lax.ppermute(first, hier, backward)  5.49 us
    ppermute x1, starting transfers between devices, on_device(): below = lax.ppermute(last, hier, onward)  4.67 us
    ppermute x1, starting transfers between devices, on_device(): p1 = lax.ppermute(x, hier, near)  2.58 us
    ppermute x1, starting transfers between devices, on_device(): p2 = lax.ppermute(edge, hier, far)  2.4 us
    ppermute x1, waiting for transfers between devices, on_device(): pair = lax.ppermute(pair, hier, inner)  2.37 us
  transfers between devices with their start and end apart: 7, of which 5 were waited for; matrix products, arithmetic and copies ran while one was open for 1% of the time, Pallas kernels for 4%

profile of v9, /device:TPU:28, one launch (start us, length us, event | category | flops | bytes accessed | tf_op | source)
XLA Modules:
  0.0 63.5 jit_solution(8784545401865980275)
XLA Ops:
  0.0 1.0 %copy-done.1 = f32[4,2,16,256]{3,2,1,0:T(8,128)S(1)} copy-done((f32[4,2,16,256]{3,2,1,0:T(8,128)S(1)}, f32[4,2,16,256]{3,2,1,0:T(8,128)}, u32[]{:S(2)}) %copy-start.1) | copy-done | bytes 131096
  1.0 0.8 %own.1 = f32[32,8,128]{2,1,0:T(8,128)} custom-call(f32[128,256]{1,0:T(8,128)S(1)} %bitcast.3), custom_call_target="tpu_custom_call" | custom-call | flops 1000000 | bytes 4000000 | tf_op jit(solution)/shard_map/own/pallas_call | solution.py:445
  1.7 12.1 %all-to-all-start = ((f32[32,8,128]{2,1,0:T(8,128)}), f32[32,8,128]{2,1,0:T(8,128)S(1)}, u32[]{:S(2)}, u32[]{:S(2)}) async-start(f32[32,8,128]{2,1,0:T(8,128)} %own.1), calls=%async_computation | async-start | bytes 262144 | tf_op jit(solution)/shard_map/all_to_all | solution.py:440
  13.8 2.6 %collective-permute-start = (f32[4,2,16,256]{3,2,1,0:T(8,128)}, f32[4,2,16,256]{3,2,1,0:T(8,128)S(1)}, u32[]{:S(2)}, u32[]{:S(2)}) collective-permute-start(f32[4,2,16,256]{3,2,1,0:T(8,128)} %x_ref.1), channel_id=1, source_target_pairs={{16,32},{48,64},{80,96},{112,128},{144,160},{176,192},{208,224},{2... | collective-permute-start | bytes 393224 | tf_op jit(solution)/shard_map/ppermute | solution.py:447
  16.5 0.2 select_reduce_fusion
  16.7 0.1 reshape.68
  16.8 6.3 %all-to-all-done.got_ref = f32[32,8,128]{2,1,0:T(8,128)S(1)} async-done(((f32[32,8,128]{2,1,0:T(8,128)}), f32[32,8,128]{2,1,0:T(8,128)S(1)}, u32[]{:S(2)}, u32[]{:S(2)}) %all-to-all-start) | async-done | bytes 131104 | tf_op jit(solution)/shard_map/all_to_all | solution.py:440
  23.1 0.1 broadcast_in_dim.41.wide_ref
  23.1 0.2 edge.1
  23.3 4.7 %collective-permute-start.1 = (f32[4,2,8,256]{3,2,1,0:T(8,128)S(1)}, f32[4,2,8,256]{3,2,1,0:T(8,128)S(1)}, u32[]{:S(2)}, u32[]{:S(2)}) collective-permute-start(f32[4,2,8,256]{3,2,1,0:T(8,128)S(1)} %get-tuple-element.36), channel_id=1, source_target_pairs={{0,48},{16,32},{32,80},{48,64},{64,112},{80,96},{96,144},{112,128}... | collective-permute-start | bytes 196616 | tf_op jit(solution)/shard_map/ppermute | solution.py:449
  28.0 1.9 %collective-permute-start.2 = (f32[4,2,8,256]{3,2,1,0:T(8,128)S(1)}, f32[4,2,8,256]{3,2,1,0:T(8,128)S(1)}, u32[]{:S(2)}, u32[]{:S(2)}) collective-permute-start(f32[4,2,8,256]{3,2,1,0:T(8,128)S(1)} %get-tuple-element.37), channel_id=1, source_target_pairs={{48,0},{32,16},{80,32},{64,48},{112,64},{96,80},{144,96},{128,112}... | collective-permute-start | bytes 196616 | tf_op jit(solution)/shard_map/ppermute | solution.py:450
  30.0 0.1 pad_maximum_fusion.reals_ref
  30.0 0.6 pair.1
  30.6 0.1 weights.1
  30.8 5.5 %collective-permute-done.2.above_ref = f32[4,2,8,256]{3,2,1,0:T(8,128)S(1)} collective-permute-done((f32[4,2,8,256]{3,2,1,0:T(8,128)S(1)}, f32[4,2,8,256]{3,2,1,0:T(8,128)S(1)}, u32[]{:S(2)}, u32[]{:S(2)}) %collective-permute-start.2) | collective-permute-done | bytes 65568 | tf_op jit(solution)/shard_map/ppermute | solution.py:450
  36.4 2.0 %columns.1 = f32[32,32,128]{2,1,0:T(8,128)} custom-call(s32[16,128]{1,0:T(8,128)S(1)} %broadcast_in_dim.41.wide_ref, f32[8,128]{1,0:T(8,128)S(1)} %broadcast_in_dim.42.reals_ref, f32[8,2,8,256]{3,2,1,0:T(8,128)S(1)} %get-tuple-element.35.own_ref, f32[4,2,8,256]{3,2,1,0:T(8,128)S(1)} %collective-permute-done.1.below_ref, ...), custom_call_target="tpu_custom_call" | custom-call | flops 1000000000 | bytes 4000000 | tf_op jit(solution)/shard_map/columns/pallas_call | solution.py:456
  38.4 6.0 %all-to-all-start.1 = ((f32[32,32,128]{2,1,0:T(8,128)}), f32[32,32,128]{2,1,0:T(8,128)S(1)}, u32[]{:S(2)}, u32[]{:S(2)}) async-start(f32[32,32,128]{2,1,0:T(8,128)} %columns.1), calls=%async_computation.1 | async-start | bytes 1048576 | tf_op jit(solution)/shard_map/all_to_all | solution.py:440
  44.4 2.3 %collective-permute-start.4 = (f32[6,2,16,256]{3,2,1,0:T(8,128)S(1)}, f32[6,2,16,256]{3,2,1,0:T(8,128)S(1)}, u32[]{:S(2)}, u32[]{:S(2)}) collective-permute-start(f32[6,2,16,256]{3,2,1,0:T(8,128)S(1)} %get-tuple-element.46), channel_id=1, source_target_pairs={{0,16},{32,48},{64,80},{96,112},{128,144},{160,176},{192,208},{224... | collective-permute-start | bytes 589832 | tf_op jit(solution)/shard_map/ppermute | solution.py:460
  46.7 2.4 %collective-permute-start.3 = (f32[2,2,16,256]{3,2,1,0:T(8,128)S(1)}, f32[2,2,16,256]{3,2,1,0:T(8,128)S(1)}, u32[]{:S(2)}, u32[]{:S(2)}) collective-permute-start(f32[2,2,16,256]{3,2,1,0:T(8,128)S(1)} %get-tuple-element.45), channel_id=1, source_target_pairs={{0,32},{32,64},{64,96},{96,128},{128,160},{160,192},{192,224},{224... | collective-permute-start | bytes 196616 | tf_op jit(solution)/shard_map/ppermute | solution.py:459
  49.1 6.5 %collective-permute-done.3.p2_ref = f32[2,2,16,256]{3,2,1,0:T(8,128)S(1)} collective-permute-done((f32[2,2,16,256]{3,2,1,0:T(8,128)S(1)}, f32[2,2,16,256]{3,2,1,0:T(8,128)S(1)}, u32[]{:S(2)}, u32[]{:S(2)}) %collective-permute-start.3) | collective-permute-done | bytes 65568 | tf_op jit(solution)/shard_map/ppermute | solution.py:459
  55.6 2.4 %collective-permute-done.4.pair_ref = f32[6,2,16,256]{3,2,1,0:T(8,128)S(1)} collective-permute-done((f32[6,2,16,256]{3,2,1,0:T(8,128)S(1)}, f32[6,2,16,256]{3,2,1,0:T(8,128)S(1)}, u32[]{:S(2)}, u32[]{:S(2)}) %collective-permute-start.4) | collective-permute-done | bytes 196640 | tf_op jit(solution)/shard_map/ppermute | solution.py:460
  58.0 1.7 %rows.1.base_ref = f32[128,256]{1,0:T(8,128)S(1)} custom-call(s32[16]{0:T(128)S(1)} %fusion.3.ints_ref.ints_in, f32[78]{0:T(128)S(1)} %pad_maximum_fusion.reals_ref, f32[4,2,16,256]{3,2,1,0:T(8,128)S(1)} %copy-done.2, f32[4,2,16,256]{3,2,1,0:T(8,128)S(1)} %collective-permute-done.near_ref.p1_ref, f32[2,2,16,256]{3,2,1,0:T(8,128)S(1)} %collective-permute-done.3.p2_ref, ...), custom_call_target="tpu_custom_call" | custom-call | flops 1000000000 | bytes 4000000 | tf_op jit(solution)/shard_map/rows/pallas_call | solution.py:461
  59.7 2.5 %all-to-all-done.1.got_ref = f32[32,32,128]{2,1,0:T(8,128)S(1)} async-done(((f32[32,32,128]{2,1,0:T(8,128)}), f32[32,32,128]{2,1,0:T(8,128)S(1)}, u32[]{:S(2)}, u32[]{:S(2)}) %all-to-all-start.1) | async-done | bytes 524320 | tf_op jit(solution)/shard_map/all_to_all | solution.py:440
  62.2 1.3 %finish.1 = f32[128,256]{1,0:T(8,128)} custom-call(s32[16]{0:T(128)S(1)} %fusion.3.ints_ref.ints_in, f32[32,32,128]{2,1,0:T(8,128)S(1)} %all-to-all-done.1.got_ref, f32[128,256]{1,0:T(8,128)S(1)} %rows.1.base_ref, bf16[256,768]{1,0:T(8,128)(2,1)S(1)} %get-tuple-element.47.ghi_ref, bf16[256,768]{1,0:T(8,128)(2,1)S(1)} %get-tuple-element.48.glo_ref), custom_call_target="tpu_custom_call" | custom-call | flops 300000000 | bytes 4000000 | tf_op jit(solution)/shard_map/finish/pallas_call | solution.py:462
  (22 shorter events, 0.1 us)
Async XLA Ops:
  0.0 30.6 %copy-start = (f32[2,256,256]{2,1,0:T(8,128)S(1)}, f32[2,256,256]{2,1,0:T(8,128)}, u32[]{:S(2)}) copy-start(f32[2,256,256]{2,1,0:T(8,128)} %q_ref) | copy-start | bytes 1572868
  0.0 1.0 %copy-start.1 = (f32[4,2,16,256]{3,2,1,0:T(8,128)S(1)}, f32[4,2,16,256]{3,2,1,0:T(8,128)}, u32[]{:S(2)}) copy-start(f32[4,2,16,256]{3,2,1,0:T(8,128)} %x_ref.1) | copy-start | bytes 393220
  1.7 14.8 %copy-start.4 = (s32[32]{0:T(128)S(1)}, s32[32]{0:T(128)}, u32[]{:S(2)}) copy-start(s32[32]{0:T(128)} %param.11) | copy-start | bytes 388
  1.7 15.0 %copy-start.6 = (f32[2,2]{1,0:T(2,128)S(1)}, f32[2,2]{1,0:T(2,128)}, u32[]{:S(2)}) copy-start(f32[2,2]{1,0:T(2,128)} %param.10) | copy-start | bytes 52
  1.7 28.2 %copy-start.5 = (f32[2]{0:T(128)S(1)}, f32[2]{0:T(128)}, u32[]{:S(2)}) copy-start(f32[2]{0:T(128)} %param.9) | copy-start | bytes 28
  1.7 21.3 %all-to-all-start = ((f32[32,8,128]{2,1,0:T(8,128)}), f32[32,8,128]{2,1,0:T(8,128)S(1)}, u32[]{:S(2)}, u32[]{:S(2)}) async-start(f32[32,8,128]{2,1,0:T(8,128)} %own.1), calls=%async_computation | async-start | bytes 262144 | tf_op jit(solution)/shard_map/all_to_all | solution.py:440
  13.8 16.2 %copy-start.2 = (f32[4,2,16,256]{3,2,1,0:T(8,128)S(1)}, f32[4,2,16,256]{3,2,1,0:T(8,128)}, u32[]{:S(2)}) copy-start(f32[4,2,16,256]{3,2,1,0:T(8,128)} %x_ref.1) | copy-start | bytes 393220
  13.8 16.8 %copy-start.3 = (f32[256,256]{1,0:T(8,128)S(1)}, f32[256,256]{1,0:T(8,128)}, u32[]{:S(2)}) copy-start(f32[256,256]{1,0:T(8,128)} %h_ref) | copy-start | bytes 786436
  13.8 16.2 %collective-permute-start = (f32[4,2,16,256]{3,2,1,0:T(8,128)}, f32[4,2,16,256]{3,2,1,0:T(8,128)S(1)}, u32[]{:S(2)}, u32[]{:S(2)}) collective-permute-start(f32[4,2,16,256]{3,2,1,0:T(8,128)} %x_ref.1), channel_id=1, source_target_pairs={{16,32},{48,64},{80,96},{112,128},{144,160},{176,192},{208,224},{2... | collective-permute-start | bytes 393224 | tf_op jit(solution)/shard_map/ppermute | solution.py:447
  23.3 7.4 %collective-permute-start.1 = (f32[4,2,8,256]{3,2,1,0:T(8,128)S(1)}, f32[4,2,8,256]{3,2,1,0:T(8,128)S(1)}, u32[]{:S(2)}, u32[]{:S(2)}) collective-permute-start(f32[4,2,8,256]{3,2,1,0:T(8,128)S(1)} %get-tuple-element.36), channel_id=1, source_target_pairs={{0,48},{16,32},{32,80},{48,64},{64,112},{80,96},{96,144},{112,128}... | collective-permute-start | bytes 196616 | tf_op jit(solution)/shard_map/ppermute | solution.py:449
  28.0 8.3 %collective-permute-start.2 = (f32[4,2,8,256]{3,2,1,0:T(8,128)S(1)}, f32[4,2,8,256]{3,2,1,0:T(8,128)S(1)}, u32[]{:S(2)}, u32[]{:S(2)}) collective-permute-start(f32[4,2,8,256]{3,2,1,0:T(8,128)S(1)} %get-tuple-element.37), channel_id=1, source_target_pairs={{48,0},{32,16},{80,32},{64,48},{112,64},{96,80},{144,96},{128,112}... | collective-permute-start | bytes 196616 | tf_op jit(solution)/shard_map/ppermute | solution.py:450
  38.4 23.8 %all-to-all-start.1 = ((f32[32,32,128]{2,1,0:T(8,128)}), f32[32,32,128]{2,1,0:T(8,128)S(1)}, u32[]{:S(2)}, u32[]{:S(2)}) async-start(f32[32,32,128]{2,1,0:T(8,128)} %columns.1), calls=%async_computation.1 | async-start | bytes 1048576 | tf_op jit(solution)/shard_map/all_to_all | solution.py:440
  44.4 13.6 %collective-permute-start.4 = (f32[6,2,16,256]{3,2,1,0:T(8,128)S(1)}, f32[6,2,16,256]{3,2,1,0:T(8,128)S(1)}, u32[]{:S(2)}, u32[]{:S(2)}) collective-permute-start(f32[6,2,16,256]{3,2,1,0:T(8,128)S(1)} %get-tuple-element.46), channel_id=1, source_target_pairs={{0,16},{32,48},{64,80},{96,112},{128,144},{160,176},{192,208},{224... | collective-permute-start | bytes 589832 | tf_op jit(solution)/shard_map/ppermute | solution.py:460
  46.7 8.9 %collective-permute-start.3 = (f32[2,2,16,256]{3,2,1,0:T(8,128)S(1)}, f32[2,2,16,256]{3,2,1,0:T(8,128)S(1)}, u32[]{:S(2)}, u32[]{:S(2)}) collective-permute-start(f32[2,2,16,256]{3,2,1,0:T(8,128)S(1)} %get-tuple-element.45), channel_id=1, source_target_pairs={{0,32},{32,64},{64,96},{96,128},{128,160},{160,192},{192,224},{224... | collective-permute-start | bytes 196616 | tf_op jit(solution)/shard_map/ppermute | solution.py:459

commit v10 on v9

--- a/solution.py
+++ b/solution.py
@@ -166,7 +166,7 @@
     return ref[i : i + 1, 0:1][0, 0]
 
 
-def edge_kernel(wide_ref, got_ref, own_ref, first_ref, last_ref, y_ref):
+def edge_kernel(wide_ref, got_ref, own_ref, ring_ref, cross_ref, y_ref):
     side, before, here, after, odd = (taken(wide_ref, i) for i in (SIDE, COUNTS + 1, COUNTS + 2, COUNTS + 3, ODD))
     own, other = jnp.where(side == 0, here, before), jnp.where(side == 0, after, here)
     for place in range(2):
@@ -181,9 +181,10 @@
 
     for j in range(8):
         own_ref[j] = node(j)
+    behind, ahead = jnp.where(odd == 0, own + other - 4, 0), jnp.where(odd == 0, 0, own + other - 4)
     for j in range(4):
-        first_ref[j] = node(j)
-        last_ref[j] = node(own + other - 4 + j)
+        ring_ref[j] = node(behind + j)
+        cross_ref[j] = node(ahead + j)
 
 
 def pair_kernel(ints_ref, x_ref, near_ref, o_ref, far_ref):
@@ -193,7 +194,7 @@
 
 
 def column_kernel(
-    wide_ref, reals_ref, own_ref, below_ref, above_ref, ghi_ref, glo_ref, o_ref, y_ref, hi_ref, lo_ref, hi2_ref, lo2_ref, z_ref, send_ref, out_sem
+    wide_ref, reals_ref, own_ref, cross_ref, ring_ref, ghi_ref, glo_ref, o_ref, y_ref, hi_ref, lo_ref, hi2_ref, lo2_ref, z_ref, send_ref, out_sem
 ):
     total, begin, side, before, here, after, odd = (
         taken(wide_ref, i) for i in (TOTAL, TEAM_BEGIN, SIDE, COUNTS + 1, COUNTS + 2, COUNTS + 3, ODD)
@@ -206,10 +207,10 @@
 
     nodes = Nodes(total, begin, reals, root)
     re, im = nodes.re, nodes.im
-    y_ref[0:4] = below_ref[...]
     y_ref[4:12] = own_ref[...]
-    y_ref[12:16] = above_ref[...]
-    y_ref[pl.ds(4 + own + other, 4)] = above_ref[...]
+    y_ref[12:16] = ring_ref[...]
+    y_ref[pl.ds(jnp.where(odd == 0, 4 + own + other, 0), 4)] = ring_ref[...]
+    y_ref[pl.ds(jnp.where(odd == 0, 0, 4 + own + other), 4)] = cross_ref[...]
     x = []
     for p in range(16):
         v = y_ref[p]
@@ -403,7 +404,9 @@
     pairs = [(i, i + 1) for i in range(0, shards, 2)]
     inner = pairs + [(b, a) for a, b in pairs]
     onward = [(i, (i // 2 + 1) * 2 + 1 - i % 2) for i in range(shards - 2)]
-    return near, far, inner, onward, [(b, a) for a, b in onward]
+    ring = [(a, b) for a, b in onward if a // 2 % 2 == 0]
+    cross = [(a, b) for a, b in onward if a // 2 % 2 == 1]
+    return near, far, inner, ring + [(b, a) for a, b in ring], cross + [(b, a) for a, b in cross]
 
 
 def groups(shards, columns):
@@ -434,7 +437,7 @@
     shards = node_count.shape[0]
     everyone = ("team", "r", "col")
     lists = groups(shards, lax.axis_size("col"))
-    near, far, inner, onward, backward = routes(shards)
+    near, far, inner, ring, cross = routes(shards)
 
     def exchange(v):
         return lax.all_to_all(v, everyone, 0, 0, axis_index_groups=lists, tiled=True)
@@ -445,15 +448,15 @@
     sent, x = lax.optimization_barrier((own_call(densities.reshape(128, 256)), densities))
     got = exchange(sent)
     p1 = lax.ppermute(x, hier, near)
-    own, first, last = edge_call(wide, got)
-    below = lax.ppermute(last, hier, onward)
-    above = lax.ppermute(first, hier, backward)
+    own, ring_edge, cross_edge = edge_call(wide, got)
+    cross_got = lax.ppermute(cross_edge, hier, cross)
+    ring_got = lax.ppermute(ring_edge, hier, ring)
     own, p1, x, hamiltonian, couplings = lax.optimization_barrier((own, p1, x, hamiltonian, couplings))
     vhi, vlo, hhi, hlo = weights_call(hamiltonian, couplings)
     wide_reals = jnp.broadcast_to(reals[:8, None], (8, 128))
     pair, edge = pair_call(ints, x, p1)
     own, pair, edge = lax.optimization_barrier((own, pair, edge))
-    back_sent = column_call(wide, wide_reals, own, below, above, vhi, vlo)
+    back_sent = column_call(wide, wide_reals, own, cross_got, ring_got, vhi, vlo)
     back_sent, pair, edge = lax.optimization_barrier((back_sent, pair, edge))
     back_got = exchange(back_sent)
     p2 = lax.ppermute(edge, hier, far)

time: 63.9 us -> 61.9 us (0.969)
  waiting for transfers between devices: 23.2 us -> 19.1 us
  starting transfers between devices: 31.9 us -> 33.9 us
    ppermute x1, waiting for transfers between devices: 2.37 us -> 0.26 us  [on_device(): pair = lax.ppermute(pair, hier, inner)]
    ppermute x2, waiting for transfers between devices: 5.5 us -> 3.39 us  [the longest x1 2.56 us: on_device(): ring_got = lax.ppermute(ring_edge, hier, ring)]
    ppermute x1, starting transfers between devices: 2.4 us -> 4.4 us  [on_device(): p2 = lax.ppermute(edge, hier, far)]
  transfers between devices with their start and end apart: 7 -> 7, of which waited for: 5 -> 6; matrix products, arithmetic and copies ran while one was open for 1% -> 1% of each run, Pallas kernels for 4% -> 4%
where the time goes in v10:
time: 61.9 us; the launch traced here: 61.4 us
  starting transfers between devices  33.9 us (55%)
  waiting for transfers between devices  19.1 us (31%)
  Pallas kernels  6.7 us (11%)
  local copies, waits for them, and re-layouts  1.22 us (2%)
    all_to_all x2, starting transfers between devices, exchange(): lax.all_to_all(v, everyone, 0, 0, axis_index_groups=lists, tiled=True)  18.1 us
    all_to_all x2, waiting for transfers between devices, exchange(): lax.all_to_all(v, everyone, 0, 0, axis_index_groups=lists, tiled=True)  8.81 us
    ppermute x1, waiting for transfers between devices, on_device(): p2 = lax.ppermute(edge, hier, far)  6.64 us
    ppermute x1, starting transfers between devices, on_device(): cross_got = lax.ppermute(cross_edge, hier, cross)  4.67 us
    ppermute x1, starting transfers between devices, on_device(): p2 = lax.ppermute(edge, hier, far)  4.4 us
    ppermute x1, starting transfers between devices, on_device(): p1 = lax.ppermute(x, hier, near)  2.58 us
    ppermute x1, waiting for transfers between devices, on_device(): ring_got = lax.ppermute(ring_edge, hier, ring)  2.56 us
    ppermute x1, starting transfers between devices, on_device(): pair = lax.ppermute(pair, hier, inner)  2.26 us
  transfers between devices with their start and end apart: 7, of which 6 were waited for; matrix products, arithmetic and copies ran while one was open for 1% of the time, Pallas kernels for 4%

profile of v10, /device:TPU:28, one launch (start us, length us, event | category | flops | bytes accessed | tf_op | source)
XLA Modules:
  0.0 61.4 jit_solution(11376810135013549764)
XLA Ops:
  0.0 1.0 %copy-done.1 = f32[4,2,16,256]{3,2,1,0:T(8,128)S(1)} copy-done((f32[4,2,16,256]{3,2,1,0:T(8,128)S(1)}, f32[4,2,16,256]{3,2,1,0:T(8,128)}, u32[]{:S(2)}) %copy-start.1) | copy-done | bytes 131096
  1.0 0.8 %own.1 = f32[32,8,128]{2,1,0:T(8,128)} custom-call(f32[128,256]{1,0:T(8,128)S(1)} %bitcast.3), custom_call_target="tpu_custom_call" | custom-call | flops 1000000 | bytes 4000000 | tf_op jit(solution)/shard_map/own/pallas_call | solution.py:448
  1.7 12.1 %all-to-all-start = ((f32[32,8,128]{2,1,0:T(8,128)}), f32[32,8,128]{2,1,0:T(8,128)S(1)}, u32[]{:S(2)}, u32[]{:S(2)}) async-start(f32[32,8,128]{2,1,0:T(8,128)} %own.1), calls=%async_computation | async-start | bytes 262144 | tf_op jit(solution)/shard_map/all_to_all | solution.py:443
  13.8 2.6 %collective-permute-start = (f32[4,2,16,256]{3,2,1,0:T(8,128)}, f32[4,2,16,256]{3,2,1,0:T(8,128)S(1)}, u32[]{:S(2)}, u32[]{:S(2)}) collective-permute-start(f32[4,2,16,256]{3,2,1,0:T(8,128)} %x_ref.1), channel_id=1, source_target_pairs={{16,32},{48,64},{80,96},{112,128},{144,160},{176,192},{208,224},{2... | collective-permute-start | bytes 393224 | tf_op jit(solution)/shard_map/ppermute | solution.py:450
  16.5 0.2 select_reduce_fusion
  16.7 0.1 reshape.68
  16.8 6.3 %all-to-all-done.got_ref = f32[32,8,128]{2,1,0:T(8,128)S(1)} async-done(((f32[32,8,128]{2,1,0:T(8,128)}), f32[32,8,128]{2,1,0:T(8,128)S(1)}, u32[]{:S(2)}, u32[]{:S(2)}) %all-to-all-start) | async-done | bytes 131104 | tf_op jit(solution)/shard_map/all_to_all | solution.py:443
  23.1 0.2 edge.1
  23.4 4.7 %collective-permute-start.1 = (f32[4,2,8,256]{3,2,1,0:T(8,128)S(1)}, f32[4,2,8,256]{3,2,1,0:T(8,128)S(1)}, u32[]{:S(2)}, u32[]{:S(2)}) collective-permute-start(f32[4,2,8,256]{3,2,1,0:T(8,128)S(1)} %get-tuple-element.36), channel_id=1, source_target_pairs={{32,80},{48,64},{96,144},{112,128},{160,208},{176,192},{224,272},{... | collective-permute-start | bytes 196616 | tf_op jit(solution)/shard_map/ppermute | solution.py:452
  28.0 1.9 %collective-permute-start.2 = (f32[4,2,8,256]{3,2,1,0:T(8,128)S(1)}, f32[4,2,8,256]{3,2,1,0:T(8,128)S(1)}, u32[]{:S(2)}, u32[]{:S(2)}) collective-permute-start(f32[4,2,8,256]{3,2,1,0:T(8,128)S(1)} %get-tuple-element.37), channel_id=1, source_target_pairs={{0,48},{16,32},{64,112},{80,96},{128,176},{144,160},{192,240},{208... | collective-permute-start | bytes 196616 | tf_op jit(solution)/shard_map/ppermute | solution.py:453
  30.0 0.1 pad_maximum_fusion.reals_ref
  30.0 0.6 pair.1
  30.6 0.1 weights.1
  30.8 0.8 %collective-permute-done.1.cross_ref = f32[4,2,8,256]{3,2,1,0:T(8,128)S(1)} collective-permute-done((f32[4,2,8,256]{3,2,1,0:T(8,128)S(1)}, f32[4,2,8,256]{3,2,1,0:T(8,128)S(1)}, u32[]{:S(2)}, u32[]{:S(2)}) %collective-permute-start.1) | collective-permute-done | bytes 65568 | tf_op jit(solution)/shard_map/ppermute | solution.py:452
  31.6 2.6 %collective-permute-done.2.ring_ref = f32[4,2,8,256]{3,2,1,0:T(8,128)S(1)} collective-permute-done((f32[4,2,8,256]{3,2,1,0:T(8,128)S(1)}, f32[4,2,8,256]{3,2,1,0:T(8,128)S(1)}, u32[]{:S(2)}, u32[]{:S(2)}) %collective-permute-start.2) | collective-permute-done | bytes 65568 | tf_op jit(solution)/shard_map/ppermute | solution.py:453
  34.3 2.0 %columns.1 = f32[32,32,128]{2,1,0:T(8,128)} custom-call(s32[16,128]{1,0:T(8,128)S(1)} %broadcast_in_dim.41.wide_ref, f32[8,128]{1,0:T(8,128)S(1)} %broadcast_in_dim.42.reals_ref, f32[8,2,8,256]{3,2,1,0:T(8,128)S(1)} %get-tuple-element.35.own_ref, f32[4,2,8,256]{3,2,1,0:T(8,128)S(1)} %collective-permute-done.1.cross_ref, ...), custom_call_target="tpu_custom_call" | custom-call | flops 1000000000 | bytes 4000000 | tf_op jit(solution)/shard_map/columns/pallas_call | solution.py:459
  36.3 6.0 %all-to-all-start.1 = ((f32[32,32,128]{2,1,0:T(8,128)}), f32[32,32,128]{2,1,0:T(8,128)S(1)}, u32[]{:S(2)}, u32[]{:S(2)}) async-start(f32[32,32,128]{2,1,0:T(8,128)} %columns.1), calls=%async_computation.1 | async-start | bytes 1048576 | tf_op jit(solution)/shard_map/all_to_all | solution.py:443
  42.3 2.3 %collective-permute-start.4 = (f32[6,2,16,256]{3,2,1,0:T(8,128)S(1)}, f32[6,2,16,256]{3,2,1,0:T(8,128)S(1)}, u32[]{:S(2)}, u32[]{:S(2)}) collective-permute-start(f32[6,2,16,256]{3,2,1,0:T(8,128)S(1)} %get-tuple-element.46), channel_id=1, source_target_pairs={{0,16},{32,48},{64,80},{96,112},{128,144},{160,176},{192,208},{224... | collective-permute-start | bytes 589832 | tf_op jit(solution)/shard_map/ppermute | solution.py:463
  44.6 4.4 %collective-permute-start.3 = (f32[2,2,16,256]{3,2,1,0:T(8,128)S(1)}, f32[2,2,16,256]{3,2,1,0:T(8,128)S(1)}, u32[]{:S(2)}, u32[]{:S(2)}) collective-permute-start(f32[2,2,16,256]{3,2,1,0:T(8,128)S(1)} %get-tuple-element.45), channel_id=1, source_target_pairs={{0,32},{32,64},{64,96},{96,128},{128,160},{160,192},{192,224},{224... | collective-permute-start | bytes 196616 | tf_op jit(solution)/shard_map/ppermute | solution.py:462
  49.0 6.6 %collective-permute-done.3.p2_ref = f32[2,2,16,256]{3,2,1,0:T(8,128)S(1)} collective-permute-done((f32[2,2,16,256]{3,2,1,0:T(8,128)S(1)}, f32[2,2,16,256]{3,2,1,0:T(8,128)S(1)}, u32[]{:S(2)}, u32[]{:S(2)}) %collective-permute-start.3) | collective-permute-done | bytes 65568 | tf_op jit(solution)/shard_map/ppermute | solution.py:462
  55.6 0.3 collective-permute-done.4.pair_ref
  55.9 1.7 %rows.1.base_ref = f32[128,256]{1,0:T(8,128)S(1)} custom-call(s32[16]{0:T(128)S(1)} %fusion.3.ints_ref.ints_in, f32[78]{0:T(128)S(1)} %pad_maximum_fusion.reals_ref, f32[4,2,16,256]{3,2,1,0:T(8,128)S(1)} %copy-done.2, f32[4,2,16,256]{3,2,1,0:T(8,128)S(1)} %collective-permute-done.near_ref.p1_ref, f32[2,2,16,256]{3,2,1,0:T(8,128)S(1)} %collective-permute-done.3.p2_ref, ...), custom_call_target="tpu_custom_call" | custom-call | flops 1000000000 | bytes 4000000 | tf_op jit(solution)/shard_map/rows/pallas_call | solution.py:464
  57.6 2.5 %all-to-all-done.1.got_ref = f32[32,32,128]{2,1,0:T(8,128)S(1)} async-done(((f32[32,32,128]{2,1,0:T(8,128)}), f32[32,32,128]{2,1,0:T(8,128)S(1)}, u32[]{:S(2)}, u32[]{:S(2)}) %all-to-all-start.1) | async-done | bytes 524320 | tf_op jit(solution)/shard_map/all_to_all | solution.py:443
  60.1 1.3 %finish.1 = f32[128,256]{1,0:T(8,128)} custom-call(s32[16]{0:T(128)S(1)} %fusion.3.ints_ref.ints_in, f32[32,32,128]{2,1,0:T(8,128)S(1)} %all-to-all-done.1.got_ref, f32[128,256]{1,0:T(8,128)S(1)} %rows.1.base_ref, bf16[256,768]{1,0:T(8,128)(2,1)S(1)} %get-tuple-element.47.ghi_ref, bf16[256,768]{1,0:T(8,128)(2,1)S(1)} %get-tuple-element.48.glo_ref), custom_call_target="tpu_custom_call" | custom-call | flops 300000000 | bytes 4000000 | tf_op jit(solution)/shard_map/finish/pallas_call | solution.py:465
  (22 shorter events, 0.2 us)
Async XLA Ops:
  0.0 30.6 %copy-start = (f32[2,256,256]{2,1,0:T(8,128)S(1)}, f32[2,256,256]{2,1,0:T(8,128)}, u32[]{:S(2)}) copy-start(f32[2,256,256]{2,1,0:T(8,128)} %q_ref) | copy-start | bytes 1572868
  0.0 1.0 %copy-start.1 = (f32[4,2,16,256]{3,2,1,0:T(8,128)S(1)}, f32[4,2,16,256]{3,2,1,0:T(8,128)}, u32[]{:S(2)}) copy-start(f32[4,2,16,256]{3,2,1,0:T(8,128)} %x_ref.1) | copy-start | bytes 393220
  1.7 14.8 %copy-start.4 = (s32[32]{0:T(128)S(1)}, s32[32]{0:T(128)}, u32[]{:S(2)}) copy-start(s32[32]{0:T(128)} %param.11) | copy-start | bytes 388
  1.7 15.0 %copy-start.6 = (f32[2,2]{1,0:T(2,128)S(1)}, f32[2,2]{1,0:T(2,128)}, u32[]{:S(2)}) copy-start(f32[2,2]{1,0:T(2,128)} %param.10) | copy-start | bytes 52
  1.7 28.2 %copy-start.5 = (f32[2]{0:T(128)S(1)}, f32[2]{0:T(128)}, u32[]{:S(2)}) copy-start(f32[2]{0:T(128)} %param.9) | copy-start | bytes 28
  1.7 21.3 %all-to-all-start = ((f32[32,8,128]{2,1,0:T(8,128)}), f32[32,8,128]{2,1,0:T(8,128)S(1)}, u32[]{:S(2)}, u32[]{:S(2)}) async-start(f32[32,8,128]{2,1,0:T(8,128)} %own.1), calls=%async_computation | async-start | bytes 262144 | tf_op jit(solution)/shard_map/all_to_all | solution.py:443
  13.8 16.2 %copy-start.2 = (f32[4,2,16,256]{3,2,1,0:T(8,128)S(1)}, f32[4,2,16,256]{3,2,1,0:T(8,128)}, u32[]{:S(2)}) copy-start(f32[4,2,16,256]{3,2,1,0:T(8,128)} %x_ref.1) | copy-start | bytes 393220
  13.8 16.8 %copy-start.3 = (f32[256,256]{1,0:T(8,128)S(1)}, f32[256,256]{1,0:T(8,128)}, u32[]{:S(2)}) copy-start(f32[256,256]{1,0:T(8,128)} %h_ref) | copy-start | bytes 786436
  13.8 16.2 %collective-permute-start = (f32[4,2,16,256]{3,2,1,0:T(8,128)}, f32[4,2,16,256]{3,2,1,0:T(8,128)S(1)}, u32[]{:S(2)}, u32[]{:S(2)}) collective-permute-start(f32[4,2,16,256]{3,2,1,0:T(8,128)} %x_ref.1), channel_id=1, source_target_pairs={{16,32},{48,64},{80,96},{112,128},{144,160},{176,192},{208,224},{2... | collective-permute-start | bytes 393224 | tf_op jit(solution)/shard_map/ppermute | solution.py:450
  23.4 8.3 %collective-permute-start.1 = (f32[4,2,8,256]{3,2,1,0:T(8,128)S(1)}, f32[4,2,8,256]{3,2,1,0:T(8,128)S(1)}, u32[]{:S(2)}, u32[]{:S(2)}) collective-permute-start(f32[4,2,8,256]{3,2,1,0:T(8,128)S(1)} %get-tuple-element.36), channel_id=1, source_target_pairs={{32,80},{48,64},{96,144},{112,128},{160,208},{176,192},{224,272},{... | collective-permute-start | bytes 196616 | tf_op jit(solution)/shard_map/ppermute | solution.py:452
  28.0 6.2 %collective-permute-start.2 = (f32[4,2,8,256]{3,2,1,0:T(8,128)S(1)}, f32[4,2,8,256]{3,2,1,0:T(8,128)S(1)}, u32[]{:S(2)}, u32[]{:S(2)}) collective-permute-start(f32[4,2,8,256]{3,2,1,0:T(8,128)S(1)} %get-tuple-element.37), channel_id=1, source_target_pairs={{0,48},{16,32},{64,112},{80,96},{128,176},{144,160},{192,240},{208... | collective-permute-start | bytes 196616 | tf_op jit(solution)/shard_map/ppermute | solution.py:453
  36.3 23.8 %all-to-all-start.1 = ((f32[32,32,128]{2,1,0:T(8,128)}), f32[32,32,128]{2,1,0:T(8,128)S(1)}, u32[]{:S(2)}, u32[]{:S(2)}) async-start(f32[32,32,128]{2,1,0:T(8,128)} %columns.1), calls=%async_computation.1 | async-start | bytes 1048576 | tf_op jit(solution)/shard_map/all_to_all | solution.py:443
  42.3 13.6 %collective-permute-start.4 = (f32[6,2,16,256]{3,2,1,0:T(8,128)S(1)}, f32[6,2,16,256]{3,2,1,0:T(8,128)S(1)}, u32[]{:S(2)}, u32[]{:S(2)}) collective-permute-start(f32[6,2,16,256]{3,2,1,0:T(8,128)S(1)} %get-tuple-element.46), channel_id=1, source_target_pairs={{0,16},{32,48},{64,80},{96,112},{128,144},{160,176},{192,208},{224... | collective-permute-start | bytes 589832 | tf_op jit(solution)/shard_map/ppermute | solution.py:463
  44.6 11.0 %collective-permute-start.3 = (f32[2,2,16,256]{3,2,1,0:T(8,128)S(1)}, f32[2,2,16,256]{3,2,1,0:T(8,128)S(1)}, u32[]{:S(2)}, u32[]{:S(2)}) collective-permute-start(f32[2,2,16,256]{3,2,1,0:T(8,128)S(1)} %get-tuple-element.45), channel_id=1, source_target_pairs={{0,32},{32,64},{64,96},{96,128},{128,160},{160,192},{192,224},{224... | collective-permute-start | bytes 196616 | tf_op jit(solution)/shard_map/ppermute | solution.py:462

commit v11 on v10

--- a/solution.py
+++ b/solution.py
@@ -194,7 +194,7 @@
 
 
 def column_kernel(
-    wide_ref, reals_ref, own_ref, cross_ref, ring_ref, ghi_ref, glo_ref, o_ref, y_ref, hi_ref, lo_ref, hi2_ref, lo2_ref, z_ref, send_ref, out_sem
+    wide_ref, reals_ref, own_ref, ring_ref, cross_ref, ghi_ref, glo_ref, o_ref, y_ref, hi_ref, lo_ref, hi2_ref, lo2_ref, z_ref, send_ref, out_sem
 ):
     total, begin, side, before, here, after, odd = (
         taken(wide_ref, i) for i in (TOTAL, TEAM_BEGIN, SIDE, COUNTS + 1, COUNTS + 2, COUNTS + 3, ODD)
@@ -456,7 +456,7 @@
     wide_reals = jnp.broadcast_to(reals[:8, None], (8, 128))
     pair, edge = pair_call(ints, x, p1)
     own, pair, edge = lax.optimization_barrier((own, pair, edge))
-    back_sent = column_call(wide, wide_reals, own, cross_got, ring_got, vhi, vlo)
+    back_sent = column_call(wide, wide_reals, own, ring_got, cross_got, vhi, vlo)
     back_sent, pair, edge = lax.optimization_barrier((back_sent, pair, edge))
     back_got = exchange(back_sent)
     p2 = lax.ppermute(edge, hier, far)

time: 61.9 us -> 62.7 us (1.013)
  the two profiles are of different devices: /device:TPU:28 before, /device:TPU:34 now
where the time goes in v11:
time: 62.7 us; the launch traced here: 62.3 us
  starting transfers between devices  33 us (53%)
  waiting for transfers between devices  20.8 us (33%)
  Pallas kernels  6.7 us (11%)
  local copies, waits for them, and re-layouts  1.22 us (2%)
    all_to_all x2, starting transfers between devices, exchange(): lax.all_to_all(v, everyone, 0, 0, axis_index_groups=lists, tiled=True)  18.1 us
    all_to_all x2, waiting for transfers between devices, exchange(): lax.all_to_all(v, everyone, 0, 0, axis_index_groups=lists, tiled=True)  7.85 us
    ppermute x1, waiting for transfers between devices, on_device(): p2 = lax.ppermute(edge, hier, far)  7.51 us
    ppermute x1, waiting for transfers between devices, on_device(): cross_got = lax.ppermute(cross_edge, hier, cross)  5.09 us
    ppermute x1, starting transfers between devices, on_device(): p1 = lax.ppermute(x, hier, near)  3.53 us
    ppermute x1, starting transfers between devices, on_device(): p2 = lax.ppermute(edge, hier, far)  3.44 us
    ppermute x1, starting transfers between devices, on_device(): ring_got = lax.ppermute(ring_edge, hier, ring)  3.4 us
    ppermute x1, starting transfers between devices, on_device(): cross_got = lax.ppermute(cross_edge, hier, cross)  2.33 us
  transfers between devices with their start and end apart: 7, of which 5 were waited for; matrix products, arithmetic and copies ran while one was open for 1% of the time, Pallas kernels for 4%

profile of v11, /device:TPU:34, one launch (start us, length us, event | category | flops | bytes accessed | tf_op | source)
XLA Modules:
  0.0 62.3 jit_solution(9032191224570381690)
XLA Ops:
  0.0 1.0 %copy-done.1 = f32[4,2,16,256]{3,2,1,0:T(8,128)S(1)} copy-done((f32[4,2,16,256]{3,2,1,0:T(8,128)S(1)}, f32[4,2,16,256]{3,2,1,0:T(8,128)}, u32[]{:S(2)}) %copy-start.1) | copy-done | bytes 131096
  1.0 0.8 %own.1 = f32[32,8,128]{2,1,0:T(8,128)} custom-call(f32[128,256]{1,0:T(8,128)S(1)} %bitcast.3), custom_call_target="tpu_custom_call" | custom-call | flops 1000000 | bytes 4000000 | tf_op jit(solution)/shard_map/own/pallas_call | solution.py:448
  1.7 12.1 %all-to-all-start = ((f32[32,8,128]{2,1,0:T(8,128)}), f32[32,8,128]{2,1,0:T(8,128)S(1)}, u32[]{:S(2)}, u32[]{:S(2)}) async-start(f32[32,8,128]{2,1,0:T(8,128)} %own.1), calls=%async_computation | async-start | bytes 262144 | tf_op jit(solution)/shard_map/all_to_all | solution.py:443
  13.8 3.5 %collective-permute-start = (f32[4,2,16,256]{3,2,1,0:T(8,128)}, f32[4,2,16,256]{3,2,1,0:T(8,128)S(1)}, u32[]{:S(2)}, u32[]{:S(2)}) collective-permute-start(f32[4,2,16,256]{3,2,1,0:T(8,128)} %x_ref.1), channel_id=1, source_target_pairs={{16,32},{48,64},{80,96},{112,128},{144,160},{176,192},{208,224},{2... | collective-permute-start | bytes 393224 | tf_op jit(solution)/shard_map/ppermute | solution.py:450
  17.4 0.2 select_reduce_fusion
  17.7 0.1 reshape.68
  17.8 5.3 %all-to-all-done.got_ref = f32[32,8,128]{2,1,0:T(8,128)S(1)} async-done(((f32[32,8,128]{2,1,0:T(8,128)}), f32[32,8,128]{2,1,0:T(8,128)S(1)}, u32[]{:S(2)}, u32[]{:S(2)}) %all-to-all-start) | async-done | bytes 131104 | tf_op jit(solution)/shard_map/all_to_all | solution.py:443
  23.1 0.1 broadcast_in_dim.41.wide_ref
  23.1 0.2 edge.1
  23.4 3.4 %collective-permute-start.1 = (f32[4,2,8,256]{3,2,1,0:T(8,128)S(1)}, f32[4,2,8,256]{3,2,1,0:T(8,128)S(1)}, u32[]{:S(2)}, u32[]{:S(2)}) collective-permute-start(f32[4,2,8,256]{3,2,1,0:T(8,128)S(1)} %get-tuple-element.36), channel_id=1, source_target_pairs={{0,48},{16,32},{64,112},{80,96},{128,176},{144,160},{192,240},{208... | collective-permute-start | bytes 196616 | tf_op jit(solution)/shard_map/ppermute | solution.py:453
  26.8 2.3 %collective-permute-start.2 = (f32[4,2,8,256]{3,2,1,0:T(8,128)S(1)}, f32[4,2,8,256]{3,2,1,0:T(8,128)S(1)}, u32[]{:S(2)}, u32[]{:S(2)}) collective-permute-start(f32[4,2,8,256]{3,2,1,0:T(8,128)S(1)} %get-tuple-element.37), channel_id=1, source_target_pairs={{32,80},{48,64},{96,144},{112,128},{160,208},{176,192},{224,272},{... | collective-permute-start | bytes 196616 | tf_op jit(solution)/shard_map/ppermute | solution.py:452
  29.1 0.1 pad_maximum_fusion.reals_ref
  29.2 0.6 pair.1
  29.8 0.1 weights.1
  29.9 5.1 %collective-permute-done.2.cross_ref = f32[4,2,8,256]{3,2,1,0:T(8,128)S(1)} collective-permute-done((f32[4,2,8,256]{3,2,1,0:T(8,128)S(1)}, f32[4,2,8,256]{3,2,1,0:T(8,128)S(1)}, u32[]{:S(2)}, u32[]{:S(2)}) %collective-permute-start.2) | collective-permute-done | bytes 65568 | tf_op jit(solution)/shard_map/ppermute | solution.py:452
  35.1 2.0 %columns.1 = f32[32,32,128]{2,1,0:T(8,128)} custom-call(s32[16,128]{1,0:T(8,128)S(1)} %broadcast_in_dim.41.wide_ref, f32[8,128]{1,0:T(8,128)S(1)} %broadcast_in_dim.42.reals_ref, f32[8,2,8,256]{3,2,1,0:T(8,128)S(1)} %get-tuple-element.35.own_ref, f32[4,2,8,256]{3,2,1,0:T(8,128)S(1)} %collective-permute-done.1.ring_ref, ...), custom_call_target="tpu_custom_call" | custom-call | flops 1000000000 | bytes 4000000 | tf_op jit(solution)/shard_map/columns/pallas_call | solution.py:459
  37.1 6.0 %all-to-all-start.1 = ((f32[32,32,128]{2,1,0:T(8,128)}), f32[32,32,128]{2,1,0:T(8,128)S(1)}, u32[]{:S(2)}, u32[]{:S(2)}) async-start(f32[32,32,128]{2,1,0:T(8,128)} %columns.1), calls=%async_computation.1 | async-start | bytes 1048576 | tf_op jit(solution)/shard_map/all_to_all | solution.py:443
  43.2 2.3 %collective-permute-start.4 = (f32[6,2,16,256]{3,2,1,0:T(8,128)S(1)}, f32[6,2,16,256]{3,2,1,0:T(8,128)S(1)}, u32[]{:S(2)}, u32[]{:S(2)}) collective-permute-start(f32[6,2,16,256]{3,2,1,0:T(8,128)S(1)} %get-tuple-element.46), channel_id=1, source_target_pairs={{0,16},{32,48},{64,80},{96,112},{128,144},{160,176},{192,208},{224... | collective-permute-start | bytes 589832 | tf_op jit(solution)/shard_map/ppermute | solution.py:463
  45.4 3.4 %collective-permute-start.3 = (f32[2,2,16,256]{3,2,1,0:T(8,128)S(1)}, f32[2,2,16,256]{3,2,1,0:T(8,128)S(1)}, u32[]{:S(2)}, u32[]{:S(2)}) collective-permute-start(f32[2,2,16,256]{3,2,1,0:T(8,128)S(1)} %get-tuple-element.45), channel_id=1, source_target_pairs={{0,32},{32,64},{64,96},{96,128},{128,160},{160,192},{192,224},{224... | collective-permute-start | bytes 196616 | tf_op jit(solution)/shard_map/ppermute | solution.py:462
  48.9 7.5 %collective-permute-done.3.p2_ref = f32[2,2,16,256]{3,2,1,0:T(8,128)S(1)} collective-permute-done((f32[2,2,16,256]{3,2,1,0:T(8,128)S(1)}, f32[2,2,16,256]{3,2,1,0:T(8,128)S(1)}, u32[]{:S(2)}, u32[]{:S(2)}) %collective-permute-start.3) | collective-permute-done | bytes 65568 | tf_op jit(solution)/shard_map/ppermute | solution.py:462
  56.4 0.3 collective-permute-done.4.pair_ref
  56.7 1.7 %rows.1.base_ref = f32[128,256]{1,0:T(8,128)S(1)} custom-call(s32[16]{0:T(128)S(1)} %fusion.3.ints_ref.ints_in, f32[78]{0:T(128)S(1)} %pad_maximum_fusion.reals_ref, f32[4,2,16,256]{3,2,1,0:T(8,128)S(1)} %copy-done.2, f32[4,2,16,256]{3,2,1,0:T(8,128)S(1)} %collective-permute-done.near_ref.p1_ref, f32[2,2,16,256]{3,2,1,0:T(8,128)S(1)} %collective-permute-done.3.p2_ref, ...), custom_call_target="tpu_custom_call" | custom-call | flops 1000000000 | bytes 4000000 | tf_op jit(solution)/shard_map/rows/pallas_call | solution.py:464
  58.4 2.5 %all-to-all-done.1.got_ref = f32[32,32,128]{2,1,0:T(8,128)S(1)} async-done(((f32[32,32,128]{2,1,0:T(8,128)}), f32[32,32,128]{2,1,0:T(8,128)S(1)}, u32[]{:S(2)}, u32[]{:S(2)}) %all-to-all-start.1) | async-done | bytes 524320 | tf_op jit(solution)/shard_map/all_to_all | solution.py:443
  60.9 1.3 %finish.1 = f32[128,256]{1,0:T(8,128)} custom-call(s32[16]{0:T(128)S(1)} %fusion.3.ints_ref.ints_in, f32[32,32,128]{2,1,0:T(8,128)S(1)} %all-to-all-done.1.got_ref, f32[128,256]{1,0:T(8,128)S(1)} %rows.1.base_ref, bf16[256,768]{1,0:T(8,128)(2,1)S(1)} %get-tuple-element.47.ghi_ref, bf16[256,768]{1,0:T(8,128)(2,1)S(1)} %get-tuple-element.48.glo_ref), custom_call_target="tpu_custom_call" | custom-call | flops 300000000 | bytes 4000000 | tf_op jit(solution)/shard_map/finish/pallas_call | solution.py:465
  (22 shorter events, 0.1 us)
Async XLA Ops:
  0.0 29.8 %copy-start = (f32[2,256,256]{2,1,0:T(8,128)S(1)}, f32[2,256,256]{2,1,0:T(8,128)}, u32[]{:S(2)}) copy-start(f32[2,256,256]{2,1,0:T(8,128)} %q_ref) | copy-start | bytes 1572868
  0.0 1.0 %copy-start.1 = (f32[4,2,16,256]{3,2,1,0:T(8,128)S(1)}, f32[4,2,16,256]{3,2,1,0:T(8,128)}, u32[]{:S(2)}) copy-start(f32[4,2,16,256]{3,2,1,0:T(8,128)} %x_ref.1) | copy-start | bytes 393220
  1.7 15.7 %copy-start.4 = (s32[32]{0:T(128)S(1)}, s32[32]{0:T(128)}, u32[]{:S(2)}) copy-start(s32[32]{0:T(128)} %param.11) | copy-start | bytes 388
  1.7 15.9 %copy-start.6 = (f32[2,2]{1,0:T(2,128)S(1)}, f32[2,2]{1,0:T(2,128)}, u32[]{:S(2)}) copy-start(f32[2,2]{1,0:T(2,128)} %param.10) | copy-start | bytes 52
  1.7 27.4 %copy-start.5 = (f32[2]{0:T(128)S(1)}, f32[2]{0:T(128)}, u32[]{:S(2)}) copy-start(f32[2]{0:T(128)} %param.9) | copy-start | bytes 28
  1.7 21.3 %all-to-all-start = ((f32[32,8,128]{2,1,0:T(8,128)}), f32[32,8,128]{2,1,0:T(8,128)S(1)}, u32[]{:S(2)}, u32[]{:S(2)}) async-start(f32[32,8,128]{2,1,0:T(8,128)} %own.1), calls=%async_computation | async-start | bytes 262144 | tf_op jit(solution)/shard_map/all_to_all | solution.py:443
  13.8 15.4 %copy-start.2 = (f32[4,2,16,256]{3,2,1,0:T(8,128)S(1)}, f32[4,2,16,256]{3,2,1,0:T(8,128)}, u32[]{:S(2)}) copy-start(f32[4,2,16,256]{3,2,1,0:T(8,128)} %x_ref.1) | copy-start | bytes 393220
  13.8 16.0 %copy-start.3 = (f32[256,256]{1,0:T(8,128)S(1)}, f32[256,256]{1,0:T(8,128)}, u32[]{:S(2)}) copy-start(f32[256,256]{1,0:T(8,128)} %h_ref) | copy-start | bytes 786436
  13.8 15.4 %collective-permute-start = (f32[4,2,16,256]{3,2,1,0:T(8,128)}, f32[4,2,16,256]{3,2,1,0:T(8,128)S(1)}, u32[]{:S(2)}, u32[]{:S(2)}) collective-permute-start(f32[4,2,16,256]{3,2,1,0:T(8,128)} %x_ref.1), channel_id=1, source_target_pairs={{16,32},{48,64},{80,96},{112,128},{144,160},{176,192},{208,224},{2... | collective-permute-start | bytes 393224 | tf_op jit(solution)/shard_map/ppermute | solution.py:450
  23.4 6.6 %collective-permute-start.1 = (f32[4,2,8,256]{3,2,1,0:T(8,128)S(1)}, f32[4,2,8,256]{3,2,1,0:T(8,128)S(1)}, u32[]{:S(2)}, u32[]{:S(2)}) collective-permute-start(f32[4,2,8,256]{3,2,1,0:T(8,128)S(1)} %get-tuple-element.36), channel_id=1, source_target_pairs={{0,48},{16,32},{64,112},{80,96},{128,176},{144,160},{192,240},{208... | collective-permute-start | bytes 196616 | tf_op jit(solution)/shard_map/ppermute | solution.py:453
  26.8 8.3 %collective-permute-start.2 = (f32[4,2,8,256]{3,2,1,0:T(8,128)S(1)}, f32[4,2,8,256]{3,2,1,0:T(8,128)S(1)}, u32[]{:S(2)}, u32[]{:S(2)}) collective-permute-start(f32[4,2,8,256]{3,2,1,0:T(8,128)S(1)} %get-tuple-element.37), channel_id=1, source_target_pairs={{32,80},{48,64},{96,144},{112,128},{160,208},{176,192},{224,272},{... | collective-permute-start | bytes 196616 | tf_op jit(solution)/shard_map/ppermute | solution.py:452
  37.1 23.8 %all-to-all-start.1 = ((f32[32,32,128]{2,1,0:T(8,128)}), f32[32,32,128]{2,1,0:T(8,128)S(1)}, u32[]{:S(2)}, u32[]{:S(2)}) async-start(f32[32,32,128]{2,1,0:T(8,128)} %columns.1), calls=%async_computation.1 | async-start | bytes 1048576 | tf_op jit(solution)/shard_map/all_to_all | solution.py:443
  43.2 13.6 %collective-permute-start.4 = (f32[6,2,16,256]{3,2,1,0:T(8,128)S(1)}, f32[6,2,16,256]{3,2,1,0:T(8,128)S(1)}, u32[]{:S(2)}, u32[]{:S(2)}) collective-permute-start(f32[6,2,16,256]{3,2,1,0:T(8,128)S(1)} %get-tuple-element.46), channel_id=1, source_target_pairs={{0,16},{32,48},{64,80},{96,112},{128,144},{160,176},{192,208},{224... | collective-permute-start | bytes 589832 | tf_op jit(solution)/shard_map/ppermute | solution.py:463
  45.4 11.0 %collective-permute-start.3 = (f32[2,2,16,256]{3,2,1,0:T(8,128)S(1)}, f32[2,2,16,256]{3,2,1,0:T(8,128)S(1)}, u32[]{:S(2)}, u32[]{:S(2)}) collective-permute-start(f32[2,2,16,256]{3,2,1,0:T(8,128)S(1)} %get-tuple-element.45), channel_id=1, source_target_pairs={{0,32},{32,64},{64,96},{96,128},{128,160},{160,192},{192,224},{224... | collective-permute-start | bytes 196616 | tf_op jit(solution)/shard_map/ppermute | solution.py:462

commit v12 on v10

--- a/solution.py
+++ b/solution.py
@@ -135,7 +135,9 @@
 
 
 def product(hi, lo, ghi, glo):
-    return dot(hi, ghi) + dot(lo, ghi) + dot(hi, glo)
+    rows = hi.shape[0]
+    both_parts = dot(jnp.concatenate([hi, lo], axis=0), ghi)
+    return both_parts[:rows] + both_parts[rows:] + dot(hi, glo)
 
 
 def times_weights(hi_ref, lo_ref, ghi_ref, glo_ref):
@@ -151,8 +153,18 @@
         hlo[:, 256 * b : 256 * b + 256] = lo
 
 
-def own_kernel(x_ref, o_ref):
-    o_ref[...] = x_ref[...].T.reshape(32, 8, 128)
+def own_kernel(x_ref, o_ref, v_ref, t_ref, in_sem, out_sem):
+    copies = [pltpu.make_async_copy(x_ref.at[i], v_ref.at[i], in_sem.at[i]) for i in range(4)]
+    for copy in copies:
+        copy.start()
+    for copy in copies:
+        copy.wait()
+    t_ref[...] = v_ref[...].reshape(128, 256).T.reshape(32, 8, 128)
+    copies = [pltpu.make_async_copy(t_ref.at[pl.ds(8 * i, 8)], o_ref.at[pl.ds(8 * i, 8)], out_sem.at[i]) for i in range(4)]
+    for copy in copies:
+        copy.start()
+    for copy in copies:
+        copy.wait()
 
 
 def fetch(pairs, sem):
@@ -247,8 +259,8 @@
         copy.start()
         return copy
 
+    copies = [send(z) for z in range(1, 4)]
     last = times_weights(hi2_ref, lo2_ref, ghi_ref, glo_ref)
-    copies = [send(z) for z in range(1, 4)]
     z_ref[0] = last.reshape(8, 2, 8, 256)
     for copy in [*copies, send(0)]:
         copy.wait()
@@ -350,7 +362,19 @@
     [VMEM] * 2,
     name="weights",
 )
-own_call = call(own_kernel, struct((32, 8, 128)), [VMEM], name="own")
+own_call = call(
+    own_kernel,
+    struct((32, 8, 128)),
+    [ANY],
+    [
+        pltpu.VMEM((4, 2, 16, 256), F32),
+        pltpu.VMEM((32, 8, 128), F32),
+        pltpu.SemaphoreType.DMA((4,)),
+        pltpu.SemaphoreType.DMA((4,)),
+    ],
+    out_specs=ANY,
+    name="own",
+)
 INTS = pltpu.SMEM((16,), jnp.int32)
 edge_call = call(
     edge_kernel,
@@ -445,7 +469,7 @@
     ints = integers(node_count)
     wide = jnp.broadcast_to(ints[:, None], (16, 128))
     reals = jnp.concatenate([gamma, coeff.reshape(4), jnp.sqrt(jnp.arange(ROOTS, dtype=F32))])
-    sent, x = lax.optimization_barrier((own_call(densities.reshape(128, 256)), densities))
+    sent, x = lax.optimization_barrier((own_call(densities), densities))
     got = exchange(sent)
     p1 = lax.ppermute(x, hier, near)
     own, ring_edge, cross_edge = edge_call(wide, got)

time: 61.9 us -> 62 us (level)
  no operation moved by 1% of the time
where the time goes in v12:
time: 62 us; the launch traced here: 61.6 us
  starting transfers between devices  33.9 us (55%)
  waiting for transfers between devices  19.1 us (31%)
  Pallas kernels  6.83 us (11%)
  local copies, waits for them, and re-layouts  1.17 us (2%)
    all_to_all x2, starting transfers between devices, exchange(): lax.all_to_all(v, everyone, 0, 0, axis_index_groups=lists, tiled=True)  18.1 us
    all_to_all x2, waiting for transfers between devices, exchange(): lax.all_to_all(v, everyone, 0, 0, axis_index_groups=lists, tiled=True)  8.83 us
    ppermute x1, waiting for transfers between devices, on_device(): p2 = lax.ppermute(edge, hier, far)  6.64 us
    ppermute x1, starting transfers between devices, on_device(): cross_got = lax.ppermute(cross_edge, hier, cross)  4.67 us
    ppermute x1, starting transfers between devices, on_device(): p2 = lax.ppermute(edge, hier, far)  4.4 us
    ppermute x1, starting transfers between devices, on_device(): p1 = lax.ppermute(x, hier, near)  2.58 us
    ppermute x1, waiting for transfers between devices, on_device(): ring_got = lax.ppermute(ring_edge, hier, ring)  2.56 us
    ppermute x1, starting transfers between devices, on_device(): pair = lax.ppermute(pair, hier, inner)  2.26 us
  transfers between devices with their start and end apart: 7, of which 6 were waited for; matrix products, arithmetic and copies ran while one was open for 1% of the time, Pallas kernels for 4%

profile of v12, /device:TPU:28, one launch (start us, length us, event | category | flops | bytes accessed | tf_op | source)
XLA Modules:
  0.0 61.6 jit_solution(14700348936082079956)
XLA Ops:
  0.0 0.9 %copy-done.1 = f32[4,2,16,256]{3,2,1,0:T(8,128)S(1)} copy-done((f32[4,2,16,256]{3,2,1,0:T(8,128)S(1)}, f32[4,2,16,256]{3,2,1,0:T(8,128)}, u32[]{:S(2)}) %copy-start.1) | copy-done | bytes 131096
  0.9 1.0 %own.1 = f32[32,8,128]{2,1,0:T(8,128)} custom-call(f32[4,2,16,256]{3,2,1,0:T(8,128)S(1)} %copy-done.1), custom_call_target="tpu_custom_call" | custom-call | flops 1000000 | bytes 4000000 | tf_op jit(solution)/shard_map/own/pallas_call | solution.py:472
  1.9 12.1 %all-to-all-start = ((f32[32,8,128]{2,1,0:T(8,128)}), f32[32,8,128]{2,1,0:T(8,128)S(1)}, u32[]{:S(2)}, u32[]{:S(2)}) async-start(f32[32,8,128]{2,1,0:T(8,128)} %own.1), calls=%async_computation | async-start | bytes 262144 | tf_op jit(solution)/shard_map/all_to_all | solution.py:467
  14.0 2.6 %collective-permute-start = (f32[4,2,16,256]{3,2,1,0:T(8,128)}, f32[4,2,16,256]{3,2,1,0:T(8,128)S(1)}, u32[]{:S(2)}, u32[]{:S(2)}) collective-permute-start(f32[4,2,16,256]{3,2,1,0:T(8,128)} %x_ref.3), channel_id=1, source_target_pairs={{16,32},{48,64},{80,96},{112,128},{144,160},{176,192},{208,224},{2... | collective-permute-start | bytes 393224 | tf_op jit(solution)/shard_map/ppermute | solution.py:474
  16.7 0.2 select_reduce_fusion
  16.9 0.1 reshape.65
  17.0 6.3 %all-to-all-done.got_ref = f32[32,8,128]{2,1,0:T(8,128)S(1)} async-done(((f32[32,8,128]{2,1,0:T(8,128)}), f32[32,8,128]{2,1,0:T(8,128)S(1)}, u32[]{:S(2)}, u32[]{:S(2)}) %all-to-all-start) | async-done | bytes 131104 | tf_op jit(solution)/shard_map/all_to_all | solution.py:467
  23.3 0.2 edge.1
  23.6 4.7 %collective-permute-start.1 = (f32[4,2,8,256]{3,2,1,0:T(8,128)S(1)}, f32[4,2,8,256]{3,2,1,0:T(8,128)S(1)}, u32[]{:S(2)}, u32[]{:S(2)}) collective-permute-start(f32[4,2,8,256]{3,2,1,0:T(8,128)S(1)} %get-tuple-element.36), channel_id=1, source_target_pairs={{32,80},{48,64},{96,144},{112,128},{160,208},{176,192},{224,272},{... | collective-permute-start | bytes 196616 | tf_op jit(solution)/shard_map/ppermute | solution.py:476
  28.2 1.9 %collective-permute-start.2 = (f32[4,2,8,256]{3,2,1,0:T(8,128)S(1)}, f32[4,2,8,256]{3,2,1,0:T(8,128)S(1)}, u32[]{:S(2)}, u32[]{:S(2)}) collective-permute-start(f32[4,2,8,256]{3,2,1,0:T(8,128)S(1)} %get-tuple-element.37), channel_id=1, source_target_pairs={{0,48},{16,32},{64,112},{80,96},{128,176},{144,160},{192,240},{208... | collective-permute-start | bytes 196616 | tf_op jit(solution)/shard_map/ppermute | solution.py:477
  30.2 0.1 pad_maximum_fusion.reals_ref
  30.2 0.6 pair.1
  30.8 0.1 weights.1
  31.0 0.8 %collective-permute-done.1.cross_ref = f32[4,2,8,256]{3,2,1,0:T(8,128)S(1)} collective-permute-done((f32[4,2,8,256]{3,2,1,0:T(8,128)S(1)}, f32[4,2,8,256]{3,2,1,0:T(8,128)S(1)}, u32[]{:S(2)}, u32[]{:S(2)}) %collective-permute-start.1) | collective-permute-done | bytes 65568 | tf_op jit(solution)/shard_map/ppermute | solution.py:476
  31.8 2.6 %collective-permute-done.2.ring_ref = f32[4,2,8,256]{3,2,1,0:T(8,128)S(1)} collective-permute-done((f32[4,2,8,256]{3,2,1,0:T(8,128)S(1)}, f32[4,2,8,256]{3,2,1,0:T(8,128)S(1)}, u32[]{:S(2)}, u32[]{:S(2)}) %collective-permute-start.2) | collective-permute-done | bytes 65568 | tf_op jit(solution)/shard_map/ppermute | solution.py:477
  34.5 2.0 %columns.1 = f32[32,32,128]{2,1,0:T(8,128)} custom-call(s32[16,128]{1,0:T(8,128)S(1)} %broadcast_in_dim.41.wide_ref, f32[8,128]{1,0:T(8,128)S(1)} %broadcast_in_dim.42.reals_ref, f32[8,2,8,256]{3,2,1,0:T(8,128)S(1)} %get-tuple-element.35.own_ref, f32[4,2,8,256]{3,2,1,0:T(8,128)S(1)} %collective-permute-done.1.cross_ref, ...), custom_call_target="tpu_custom_call" | custom-call | flops 1000000000 | bytes 4000000 | tf_op jit(solution)/shard_map/columns/pallas_call | solution.py:483
  36.5 6.0 %all-to-all-start.1 = ((f32[32,32,128]{2,1,0:T(8,128)}), f32[32,32,128]{2,1,0:T(8,128)S(1)}, u32[]{:S(2)}, u32[]{:S(2)}) async-start(f32[32,32,128]{2,1,0:T(8,128)} %columns.1), calls=%async_computation.1 | async-start | bytes 1048576 | tf_op jit(solution)/shard_map/all_to_all | solution.py:467
  42.5 2.3 %collective-permute-start.4 = (f32[6,2,16,256]{3,2,1,0:T(8,128)S(1)}, f32[6,2,16,256]{3,2,1,0:T(8,128)S(1)}, u32[]{:S(2)}, u32[]{:S(2)}) collective-permute-start(f32[6,2,16,256]{3,2,1,0:T(8,128)S(1)} %get-tuple-element.46), channel_id=1, source_target_pairs={{0,16},{32,48},{64,80},{96,112},{128,144},{160,176},{192,208},{224... | collective-permute-start | bytes 589832 | tf_op jit(solution)/shard_map/ppermute | solution.py:487
  44.7 4.4 %collective-permute-start.3 = (f32[2,2,16,256]{3,2,1,0:T(8,128)S(1)}, f32[2,2,16,256]{3,2,1,0:T(8,128)S(1)}, u32[]{:S(2)}, u32[]{:S(2)}) collective-permute-start(f32[2,2,16,256]{3,2,1,0:T(8,128)S(1)} %get-tuple-element.45), channel_id=1, source_target_pairs={{0,32},{32,64},{64,96},{96,128},{128,160},{160,192},{192,224},{224... | collective-permute-start | bytes 196616 | tf_op jit(solution)/shard_map/ppermute | solution.py:486
  49.1 6.6 %collective-permute-done.3.p2_ref = f32[2,2,16,256]{3,2,1,0:T(8,128)S(1)} collective-permute-done((f32[2,2,16,256]{3,2,1,0:T(8,128)S(1)}, f32[2,2,16,256]{3,2,1,0:T(8,128)S(1)}, u32[]{:S(2)}, u32[]{:S(2)}) %collective-permute-start.3) | collective-permute-done | bytes 65568 | tf_op jit(solution)/shard_map/ppermute | solution.py:486
  55.8 0.3 collective-permute-done.4.pair_ref
  56.0 1.7 %rows.1.base_ref = f32[128,256]{1,0:T(8,128)S(1)} custom-call(s32[16]{0:T(128)S(1)} %fusion.3.ints_ref.ints_in, f32[78]{0:T(128)S(1)} %pad_maximum_fusion.reals_ref, f32[4,2,16,256]{3,2,1,0:T(8,128)S(1)} %copy-done.2, f32[4,2,16,256]{3,2,1,0:T(8,128)S(1)} %collective-permute-done.near_ref.p1_ref, f32[2,2,16,256]{3,2,1,0:T(8,128)S(1)} %collective-permute-done.3.p2_ref, ...), custom_call_target="tpu_custom_call" | custom-call | flops 1000000000 | bytes 4000000 | tf_op jit(solution)/shard_map/rows/pallas_call | solution.py:488
  57.7 2.5 %all-to-all-done.1.got_ref = f32[32,32,128]{2,1,0:T(8,128)S(1)} async-done(((f32[32,32,128]{2,1,0:T(8,128)}), f32[32,32,128]{2,1,0:T(8,128)S(1)}, u32[]{:S(2)}, u32[]{:S(2)}) %all-to-all-start.1) | async-done | bytes 524320 | tf_op jit(solution)/shard_map/all_to_all | solution.py:467
  60.2 1.3 %finish.1 = f32[128,256]{1,0:T(8,128)} custom-call(s32[16]{0:T(128)S(1)} %fusion.3.ints_ref.ints_in, f32[32,32,128]{2,1,0:T(8,128)S(1)} %all-to-all-done.1.got_ref, f32[128,256]{1,0:T(8,128)S(1)} %rows.1.base_ref, bf16[256,768]{1,0:T(8,128)(2,1)S(1)} %get-tuple-element.47.ghi_ref, bf16[256,768]{1,0:T(8,128)(2,1)S(1)} %get-tuple-element.48.glo_ref), custom_call_target="tpu_custom_call" | custom-call | flops 300000000 | bytes 4000000 | tf_op jit(solution)/shard_map/finish/pallas_call | solution.py:489
  (22 shorter events, 0.2 us)
Async XLA Ops:
  0.0 0.9 %copy-start.1 = (f32[4,2,16,256]{3,2,1,0:T(8,128)S(1)}, f32[4,2,16,256]{3,2,1,0:T(8,128)}, u32[]{:S(2)}) copy-start(f32[4,2,16,256]{3,2,1,0:T(8,128)} %x_ref.3) | copy-start | bytes 393220
  0.9 29.9 %copy-start = (f32[2,256,256]{2,1,0:T(8,128)S(1)}, f32[2,256,256]{2,1,0:T(8,128)}, u32[]{:S(2)}) copy-start(f32[2,256,256]{2,1,0:T(8,128)} %q_ref) | copy-start | bytes 1572868
  1.9 14.8 %copy-start.4 = (s32[32]{0:T(128)S(1)}, s32[32]{0:T(128)}, u32[]{:S(2)}) copy-start(s32[32]{0:T(128)} %param.11) | copy-start | bytes 388
  1.9 15.0 %copy-start.6 = (f32[2,2]{1,0:T(2,128)S(1)}, f32[2,2]{1,0:T(2,128)}, u32[]{:S(2)}) copy-start(f32[2,2]{1,0:T(2,128)} %param.10) | copy-start | bytes 52
  1.9 28.3 %copy-start.5 = (f32[2]{0:T(128)S(1)}, f32[2]{0:T(128)}, u32[]{:S(2)}) copy-start(f32[2]{0:T(128)} %param.9) | copy-start | bytes 28
  1.9 21.4 %all-to-all-start = ((f32[32,8,128]{2,1,0:T(8,128)}), f32[32,8,128]{2,1,0:T(8,128)S(1)}, u32[]{:S(2)}, u32[]{:S(2)}) async-start(f32[32,8,128]{2,1,0:T(8,128)} %own.1), calls=%async_computation | async-start | bytes 262144 | tf_op jit(solution)/shard_map/all_to_all | solution.py:467
  14.0 16.2 %copy-start.2 = (f32[4,2,16,256]{3,2,1,0:T(8,128)S(1)}, f32[4,2,16,256]{3,2,1,0:T(8,128)}, u32[]{:S(2)}) copy-start(f32[4,2,16,256]{3,2,1,0:T(8,128)} %x_ref.3) | copy-start | bytes 393220
  14.0 16.8 %copy-start.3 = (f32[256,256]{1,0:T(8,128)S(1)}, f32[256,256]{1,0:T(8,128)}, u32[]{:S(2)}) copy-start(f32[256,256]{1,0:T(8,128)} %h_ref) | copy-start | bytes 786436
  14.0 16.2 %collective-permute-start = (f32[4,2,16,256]{3,2,1,0:T(8,128)}, f32[4,2,16,256]{3,2,1,0:T(8,128)S(1)}, u32[]{:S(2)}, u32[]{:S(2)}) collective-permute-start(f32[4,2,16,256]{3,2,1,0:T(8,128)} %x_ref.3), channel_id=1, source_target_pairs={{16,32},{48,64},{80,96},{112,128},{144,160},{176,192},{208,224},{2... | collective-permute-start | bytes 393224 | tf_op jit(solution)/shard_map/ppermute | solution.py:474
  23.6 8.3 %collective-permute-start.1 = (f32[4,2,8,256]{3,2,1,0:T(8,128)S(1)}, f32[4,2,8,256]{3,2,1,0:T(8,128)S(1)}, u32[]{:S(2)}, u32[]{:S(2)}) collective-permute-start(f32[4,2,8,256]{3,2,1,0:T(8,128)S(1)} %get-tuple-element.36), channel_id=1, source_target_pairs={{32,80},{48,64},{96,144},{112,128},{160,208},{176,192},{224,272},{... | collective-permute-start | bytes 196616 | tf_op jit(solution)/shard_map/ppermute | solution.py:476
  28.2 6.2 %collective-permute-start.2 = (f32[4,2,8,256]{3,2,1,0:T(8,128)S(1)}, f32[4,2,8,256]{3,2,1,0:T(8,128)S(1)}, u32[]{:S(2)}, u32[]{:S(2)}) collective-permute-start(f32[4,2,8,256]{3,2,1,0:T(8,128)S(1)} %get-tuple-element.37), channel_id=1, source_target_pairs={{0,48},{16,32},{64,112},{80,96},{128,176},{144,160},{192,240},{208... | collective-permute-start | bytes 196616 | tf_op jit(solution)/shard_map/ppermute | solution.py:477
  36.5 23.8 %all-to-all-start.1 = ((f32[32,32,128]{2,1,0:T(8,128)}), f32[32,32,128]{2,1,0:T(8,128)S(1)}, u32[]{:S(2)}, u32[]{:S(2)}) async-start(f32[32,32,128]{2,1,0:T(8,128)} %columns.1), calls=%async_computation.1 | async-start | bytes 1048576 | tf_op jit(solution)/shard_map/all_to_all | solution.py:467
  42.5 13.6 %collective-permute-start.4 = (f32[6,2,16,256]{3,2,1,0:T(8,128)S(1)}, f32[6,2,16,256]{3,2,1,0:T(8,128)S(1)}, u32[]{:S(2)}, u32[]{:S(2)}) collective-permute-start(f32[6,2,16,256]{3,2,1,0:T(8,128)S(1)} %get-tuple-element.46), channel_id=1, source_target_pairs={{0,16},{32,48},{64,80},{96,112},{128,144},{160,176},{192,208},{224... | collective-permute-start | bytes 589832 | tf_op jit(solution)/shard_map/ppermute | solution.py:487
  44.7 11.0 %collective-permute-start.3 = (f32[2,2,16,256]{3,2,1,0:T(8,128)S(1)}, f32[2,2,16,256]{3,2,1,0:T(8,128)S(1)}, u32[]{:S(2)}, u32[]{:S(2)}) collective-permute-start(f32[2,2,16,256]{3,2,1,0:T(8,128)S(1)} %get-tuple-element.45), channel_id=1, source_target_pairs={{0,32},{32,64},{64,96},{96,128},{128,160},{160,192},{192,224},{224... | collective-permute-start | bytes 196616 | tf_op jit(solution)/shard_map/ppermute | solution.py:486

commit v13 on v10

--- a/solution.py
+++ b/solution.py
@@ -135,7 +135,9 @@
 
 
 def product(hi, lo, ghi, glo):
-    return dot(hi, ghi) + dot(lo, ghi) + dot(hi, glo)
+    rows = hi.shape[0]
+    both_parts = dot(jnp.concatenate([hi, lo], axis=0), ghi)
+    return both_parts[:rows] + both_parts[rows:] + dot(hi, glo)
 
 
 def times_weights(hi_ref, lo_ref, ghi_ref, glo_ref):
@@ -247,8 +249,8 @@
         copy.start()
         return copy
 
+    copies = [send(z) for z in range(1, 4)]
     last = times_weights(hi2_ref, lo2_ref, ghi_ref, glo_ref)
-    copies = [send(z) for z in range(1, 4)]
     z_ref[0] = last.reshape(8, 2, 8, 256)
     for copy in [*copies, send(0)]:
         copy.wait()

time: 61.9 us -> 61.8 us (level)
  no operation moved by 1% of the time
where the time goes in v13:
time: 61.8 us; the launch traced here: 61.4 us
  starting transfers between devices  33.9 us (55%)
  waiting for transfers between devices  19.1 us (31%)
  Pallas kernels  6.62 us (11%)
  local copies, waits for them, and re-layouts  1.22 us (2%)
    all_to_all x2, starting transfers between devices, exchange(): lax.all_to_all(v, everyone, 0, 0, axis_index_groups=lists, tiled=True)  18.1 us
    all_to_all x2, waiting for transfers between devices, exchange(): lax.all_to_all(v, everyone, 0, 0, axis_index_groups=lists, tiled=True)  8.83 us
    ppermute x1, waiting for transfers between devices, on_device(): p2 = lax.ppermute(edge, hier, far)  6.64 us
    ppermute x1, starting transfers between devices, on_device(): cross_got = lax.ppermute(cross_edge, hier, cross)  4.67 us
    ppermute x1, starting transfers between devices, on_device(): p2 = lax.ppermute(edge, hier, far)  4.41 us
    ppermute x1, starting transfers between devices, on_device(): p1 = lax.ppermute(x, hier, near)  2.58 us
    ppermute x1, waiting for transfers between devices, on_device(): ring_got = lax.ppermute(ring_edge, hier, ring)  2.56 us
    ppermute x1, starting transfers between devices, on_device(): pair = lax.ppermute(pair, hier, inner)  2.26 us
  transfers between devices with their start and end apart: 7, of which 6 were waited for; matrix products, arithmetic and copies ran while one was open for 1% of the time, Pallas kernels for 4%

profile of v13, /device:TPU:28, one launch (start us, length us, event | category | flops | bytes accessed | tf_op | source)
XLA Modules:
  0.0 61.4 jit_solution(5065210832983174460)
XLA Ops:
  0.0 1.0 %copy-done.1 = f32[4,2,16,256]{3,2,1,0:T(8,128)S(1)} copy-done((f32[4,2,16,256]{3,2,1,0:T(8,128)S(1)}, f32[4,2,16,256]{3,2,1,0:T(8,128)}, u32[]{:S(2)}) %copy-start.1) | copy-done | bytes 131096
  1.0 0.8 %own.1 = f32[32,8,128]{2,1,0:T(8,128)} custom-call(f32[128,256]{1,0:T(8,128)S(1)} %bitcast.3), custom_call_target="tpu_custom_call" | custom-call | flops 1000000 | bytes 4000000 | tf_op jit(solution)/shard_map/own/pallas_call | solution.py:450
  1.7 12.1 %all-to-all-start = ((f32[32,8,128]{2,1,0:T(8,128)}), f32[32,8,128]{2,1,0:T(8,128)S(1)}, u32[]{:S(2)}, u32[]{:S(2)}) async-start(f32[32,8,128]{2,1,0:T(8,128)} %own.1), calls=%async_computation | async-start | bytes 262144 | tf_op jit(solution)/shard_map/all_to_all | solution.py:445
  13.8 2.6 %collective-permute-start = (f32[4,2,16,256]{3,2,1,0:T(8,128)}, f32[4,2,16,256]{3,2,1,0:T(8,128)S(1)}, u32[]{:S(2)}, u32[]{:S(2)}) collective-permute-start(f32[4,2,16,256]{3,2,1,0:T(8,128)} %x_ref.1), channel_id=1, source_target_pairs={{16,32},{48,64},{80,96},{112,128},{144,160},{176,192},{208,224},{2... | collective-permute-start | bytes 393224 | tf_op jit(solution)/shard_map/ppermute | solution.py:452
  16.5 0.2 select_reduce_fusion
  16.7 0.1 reshape.68
  16.8 6.3 %all-to-all-done.got_ref = f32[32,8,128]{2,1,0:T(8,128)S(1)} async-done(((f32[32,8,128]{2,1,0:T(8,128)}), f32[32,8,128]{2,1,0:T(8,128)S(1)}, u32[]{:S(2)}, u32[]{:S(2)}) %all-to-all-start) | async-done | bytes 131104 | tf_op jit(solution)/shard_map/all_to_all | solution.py:445
  23.1 0.2 edge.1
  23.4 4.7 %collective-permute-start.1 = (f32[4,2,8,256]{3,2,1,0:T(8,128)S(1)}, f32[4,2,8,256]{3,2,1,0:T(8,128)S(1)}, u32[]{:S(2)}, u32[]{:S(2)}) collective-permute-start(f32[4,2,8,256]{3,2,1,0:T(8,128)S(1)} %get-tuple-element.36), channel_id=1, source_target_pairs={{32,80},{48,64},{96,144},{112,128},{160,208},{176,192},{224,272},{... | collective-permute-start | bytes 196616 | tf_op jit(solution)/shard_map/ppermute | solution.py:454
  28.0 1.9 %collective-permute-start.2 = (f32[4,2,8,256]{3,2,1,0:T(8,128)S(1)}, f32[4,2,8,256]{3,2,1,0:T(8,128)S(1)}, u32[]{:S(2)}, u32[]{:S(2)}) collective-permute-start(f32[4,2,8,256]{3,2,1,0:T(8,128)S(1)} %get-tuple-element.37), channel_id=1, source_target_pairs={{0,48},{16,32},{64,112},{80,96},{128,176},{144,160},{192,240},{208... | collective-permute-start | bytes 196616 | tf_op jit(solution)/shard_map/ppermute | solution.py:455
  30.0 0.1 pad_maximum_fusion.reals_ref
  30.0 0.6 pair.1
  30.6 0.1 weights.1
  30.8 0.8 %collective-permute-done.1.cross_ref = f32[4,2,8,256]{3,2,1,0:T(8,128)S(1)} collective-permute-done((f32[4,2,8,256]{3,2,1,0:T(8,128)S(1)}, f32[4,2,8,256]{3,2,1,0:T(8,128)S(1)}, u32[]{:S(2)}, u32[]{:S(2)}) %collective-permute-start.1) | collective-permute-done | bytes 65568 | tf_op jit(solution)/shard_map/ppermute | solution.py:454
  31.6 2.6 %collective-permute-done.2.ring_ref = f32[4,2,8,256]{3,2,1,0:T(8,128)S(1)} collective-permute-done((f32[4,2,8,256]{3,2,1,0:T(8,128)S(1)}, f32[4,2,8,256]{3,2,1,0:T(8,128)S(1)}, u32[]{:S(2)}, u32[]{:S(2)}) %collective-permute-start.2) | collective-permute-done | bytes 65568 | tf_op jit(solution)/shard_map/ppermute | solution.py:455
  34.3 2.0 %columns.1 = f32[32,32,128]{2,1,0:T(8,128)} custom-call(s32[16,128]{1,0:T(8,128)S(1)} %broadcast_in_dim.41.wide_ref, f32[8,128]{1,0:T(8,128)S(1)} %broadcast_in_dim.42.reals_ref, f32[8,2,8,256]{3,2,1,0:T(8,128)S(1)} %get-tuple-element.35.own_ref, f32[4,2,8,256]{3,2,1,0:T(8,128)S(1)} %collective-permute-done.1.cross_ref, ...), custom_call_target="tpu_custom_call" | custom-call | flops 1000000000 | bytes 4000000 | tf_op jit(solution)/shard_map/columns/pallas_call | solution.py:461
  36.3 6.0 %all-to-all-start.1 = ((f32[32,32,128]{2,1,0:T(8,128)}), f32[32,32,128]{2,1,0:T(8,128)S(1)}, u32[]{:S(2)}, u32[]{:S(2)}) async-start(f32[32,32,128]{2,1,0:T(8,128)} %columns.1), calls=%async_computation.1 | async-start | bytes 1048576 | tf_op jit(solution)/shard_map/all_to_all | solution.py:445
  42.3 2.3 %collective-permute-start.4 = (f32[6,2,16,256]{3,2,1,0:T(8,128)S(1)}, f32[6,2,16,256]{3,2,1,0:T(8,128)S(1)}, u32[]{:S(2)}, u32[]{:S(2)}) collective-permute-start(f32[6,2,16,256]{3,2,1,0:T(8,128)S(1)} %get-tuple-element.46), channel_id=1, source_target_pairs={{0,16},{32,48},{64,80},{96,112},{128,144},{160,176},{192,208},{224... | collective-permute-start | bytes 589832 | tf_op jit(solution)/shard_map/ppermute | solution.py:465
  44.5 4.4 %collective-permute-start.3 = (f32[2,2,16,256]{3,2,1,0:T(8,128)S(1)}, f32[2,2,16,256]{3,2,1,0:T(8,128)S(1)}, u32[]{:S(2)}, u32[]{:S(2)}) collective-permute-start(f32[2,2,16,256]{3,2,1,0:T(8,128)S(1)} %get-tuple-element.45), channel_id=1, source_target_pairs={{0,32},{32,64},{64,96},{96,128},{128,160},{160,192},{192,224},{224... | collective-permute-start | bytes 196616 | tf_op jit(solution)/shard_map/ppermute | solution.py:464
  48.9 6.6 %collective-permute-done.3.p2_ref = f32[2,2,16,256]{3,2,1,0:T(8,128)S(1)} collective-permute-done((f32[2,2,16,256]{3,2,1,0:T(8,128)S(1)}, f32[2,2,16,256]{3,2,1,0:T(8,128)S(1)}, u32[]{:S(2)}, u32[]{:S(2)}) %collective-permute-start.3) | collective-permute-done | bytes 65568 | tf_op jit(solution)/shard_map/ppermute | solution.py:464
  55.6 0.3 collective-permute-done.4.pair_ref
  55.8 1.7 %rows.1.base_ref = f32[128,256]{1,0:T(8,128)S(1)} custom-call(s32[16]{0:T(128)S(1)} %fusion.3.ints_ref.ints_in, f32[78]{0:T(128)S(1)} %pad_maximum_fusion.reals_ref, f32[4,2,16,256]{3,2,1,0:T(8,128)S(1)} %copy-done.2, f32[4,2,16,256]{3,2,1,0:T(8,128)S(1)} %collective-permute-done.near_ref.p1_ref, f32[2,2,16,256]{3,2,1,0:T(8,128)S(1)} %collective-permute-done.3.p2_ref, ...), custom_call_target="tpu_custom_call" | custom-call | flops 1000000000 | bytes 4000000 | tf_op jit(solution)/shard_map/rows/pallas_call | solution.py:466
  57.5 2.5 %all-to-all-done.1.got_ref = f32[32,32,128]{2,1,0:T(8,128)S(1)} async-done(((f32[32,32,128]{2,1,0:T(8,128)}), f32[32,32,128]{2,1,0:T(8,128)S(1)}, u32[]{:S(2)}, u32[]{:S(2)}) %all-to-all-start.1) | async-done | bytes 524320 | tf_op jit(solution)/shard_map/all_to_all | solution.py:445
  60.0 1.3 %finish.1 = f32[128,256]{1,0:T(8,128)} custom-call(s32[16]{0:T(128)S(1)} %fusion.3.ints_ref.ints_in, f32[32,32,128]{2,1,0:T(8,128)S(1)} %all-to-all-done.1.got_ref, f32[128,256]{1,0:T(8,128)S(1)} %rows.1.base_ref, bf16[256,768]{1,0:T(8,128)(2,1)S(1)} %get-tuple-element.47.ghi_ref, bf16[256,768]{1,0:T(8,128)(2,1)S(1)} %get-tuple-element.48.glo_ref), custom_call_target="tpu_custom_call" | custom-call | flops 300000000 | bytes 4000000 | tf_op jit(solution)/shard_map/finish/pallas_call | solution.py:467
  (22 shorter events, 0.2 us)
Async XLA Ops:
  0.0 30.6 %copy-start = (f32[2,256,256]{2,1,0:T(8,128)S(1)}, f32[2,256,256]{2,1,0:T(8,128)}, u32[]{:S(2)}) copy-start(f32[2,256,256]{2,1,0:T(8,128)} %q_ref) | copy-start | bytes 1572868
  0.0 1.0 %copy-start.1 = (f32[4,2,16,256]{3,2,1,0:T(8,128)S(1)}, f32[4,2,16,256]{3,2,1,0:T(8,128)}, u32[]{:S(2)}) copy-start(f32[4,2,16,256]{3,2,1,0:T(8,128)} %x_ref.1) | copy-start | bytes 393220
  1.7 14.8 %copy-start.4 = (s32[32]{0:T(128)S(1)}, s32[32]{0:T(128)}, u32[]{:S(2)}) copy-start(s32[32]{0:T(128)} %param.11) | copy-start | bytes 388
  1.7 15.0 %copy-start.6 = (f32[2,2]{1,0:T(2,128)S(1)}, f32[2,2]{1,0:T(2,128)}, u32[]{:S(2)}) copy-start(f32[2,2]{1,0:T(2,128)} %param.10) | copy-start | bytes 52
  1.7 28.2 %copy-start.5 = (f32[2]{0:T(128)S(1)}, f32[2]{0:T(128)}, u32[]{:S(2)}) copy-start(f32[2]{0:T(128)} %param.9) | copy-start | bytes 28
  1.7 21.3 %all-to-all-start = ((f32[32,8,128]{2,1,0:T(8,128)}), f32[32,8,128]{2,1,0:T(8,128)S(1)}, u32[]{:S(2)}, u32[]{:S(2)}) async-start(f32[32,8,128]{2,1,0:T(8,128)} %own.1), calls=%async_computation | async-start | bytes 262144 | tf_op jit(solution)/shard_map/all_to_all | solution.py:445
  13.8 16.2 %copy-start.2 = (f32[4,2,16,256]{3,2,1,0:T(8,128)S(1)}, f32[4,2,16,256]{3,2,1,0:T(8,128)}, u32[]{:S(2)}) copy-start(f32[4,2,16,256]{3,2,1,0:T(8,128)} %x_ref.1) | copy-start | bytes 393220
  13.8 16.8 %copy-start.3 = (f32[256,256]{1,0:T(8,128)S(1)}, f32[256,256]{1,0:T(8,128)}, u32[]{:S(2)}) copy-start(f32[256,256]{1,0:T(8,128)} %h_ref) | copy-start | bytes 786436
  13.8 16.2 %collective-permute-start = (f32[4,2,16,256]{3,2,1,0:T(8,128)}, f32[4,2,16,256]{3,2,1,0:T(8,128)S(1)}, u32[]{:S(2)}, u32[]{:S(2)}) collective-permute-start(f32[4,2,16,256]{3,2,1,0:T(8,128)} %x_ref.1), channel_id=1, source_target_pairs={{16,32},{48,64},{80,96},{112,128},{144,160},{176,192},{208,224},{2... | collective-permute-start | bytes 393224 | tf_op jit(solution)/shard_map/ppermute | solution.py:452
  23.4 8.3 %collective-permute-start.1 = (f32[4,2,8,256]{3,2,1,0:T(8,128)S(1)}, f32[4,2,8,256]{3,2,1,0:T(8,128)S(1)}, u32[]{:S(2)}, u32[]{:S(2)}) collective-permute-start(f32[4,2,8,256]{3,2,1,0:T(8,128)S(1)} %get-tuple-element.36), channel_id=1, source_target_pairs={{32,80},{48,64},{96,144},{112,128},{160,208},{176,192},{224,272},{... | collective-permute-start | bytes 196616 | tf_op jit(solution)/shard_map/ppermute | solution.py:454
  28.0 6.2 %collective-permute-start.2 = (f32[4,2,8,256]{3,2,1,0:T(8,128)S(1)}, f32[4,2,8,256]{3,2,1,0:T(8,128)S(1)}, u32[]{:S(2)}, u32[]{:S(2)}) collective-permute-start(f32[4,2,8,256]{3,2,1,0:T(8,128)S(1)} %get-tuple-element.37), channel_id=1, source_target_pairs={{0,48},{16,32},{64,112},{80,96},{128,176},{144,160},{192,240},{208... | collective-permute-start | bytes 196616 | tf_op jit(solution)/shard_map/ppermute | solution.py:455
  36.3 23.8 %all-to-all-start.1 = ((f32[32,32,128]{2,1,0:T(8,128)}), f32[32,32,128]{2,1,0:T(8,128)S(1)}, u32[]{:S(2)}, u32[]{:S(2)}) async-start(f32[32,32,128]{2,1,0:T(8,128)} %columns.1), calls=%async_computation.1 | async-start | bytes 1048576 | tf_op jit(solution)/shard_map/all_to_all | solution.py:445
  42.3 13.6 %collective-permute-start.4 = (f32[6,2,16,256]{3,2,1,0:T(8,128)S(1)}, f32[6,2,16,256]{3,2,1,0:T(8,128)S(1)}, u32[]{:S(2)}, u32[]{:S(2)}) collective-permute-start(f32[6,2,16,256]{3,2,1,0:T(8,128)S(1)} %get-tuple-element.46), channel_id=1, source_target_pairs={{0,16},{32,48},{64,80},{96,112},{128,144},{160,176},{192,208},{224... | collective-permute-start | bytes 589832 | tf_op jit(solution)/shard_map/ppermute | solution.py:465
  44.5 11.1 %collective-permute-start.3 = (f32[2,2,16,256]{3,2,1,0:T(8,128)S(1)}, f32[2,2,16,256]{3,2,1,0:T(8,128)S(1)}, u32[]{:S(2)}, u32[]{:S(2)}) collective-permute-start(f32[2,2,16,256]{3,2,1,0:T(8,128)S(1)} %get-tuple-element.45), channel_id=1, source_target_pairs={{0,32},{32,64},{64,96},{96,128},{128,160},{160,192},{192,224},{224... | collective-permute-start | bytes 196616 | tf_op jit(solution)/shard_map/ppermute | solution.py:464
